TPU v7x, 512 devices: a whole 4x8x8 slice. The times are simulated.
512 devices in a mesh: group: 2 (over x_hi), dp: 256 (over y, x_lo, z, core).
Axes of the slice: x: 4 (x_hi: 2, x_lo: 2; x = x_hi * 2 + x_lo), y: 8, z: 8, core: 2. Of those that a mesh axis runs over, the one named last changes fastest.
Arguments:
- operands: bfloat16 [2, 256, 256, 4096], P('group', 'dp'), may hold values from -32 to 32
Outputs:
- results: bfloat16 [2, 256, 256, 4096], P('group', 'dp')
All inputs are finite; a program needn't handle non-finite values.
Results may differ from a plain program's by a relative error of at most 0.013.
Values may be sent and summed in bfloat16 or wider, within the bound.
No kernel may reach another device: no remote copies, remote signals or barrier semaphores. Data moves between devices by JAX's collectives and lax.ppermute only.
A program may use at most 64 MiB of HBM per device.

v0:
```python
import jax
import jax.numpy as jnp
from jax import lax
from jax.sharding import PartitionSpec as P

HEADS = 8
HEAD = 256


def from_behind(x, axis, by):
    count = lax.axis_size(axis)
    pairs = [(i, i + by) for i in range(count) if 0 <= i + by < count]
    return lax.ppermute(x, axis, pairs)


def as_heads(half):
    return half.reshape(half.shape[0], half.shape[1], HEADS, HEAD)


def merge_heads(array):
    return array.reshape(array.shape[0], array.shape[1], -1)


def forward_part(query_rows, key_rows, value_rows):
    factor = HEAD ** (-0.5)
    scores = (
        jnp.einsum("sqhe,skhe->shqk", query_rows, key_rows, preferred_element_type=jnp.float32)
        * factor
    )
    maximum = jnp.max(scores, axis=-1, keepdims=True)
    exponent = jnp.exp(scores - maximum)
    weights = exponent / jnp.sum(exponent, axis=-1, keepdims=True)
    weights_b = weights.astype(jnp.bfloat16)
    attended = jnp.einsum(
        "shqk,skhe->sqhe", weights_b, value_rows, preferred_element_type=jnp.float32
    )
    return (weights, weights_b, attended)


def score_grads(weights, attended, out_grad, value_rows):
    factor = HEAD ** (-0.5)
    grad_weights = jnp.einsum(
        "sqhe,skhe->shqk", out_grad, value_rows, preferred_element_type=jnp.float32
    )
    row_delta = jnp.sum(out_grad.astype(jnp.float32) * attended, axis=-1)
    row_delta = jnp.transpose(row_delta, (0, 2, 1))[:, :, :, None]
    return (weights * (grad_weights - row_delta) * factor).astype(jnp.bfloat16)


def query_side(grad_scores, key_rows):
    return jnp.einsum("shqk,skhe->sqhe", grad_scores, key_rows, preferred_element_type=jnp.float32)


def key_side(grad_scores, weights_b, query_rows, out_grad):
    key_grad = jnp.einsum(
        "shqk,sqhe->skhe", grad_scores, query_rows, preferred_element_type=jnp.float32
    )
    value_grad = jnp.einsum(
        "shqk,sqhe->skhe", weights_b, out_grad, preferred_element_type=jnp.float32
    )
    return jnp.concatenate([merge_heads(key_grad), merge_heads(value_grad)], axis=-1).astype(
        jnp.bfloat16
    )


def split_pair(block):
    width = block.shape[-1] // 2
    return (as_heads(block[:, :, :width]), as_heads(block[:, :, width:]))


def local(operands):
    block_in = operands[0]
    on_decoder = lax.axis_index("group") == 1
    empty = jnp.zeros(block_in.shape, jnp.bfloat16)
    received = from_behind(operands, ("group", "dp"), lax.axis_size("dp"))

    def decoder_work(pieces):
        query_rows, out_grad = split_pair(pieces[0])
        key_rows, value_rows = split_pair(pieces[1])
        weights, weights_b, attended = forward_part(query_rows, key_rows, value_rows)
        grad_scores = score_grads(weights, attended, out_grad, value_rows)
        query_grad = query_side(grad_scores, key_rows)
        front = jnp.concatenate([merge_heads(attended), merge_heads(query_grad)], axis=-1).astype(
            jnp.bfloat16
        )
        back = key_side(grad_scores, weights_b, query_rows, out_grad)
        return (front, back)

    def encoder_rest(pieces):
        return (empty, empty)

    front, back = lax.cond(on_decoder, decoder_work, encoder_rest, (block_in, received[0]))
    returned = from_behind(back[None], ("group", "dp"), -lax.axis_size("dp"))
    result = jnp.where(on_decoder, front, returned[0])
    return result[None]


def solution(mesh):
    in_specs = (P("group", "dp", None, None),)
    out_specs = P("group", "dp", None, None)
    return jax.shard_map(local, mesh=mesh, in_specs=in_specs, out_specs=out_specs, check_vma=False)
```

profile of v0, /device:TPU:56, one launch (start us, length us, event | category | flops | bytes accessed | tf_op | source)
XLA Modules:
  0.0 132.3 jit_solution(13858863118445175129)
XLA Ops:
  0.0 4.1 %copy.24 = bf16[1,1,256,4096]{2,3,1,0:T(8,128)(2,1)} copy(bf16[1,1,256,4096]{3,2,1,0:T(8,128)(2,1)} %param.3) | data formatting | bytes 4194304 | tf_op args[0]
  4.1 5.0 %collective-permute-start = (bf16[1,1,256,4096]{2,3,1,0:T(8,128)(2,1)}, bf16[1,1,256,4096]{2,3,1,0:T(8,128)(2,1)S(1)}, u32[]{:S(2)}, u32[]{:S(2)}) collective-permute-start(bf16[1,1,256,4096]{2,3,1,0:T(8,128)(2,1)} %copy.24), channel_id=1, source_target_pairs={{0,256},{1,257},{2,258},{3,259},{4,260},{5,261},{6,262},{7,263},{8... | collective-permute-start | bytes 6291464 | tf_op jit(solution)/shard_map/ppermute | solution.py:13
  9.1 45.0 %collective-permute-done = bf16[1,1,256,4096]{2,3,1,0:T(8,128)(2,1)S(1)} collective-permute-done((bf16[1,1,256,4096]{2,3,1,0:T(8,128)(2,1)}, bf16[1,1,256,4096]{2,3,1,0:T(8,128)(2,1)S(1)}, u32[]{:S(2)}, u32[]{:S(2)}) %collective-permute-start) | collective-permute-done | bytes 2097184 | tf_op jit(solution)/shard_map/ppermute | solution.py:13
  54.2 1.7 %conditional.1 = (bf16[1,256,4096]{1,2,0:T(8,128)(2,1)}, bf16[1,256,4096]{2,1,0:T(8,128)(2,1)S(1)}) conditional(s32[]{:T(128)} %convert_element_type.43, () %tuple.13, (bf16[1,1,256,4096]{3,2,1,0:T(8,128)(2,1)}, bf16[1,1,256,4096]{2,3,1,0:T(8,128)(2,1)S(1)}) %tuple.14), branch_computations={%region_0.0_spmd, %region_1.0_spmd} | conditional | flops 1628961024 | bytes 100712696 | solution.py:92
  54.2 1.5 %broadcast_in_dim.3 = bf16[1,256,4096]{1,2,0:T(8,128)(2,1)} broadcast(bf16[]{:T(256)} %constant.2.clone), dimensions={} | broadcast | bytes 2097154 | tf_op jit(solution)/shard_map/broadcast_in_dim | solution.py:74
  55.6 0.2 broadcast_in_dim.3.clone
  55.9 4.1 %copy.26 = bf16[1,256,4096]{2,1,0:T(8,128)(2,1)} copy(bf16[1,256,4096]{1,2,0:T(8,128)(2,1)} %get-tuple-element.16) | data formatting | bytes 4194304 | tf_op jit(solution)/shard_map/cond | solution.py:92
  60.0 1.3 collective-permute-start.1
  61.3 69.5 %collective-permute-done.1 = bf16[1,1,256,4096]{3,2,1,0:T(8,128)(2,1)S(1)} collective-permute-done((bf16[1,1,256,4096]{3,2,1,0:T(8,128)(2,1)}, bf16[1,1,256,4096]{3,2,1,0:T(8,128)(2,1)S(1)}, u32[]{:S(2)}, u32[]{:S(2)}) %collective-permute-start.1) | collective-permute-done | bytes 2097184 | tf_op jit(solution)/shard_map/ppermute | solution.py:13
  130.8 1.5 %fusion.11 = bf16[1,1,256,4096]{3,2,1,0:T(8,128)(2,1)} fusion(bf16[1,256,4096]{2,1,0:T(8,128)(2,1)S(1)} %get-tuple-element.21, bf16[1,1,256,4096]{3,2,1,0:T(8,128)(2,1)S(1)} %collective-permute-done.1, pred[]{:T(512)S(6)} %eq.3), kind=kLoop, calls=%fused_computation.20 | loop fusion | flops 1048576 | bytes 6291457 | tf_op jit(solution)/shard_map/broadcast_in_dim | solution.py:95
Async XLA Ops:
  4.1 50.1 %collective-permute-start = (bf16[1,1,256,4096]{2,3,1,0:T(8,128)(2,1)}, bf16[1,1,256,4096]{2,3,1,0:T(8,128)(2,1)S(1)}, u32[]{:S(2)}, u32[]{:S(2)}) collective-permute-start(bf16[1,1,256,4096]{2,3,1,0:T(8,128)(2,1)} %copy.24), channel_id=1, source_target_pairs={{0,256},{1,257},{2,258},{3,259},{4,260},{5,261},{6,262},{7,263},{8... | collective-permute-start | bytes 6291464 | tf_op jit(solution)/shard_map/ppermute | solution.py:13
  60.0 70.8 %collective-permute-start.1 = (bf16[1,1,256,4096]{3,2,1,0:T(8,128)(2,1)}, bf16[1,1,256,4096]{3,2,1,0:T(8,128)(2,1)S(1)}, u32[]{:S(2)}, u32[]{:S(2)}) collective-permute-start(bf16[1,1,256,4096]{3,2,1,0:T(8,128)(2,1)} %bitcast.68), channel_id=1, source_target_pairs={{256,0},{257,1},{258,2},{259,3},{260,4},{261,5},{262,6},{263,7},{2... | collective-permute-start | bytes 6291464 | tf_op jit(solution)/shard_map/ppermute | solution.py:13
where the time goes:
time: 133 us; the launch traced here: 132 us
  waiting for transfers between devices  115 us (86%)
  local copies, waits for them, and re-layouts  9.88 us (7%)
  starting transfers between devices  6.33 us (5%)
  other arithmetic  1.54 us (1%)
    ppermute x2, waiting for transfers between devices, from_behind(): return lax.ppermute(x, axis, pairs)  115 us
    ppermute x2, starting transfers between devices, from_behind(): return lax.ppermute(x, axis, pairs)  6.33 us
    cond x1, local copies, waits for them, and re-layouts, local(): lax.cond(on_decoder, decoder_work, encoder_rest, (block_in, received[0]))  4.13 us
    unnamed x1, local copies, waits for them, and re-layouts  4.06 us
  transfers between devices with their start and end apart: 2, of which 2 were waited for; matrix products, arithmetic and copies ran while one was open for 0% of the time, Pallas kernels for 0%

commit v1 on v0

v1 whole, which is shorter than its diff:
```python
import functools

import jax
import jax.numpy as jnp
from jax import lax
from jax.experimental import pallas as pl
from jax.experimental.pallas import tpu as pltpu
from jax.sharding import PartitionSpec as P

HEAD = 256
INNER = 2048
KEPT = INNER // 2
CHUNKS = (1, 1, 1, 1)
FACTOR = HEAD ** (-0.5)


def dot(a, b, dims):
    return lax.dot_general(a, b, (dims, ((), ())), preferred_element_type=jnp.float32)


def head_work(query, out_grad, key, value):
    scores = dot(query, key, ((1,), (1,))) * FACTOR
    grad_weights = dot(out_grad, value, ((1,), (1,)))
    exponent = jnp.exp(scores - jnp.max(scores, axis=-1, keepdims=True))
    weights = exponent / jnp.sum(exponent, axis=-1, keepdims=True)
    weights_b = weights.astype(jnp.bfloat16)
    attended = dot(weights_b, value, ((1,), (0,)))
    value_grad = dot(weights_b, out_grad, ((0,), (0,)))
    row_delta = jnp.sum(out_grad.astype(jnp.float32) * attended, axis=-1, keepdims=True)
    grad_scores = (weights * (grad_weights - row_delta) * FACTOR).astype(jnp.bfloat16)
    query_grad = dot(grad_scores, key, ((1,), (0,)))
    key_grad = dot(grad_scores, query, ((0,), (0,)))
    return tuple(x.astype(jnp.bfloat16) for x in (attended, query_grad, key_grad, value_grad))


def halves(block, chunk, sems, at, width):
    views = [block.at[:, pl.ds(pl.multiple_of(i * INNER + at, HEAD), width)] for i in range(2)]
    return views, [chunk.at[i] for i in range(2)], [sems.at[i] for i in range(2)]


def load(block, chunk, sems, at, width):
    views, parts, s = halves(block, chunk, sems, at, width)
    return [pltpu.make_async_copy(v, p, m) for v, p, m in zip(views, parts, s)]


def store(block, chunk, sems, at, width):
    views, parts, s = halves(block, chunk, sems, at, width)
    return [pltpu.make_async_copy(p, v, m) for v, p, m in zip(views, parts, s)]


def pack_kernel(role_ref, block, *rest):
    *chunks, sems = rest
    at = (1 - role_ref[0]) * KEPT
    copies = []
    for i, chunk in enumerate(chunks):
        copies += load(block, chunk, sems.at[i], at, chunk.shape[-1])
        at = at + chunk.shape[-1]
    for copy in copies:
        copy.start()
    for copy in copies:
        copy.wait()


def work_kernel(first, width, has_out, role_ref, block, received, *rest):
    if has_out:
        rest = rest[1:]
    out, back, own, kept, sems = rest
    role = role_ref[0]
    at = role * KEPT + first
    copies = load(block, own, sems, at, width)
    for copy in copies:
        copy.start()
    for copy in copies:
        copy.wait()

    def run(decoder):
        query_side, key_side = (own, received) if decoder else (received, own)
        front, rear = (kept, back) if decoder else (back, kept)
        for h in range(width // HEAD):
            cols = slice(h * HEAD, (h + 1) * HEAD)
            attended, query_grad, key_grad, value_grad = head_work(
                query_side[0, :, cols], query_side[1, :, cols], key_side[0, :, cols], key_side[1, :, cols]
            )
            front[0, :, cols] = attended
            front[1, :, cols] = query_grad
            rear[0, :, cols] = key_grad
            rear[1, :, cols] = value_grad

    pl.when(role == 1)(lambda: run(True))
    pl.when(role == 0)(lambda: run(False))
    copies = store(out, kept, sems, at, width)
    for copy in copies:
        copy.start()
    for copy in copies:
        copy.wait()


def place_kernel(first, width, role_ref, chunk, _, out, sems):
    at = (1 - role_ref[0]) * KEPT + first
    copies = store(out, chunk, sems, at, width)
    for copy in copies:
        copy.start()
    for copy in copies:
        copy.wait()


SMEM = pl.BlockSpec(memory_space=pltpu.SMEM)
VMEM = pl.BlockSpec(memory_space=pltpu.VMEM)
ANY = pl.BlockSpec(memory_space=pl.ANY)


def chunk_shape(rows, width):
    return jax.ShapeDtypeStruct((2, rows, width), jnp.bfloat16)


def local(operands):
    rows, both = operands.shape[2:]
    block = operands.reshape(rows, both)
    role = lax.axis_index("group").astype(jnp.int32).reshape(1)
    count = lax.axis_size("dp")
    pairs = [(i, (i + count) % (2 * count)) for i in range(2 * count)]
    widths = [n * HEAD for n in CHUNKS]
    firsts = [sum(widths[:i]) for i in range(len(widths))]

    sent = pl.pallas_call(
        pack_kernel,
        out_shape=[chunk_shape(rows, w) for w in widths],
        in_specs=[SMEM, ANY],
        out_specs=[ANY] * len(widths),
        scratch_shapes=[pltpu.SemaphoreType.DMA((len(widths), 2))],
        name="pack",
    )(role, block)
    received = [lax.ppermute(c, ("group", "dp"), pairs) for c in sent]

    out = None
    returned = []
    for first, width, chunk in zip(firsts, widths, received):
        args = [role, block, chunk] + ([out] if out is not None else [])
        out, back = pl.pallas_call(
            functools.partial(work_kernel, first, width, out is not None),
            out_shape=[jax.ShapeDtypeStruct((rows, both), jnp.bfloat16), chunk_shape(rows, width)],
            in_specs=[SMEM, ANY, VMEM] + ([ANY] if out is not None else []),
            out_specs=[ANY, VMEM],
            scratch_shapes=[
                pltpu.VMEM((2, rows, width), jnp.bfloat16),
                pltpu.VMEM((2, rows, width), jnp.bfloat16),
                pltpu.SemaphoreType.DMA((2,)),
            ],
            input_output_aliases={3: 0} if out is not None else {},
            cost_estimate=pl.CostEstimate(
                flops=12 * rows * rows * width, bytes_accessed=16 * rows * width, transcendentals=rows * width
            ),
            name="work",
        )(*args)
        returned.append(lax.ppermute(back, ("group", "dp"), pairs))
    for first, width, chunk in zip(firsts, widths, returned):
        out = pl.pallas_call(
            functools.partial(place_kernel, first, width),
            out_shape=jax.ShapeDtypeStruct((rows, both), jnp.bfloat16),
            in_specs=[SMEM, ANY, ANY],
            out_specs=ANY,
            scratch_shapes=[pltpu.SemaphoreType.DMA((2,))],
            input_output_aliases={2: 0},
            name="place",
        )(role, chunk, out)
    return out.reshape(operands.shape)


def solution(mesh):
    spec = P("group", "dp", None, None)
    return jax.shard_map(local, mesh=mesh, in_specs=(spec,), out_specs=spec, check_vma=False)
```

time: 133 us -> 127 us (0.955); the launches traced: 132 us -> 125 us
  waiting for transfers between devices: 115 us -> 3.46 us
  Pallas kernels: 0 us -> 86.1 us
  starting transfers between devices: 6.33 us -> 29.4 us
  local copies, waits for them, and re-layouts: 9.88 us -> 5.54 us
  other arithmetic: 1.54 us -> 0 us
    ppermute x2 -> x8, waiting for transfers between devices: 115 us -> 3.46 us  [the longest x4 3.45 us: local(): returned.append(lax.ppermute(back, ('group', 'dp'), pairs))]
    pallas_call x0 -> x9, Pallas kernels: none -> 86.1 us  [the longest x4 36.2 us: local(): pl.pallas_call(functools.partial(place_kernel, first, width), out_shape=j...]
    ppermute x2 -> x8, starting transfers between devices: 6.33 us -> 29.4 us  [the longest x4 14.7 us: local(): returned.append(lax.ppermute(back, ('group', 'dp'), pairs))]
    cond x1 -> x0, local copies, waits for them, and re-layouts: 4.13 us -> none  [local(): lax.cond(on_decoder, decoder_work, encoder_rest, (block_in, received[0]))]
    broadcast_in_dim x2 -> x0, local copies, waits for them, and re-layouts: 1.68 us -> none  [local(): empty = jnp.zeros(block_in.shape, jnp.bfloat16)]
    broadcast_in_dim x1 -> x0, other arithmetic: 1.54 us -> none  [local(): return result[None]]
    unnamed x1 -> x20, local copies, waits for them, and re-layouts: 4.06 us -> 5.54 us
  transfers between devices with their start and end apart: 2 -> 8, of which waited for: 2 -> 1; matrix products, arithmetic and copies ran while one was open for 0% -> 0% of each run, Pallas kernels for 0% -> 35%
where the time goes in v1:
time: 127 us; the launch traced here: 125 us
  Pallas kernels  86.1 us (68%)
  starting transfers between devices  29.4 us (23%)
  local copies, waits for them, and re-layouts  5.54 us (4%)
  waiting for transfers between devices  3.46 us (3%)
    pallas_call x4, Pallas kernels, local(): pl.pallas_call(functools.partial(place_kernel, first, width), out_shape=j...  36.2 us
    pallas_call x1, Pallas kernels, local(): pl.pallas_call(pack_kernel, out_shape=[chunk_shape(rows, w) for w in widt...  32.9 us
    pallas_call x4, Pallas kernels, local(): pl.pallas_call(functools.partial(work_kernel, first, width, out is not No...  17 us
    ppermute x4, starting transfers between devices, local(): returned.append(lax.ppermute(back, ('group', 'dp'), pairs))  14.7 us
    ppermute x4, starting transfers between devices, local(): received = [lax.ppermute(c, ('group', 'dp'), pairs) for c in sent]  14.7 us
    unnamed x20, local copies, waits for them, and re-layouts  5.54 us
    ppermute x4, waiting for transfers between devices, local(): returned.append(lax.ppermute(back, ('group', 'dp'), pairs))  3.45 us
  transfers between devices with their start and end apart: 8, of which 1 were waited for; matrix products, arithmetic and copies ran while one was open for 0% of the time, Pallas kernels for 35%

profile of v1, /device:TPU:56, one launch (start us, length us, event | category | flops | bytes accessed | tf_op | source)
XLA Modules:
  0.0 124.8 jit_solution(18430456968859028641)
XLA Ops:
  0.0 32.9 %pack.1 = (bf16[2,256,256]{2,1,0:T(8,128)(2,1)}, bf16[2,256,256]{2,1,0:T(8,128)(2,1)}, bf16[2,256,256]{2,1,0:T(8,128)(2,1)}, bf16[2,256,256]{2,1,0:T(8,128)(2,1)}) custom-call(s32[1]{0:T(128)} %bitcast.role_ref, bf16[256,4096]{1,0:T(8,128)(2,1)} %bitcast.3), custom_call_target="tpu_custom_call" | custom-call | tf_op jit(solution)/shard_map/pack/pallas_call | solution.py:125
  32.9 4.9 %collective-permute-start.3 = (bf16[2,256,256]{2,1,0:T(8,128)(2,1)}, bf16[2,256,256]{2,1,0:T(8,128)(2,1)S(1)}, u32[]{:S(2)}, u32[]{:S(2)}) collective-permute-start(bf16[2,256,256]{2,1,0:T(8,128)(2,1)} %get-tuple-element.20), channel_id=1, source_target_pairs={{0,256},{1,257},{2,258},{3,259},{4,260},{5,261},{6,262},{7,263},{8... | collective-permute-start | bytes 786440 | tf_op jit(solution)/shard_map/ppermute | solution.py:133
  37.9 2.4 %collective-permute-start.2 = (bf16[2,256,256]{2,1,0:T(8,128)(2,1)}, bf16[2,256,256]{2,1,0:T(8,128)(2,1)S(1)}, u32[]{:S(2)}, u32[]{:S(2)}) collective-permute-start(bf16[2,256,256]{2,1,0:T(8,128)(2,1)} %get-tuple-element.19), channel_id=1, source_target_pairs={{0,256},{1,257},{2,258},{3,259},{4,260},{5,261},{6,262},{7,263},{8... | collective-permute-start | bytes 786440 | tf_op jit(solution)/shard_map/ppermute | solution.py:133
  40.3 4.9 %collective-permute-start.1 = (bf16[2,256,256]{2,1,0:T(8,128)(2,1)}, bf16[2,256,256]{2,1,0:T(8,128)(2,1)S(1)}, u32[]{:S(2)}, u32[]{:S(2)}) collective-permute-start(bf16[2,256,256]{2,1,0:T(8,128)(2,1)} %get-tuple-element.18), channel_id=1, source_target_pairs={{0,256},{1,257},{2,258},{3,259},{4,260},{5,261},{6,262},{7,263},{8... | collective-permute-start | bytes 786440 | tf_op jit(solution)/shard_map/ppermute | solution.py:133
  45.2 2.4 %collective-permute-start = (bf16[2,256,256]{2,1,0:T(8,128)(2,1)}, bf16[2,256,256]{2,1,0:T(8,128)(2,1)S(1)}, u32[]{:S(2)}, u32[]{:S(2)}) collective-permute-start(bf16[2,256,256]{2,1,0:T(8,128)(2,1)} %get-tuple-element.17), channel_id=1, source_target_pairs={{0,256},{1,257},{2,258},{3,259},{4,260},{5,261},{6,262},{7,263},{8... | collective-permute-start | bytes 786440 | tf_op jit(solution)/shard_map/ppermute | solution.py:133
  47.7 0.0 collective-permute-done.3.received
  47.7 0.0 copy-start.6
  47.7 0.7 copy-done.6
  48.4 4.2 %work.4 = (bf16[256,4096]{1,0:T(8,128)(2,1)}, bf16[2,256,256]{2,1,0:T(8,128)(2,1)}) custom-call(s32[1]{0:T(128)} %bitcast.role_ref, bf16[256,4096]{1,0:T(8,128)(2,1)} %bitcast.4, bf16[2,256,256]{2,1,0:T(8,128)(2,1)} %copy-done.6), custom_call_target="tpu_custom_call" | custom-call | flops 201326592 | bytes 1048576 | tf_op jit(solution)/shard_map/work/pallas_call | solution.py:139
  52.6 0.0 collective-permute-done.2.received
  52.6 0.0 copy-start.5
  52.6 0.7 copy-done.5
  53.3 4.2 %work.5 = (bf16[256,4096]{1,0:T(8,128)(2,1)}, bf16[2,256,256]{2,1,0:T(8,128)(2,1)}) custom-call(s32[1]{0:T(128)} %bitcast.role_ref, bf16[256,4096]{1,0:T(8,128)(2,1)} %bitcast.5, bf16[2,256,256]{2,1,0:T(8,128)(2,1)} %copy-done.5, bf16[256,4096]{1,0:T(8,128)(2,1)} %get-tuple-element.21.rest_0_), custom_call_target="tpu_custom_call", output_to_operand_aliasing={{0}: (3, {})} | custom-call | flops 201326592 | bytes 1048576 | tf_op jit(solution)/shard_map/work/pallas_call | solution.py:139
  57.6 0.0 collective-permute-done.1.received
  57.6 0.0 copy-start.3
  57.6 0.7 copy-done.3
  58.3 0.0 copy-start.9
  58.3 0.0 copy-start.8
  58.3 4.3 %work.6 = (bf16[256,4096]{1,0:T(8,128)(2,1)}, bf16[2,256,256]{2,1,0:T(8,128)(2,1)}) custom-call(s32[1]{0:T(128)} %bitcast.role_ref, bf16[256,4096]{1,0:T(8,128)(2,1)} %bitcast.6, bf16[2,256,256]{2,1,0:T(8,128)(2,1)} %copy-done.3, bf16[256,4096]{1,0:T(8,128)(2,1)} %get-tuple-element.22.rest_0_), custom_call_target="tpu_custom_call", output_to_operand_aliasing={{0}: (3, {})} | custom-call | flops 201326592 | bytes 1048576 | tf_op jit(solution)/shard_map/work/pallas_call | solution.py:139
  62.6 4.9 %collective-permute-start.5 = (bf16[2,256,256]{2,1,0:T(8,128)(2,1)}, bf16[2,256,256]{2,1,0:T(8,128)(2,1)S(1)}, u32[]{:S(2)}, u32[]{:S(2)}) collective-permute-start(bf16[2,256,256]{2,1,0:T(8,128)(2,1)} %get-tuple-element.25), channel_id=1, source_target_pairs={{0,256},{1,257},{2,258},{3,259},{4,260},{5,261},{6,262},{7,263},{8... | collective-permute-start | bytes 786440 | tf_op jit(solution)/shard_map/ppermute | solution.py:155
  67.5 0.0 copy-done.9
  67.5 2.4 %collective-permute-start.6 = (bf16[2,256,256]{2,1,0:T(8,128)(2,1)S(1)}, bf16[2,256,256]{2,1,0:T(8,128)(2,1)S(1)}, u32[]{:S(2)}, u32[]{:S(2)}) collective-permute-start(bf16[2,256,256]{2,1,0:T(8,128)(2,1)S(1)} %copy-done.9), channel_id=1, source_target_pairs={{0,256},{1,257},{2,258},{3,259},{4,260},{5,261},{6,262},{7,263},{8... | collective-permute-start | bytes 786440 | tf_op jit(solution)/shard_map/ppermute | solution.py:155
  69.9 0.0 copy-done.8
  69.9 4.9 %collective-permute-start.7 = (bf16[2,256,256]{2,1,0:T(8,128)(2,1)S(1)}, bf16[2,256,256]{2,1,0:T(8,128)(2,1)S(1)}, u32[]{:S(2)}, u32[]{:S(2)}) collective-permute-start(bf16[2,256,256]{2,1,0:T(8,128)(2,1)S(1)} %copy-done.8), channel_id=1, source_target_pairs={{0,256},{1,257},{2,258},{3,259},{4,260},{5,261},{6,262},{7,263},{8... | collective-permute-start | bytes 786440 | tf_op jit(solution)/shard_map/ppermute | solution.py:155
  74.9 0.0 collective-permute-done.received
  74.9 0.0 copy-start
  74.9 0.7 copy-done
  75.6 4.2 %work.7 = (bf16[256,4096]{1,0:T(8,128)(2,1)}, bf16[2,256,256]{2,1,0:T(8,128)(2,1)}) custom-call(s32[1]{0:T(128)} %bitcast.role_ref, bf16[256,4096]{1,0:T(8,128)(2,1)} %bitcast.7, bf16[2,256,256]{2,1,0:T(8,128)(2,1)} %copy-done, bf16[256,4096]{1,0:T(8,128)(2,1)} %get-tuple-element.23.rest_0_), custom_call_target="tpu_custom_call", output_to_operand_aliasing={{0}: (3, {})} | custom-call | flops 201326592 | bytes 1048576 | tf_op jit(solution)/shard_map/work/pallas_call | solution.py:139
  79.8 2.4 %collective-permute-start.4 = (bf16[2,256,256]{2,1,0:T(8,128)(2,1)}, bf16[2,256,256]{2,1,0:T(8,128)(2,1)S(1)}, u32[]{:S(2)}, u32[]{:S(2)}) collective-permute-start(bf16[2,256,256]{2,1,0:T(8,128)(2,1)} %get-tuple-element.24), channel_id=1, source_target_pairs={{0,256},{1,257},{2,258},{3,259},{4,260},{5,261},{6,262},{7,263},{8... | collective-permute-start | bytes 786440 | tf_op jit(solution)/shard_map/ppermute | solution.py:155
  82.3 3.4 %collective-permute-done.7.chunk = bf16[2,256,256]{2,1,0:T(8,128)(2,1)S(1)} collective-permute-done((bf16[2,256,256]{2,1,0:T(8,128)(2,1)S(1)}, bf16[2,256,256]{2,1,0:T(8,128)(2,1)S(1)}, u32[]{:S(2)}, u32[]{:S(2)}) %collective-permute-start.7) | collective-permute-done | bytes 262176 | tf_op jit(solution)/shard_map/ppermute | solution.py:155
  85.7 0.0 copy-start.7
  85.7 0.7 copy-done.7
  86.4 9.1 %place.4._ = bf16[256,4096]{1,0:T(8,128)(2,1)} custom-call(s32[1]{0:T(128)} %bitcast.role_ref, bf16[2,256,256]{2,1,0:T(8,128)(2,1)} %copy-done.7, bf16[256,4096]{1,0:T(8,128)(2,1)} %get-tuple-element.28._), custom_call_target="tpu_custom_call", output_to_operand_aliasing={{}: (2, {})} | custom-call | tf_op jit(solution)/shard_map/place/pallas_call | solution.py:157
  95.5 0.0 collective-permute-done.6.chunk
  95.5 0.0 copy-start.2
  95.5 0.7 copy-done.2
  96.2 9.1 %place.5._ = bf16[256,4096]{1,0:T(8,128)(2,1)} custom-call(s32[1]{0:T(128)} %bitcast.role_ref, bf16[2,256,256]{2,1,0:T(8,128)(2,1)} %copy-done.2, bf16[256,4096]{1,0:T(8,128)(2,1)} %place.4._), custom_call_target="tpu_custom_call", output_to_operand_aliasing={{}: (2, {})} | custom-call | tf_op jit(solution)/shard_map/place/pallas_call | solution.py:157
  105.2 0.0 collective-permute-done.5.chunk
  105.2 0.0 copy-start.1
  105.2 0.7 copy-done.1
  105.9 9.1 %place.6._ = bf16[256,4096]{1,0:T(8,128)(2,1)} custom-call(s32[1]{0:T(128)} %bitcast.role_ref, bf16[2,256,256]{2,1,0:T(8,128)(2,1)} %copy-done.1, bf16[256,4096]{1,0:T(8,128)(2,1)} %place.5._), custom_call_target="tpu_custom_call", output_to_operand_aliasing={{}: (2, {})} | custom-call | tf_op jit(solution)/shard_map/place/pallas_call | solution.py:157
  115.0 0.0 collective-permute-done.4.chunk
  115.0 0.0 copy-start.4
  115.0 0.7 copy-done.4
  115.7 9.1 %place.7 = bf16[256,4096]{1,0:T(8,128)(2,1)} custom-call(s32[1]{0:T(128)} %bitcast.role_ref, bf16[2,256,256]{2,1,0:T(8,128)(2,1)} %copy-done.4, bf16[256,4096]{1,0:T(8,128)(2,1)} %place.6._), custom_call_target="tpu_custom_call", output_to_operand_aliasing={{}: (2, {})} | custom-call | tf_op jit(solution)/shard_map/place/pallas_call | solution.py:157
Async XLA Ops:
  32.9 14.7 %collective-permute-start.3 = (bf16[2,256,256]{2,1,0:T(8,128)(2,1)}, bf16[2,256,256]{2,1,0:T(8,128)(2,1)S(1)}, u32[]{:S(2)}, u32[]{:S(2)}) collective-permute-start(bf16[2,256,256]{2,1,0:T(8,128)(2,1)} %get-tuple-element.20), channel_id=1, source_target_pairs={{0,256},{1,257},{2,258},{3,259},{4,260},{5,261},{6,262},{7,263},{8... | collective-permute-start | bytes 786440 | tf_op jit(solution)/shard_map/ppermute | solution.py:133
  37.9 14.7 %collective-permute-start.2 = (bf16[2,256,256]{2,1,0:T(8,128)(2,1)}, bf16[2,256,256]{2,1,0:T(8,128)(2,1)S(1)}, u32[]{:S(2)}, u32[]{:S(2)}) collective-permute-start(bf16[2,256,256]{2,1,0:T(8,128)(2,1)} %get-tuple-element.19), channel_id=1, source_target_pairs={{0,256},{1,257},{2,258},{3,259},{4,260},{5,261},{6,262},{7,263},{8... | collective-permute-start | bytes 786440 | tf_op jit(solution)/shard_map/ppermute | solution.py:133
  40.3 17.3 %collective-permute-start.1 = (bf16[2,256,256]{2,1,0:T(8,128)(2,1)}, bf16[2,256,256]{2,1,0:T(8,128)(2,1)S(1)}, u32[]{:S(2)}, u32[]{:S(2)}) collective-permute-start(bf16[2,256,256]{2,1,0:T(8,128)(2,1)} %get-tuple-element.18), channel_id=1, source_target_pairs={{0,256},{1,257},{2,258},{3,259},{4,260},{5,261},{6,262},{7,263},{8... | collective-permute-start | bytes 786440 | tf_op jit(solution)/shard_map/ppermute | solution.py:133
  45.2 29.6 %collective-permute-start = (bf16[2,256,256]{2,1,0:T(8,128)(2,1)}, bf16[2,256,256]{2,1,0:T(8,128)(2,1)S(1)}, u32[]{:S(2)}, u32[]{:S(2)}) collective-permute-start(bf16[2,256,256]{2,1,0:T(8,128)(2,1)} %get-tuple-element.17), channel_id=1, source_target_pairs={{0,256},{1,257},{2,258},{3,259},{4,260},{5,261},{6,262},{7,263},{8... | collective-permute-start | bytes 786440 | tf_op jit(solution)/shard_map/ppermute | solution.py:133
  47.7 0.7 copy-start.6
  52.6 0.7 copy-start.5
  57.6 0.7 copy-start.3
  58.3 9.2 %copy-start.9 = (bf16[2,256,256]{2,1,0:T(8,128)(2,1)S(1)}, bf16[2,256,256]{2,1,0:T(8,128)(2,1)}, u32[]{:S(2)}) copy-start(bf16[2,256,256]{2,1,0:T(8,128)(2,1)} %get-tuple-element.26) | copy-start | bytes 786436
  58.3 11.7 %copy-start.8 = (bf16[2,256,256]{2,1,0:T(8,128)(2,1)S(1)}, bf16[2,256,256]{2,1,0:T(8,128)(2,1)}, u32[]{:S(2)}) copy-start(bf16[2,256,256]{2,1,0:T(8,128)(2,1)} %get-tuple-element.27) | copy-start | bytes 786436
  62.6 42.7 %collective-permute-start.5 = (bf16[2,256,256]{2,1,0:T(8,128)(2,1)}, bf16[2,256,256]{2,1,0:T(8,128)(2,1)S(1)}, u32[]{:S(2)}, u32[]{:S(2)}) collective-permute-start(bf16[2,256,256]{2,1,0:T(8,128)(2,1)} %get-tuple-element.25), channel_id=1, source_target_pairs={{0,256},{1,257},{2,258},{3,259},{4,260},{5,261},{6,262},{7,263},{8... | collective-permute-start | bytes 786440 | tf_op jit(solution)/shard_map/ppermute | solution.py:155
  67.5 27.9 %collective-permute-start.6 = (bf16[2,256,256]{2,1,0:T(8,128)(2,1)S(1)}, bf16[2,256,256]{2,1,0:T(8,128)(2,1)S(1)}, u32[]{:S(2)}, u32[]{:S(2)}) collective-permute-start(bf16[2,256,256]{2,1,0:T(8,128)(2,1)S(1)} %copy-done.9), channel_id=1, source_target_pairs={{0,256},{1,257},{2,258},{3,259},{4,260},{5,261},{6,262},{7,263},{8... | collective-permute-start | bytes 786440 | tf_op jit(solution)/shard_map/ppermute | solution.py:155
  69.9 15.7 %collective-permute-start.7 = (bf16[2,256,256]{2,1,0:T(8,128)(2,1)S(1)}, bf16[2,256,256]{2,1,0:T(8,128)(2,1)S(1)}, u32[]{:S(2)}, u32[]{:S(2)}) collective-permute-start(bf16[2,256,256]{2,1,0:T(8,128)(2,1)S(1)} %copy-done.8), channel_id=1, source_target_pairs={{0,256},{1,257},{2,258},{3,259},{4,260},{5,261},{6,262},{7,263},{8... | collective-permute-start | bytes 786440 | tf_op jit(solution)/shard_map/ppermute | solution.py:155
  74.9 0.7 copy-start
  79.8 35.2 %collective-permute-start.4 = (bf16[2,256,256]{2,1,0:T(8,128)(2,1)}, bf16[2,256,256]{2,1,0:T(8,128)(2,1)S(1)}, u32[]{:S(2)}, u32[]{:S(2)}) collective-permute-start(bf16[2,256,256]{2,1,0:T(8,128)(2,1)} %get-tuple-element.24), channel_id=1, source_target_pairs={{0,256},{1,257},{2,258},{3,259},{4,260},{5,261},{6,262},{7,263},{8... | collective-permute-start | bytes 786440 | tf_op jit(solution)/shard_map/ppermute | solution.py:155
  85.7 0.7 copy-start.7
  95.5 0.7 copy-start.2
  105.2 0.7 copy-start.1
  115.0 0.7 copy-start.4

commit v2 on v1

v2 whole, which is shorter than its diff:
```python
import functools

import jax
import jax.numpy as jnp
from jax import lax
from jax.experimental import pallas as pl
from jax.experimental.pallas import tpu as pltpu
from jax.sharding import PartitionSpec as P

HEAD = 256
INNER = 2048
KEPT = INNER // 2
CHUNKS = (1, 1, 1, 1)
FACTOR = HEAD ** (-0.5)
VMEM_LIMIT = 12 * 1024 * 1024

SMEM = pl.BlockSpec(memory_space=pltpu.SMEM)
VMEM = pl.BlockSpec(memory_space=pltpu.VMEM)
ANY = pl.BlockSpec(memory_space=pl.ANY)
PARAMS = pltpu.CompilerParams(vmem_limit_bytes=VMEM_LIMIT)


def dot(a, b, dims):
    return lax.dot_general(a, b, (dims, ((), ())), preferred_element_type=jnp.float32)


def head_work(query, out_grad, key, value):
    scores = dot(query, key, ((1,), (1,))) * FACTOR
    grad_weights = dot(out_grad, value, ((1,), (1,)))
    exponent = jnp.exp(scores - jnp.max(scores, axis=-1, keepdims=True))
    weights = exponent / jnp.sum(exponent, axis=-1, keepdims=True)
    weights_b = weights.astype(jnp.bfloat16)
    attended = dot(weights_b, value, ((1,), (0,)))
    value_grad = dot(weights_b, out_grad, ((0,), (0,)))
    row_delta = jnp.sum(out_grad.astype(jnp.float32) * attended, axis=-1, keepdims=True)
    grad_scores = (weights * (grad_weights - row_delta) * FACTOR).astype(jnp.bfloat16)
    query_grad = dot(grad_scores, key, ((1,), (0,)))
    key_grad = dot(grad_scores, query, ((0,), (0,)))
    return tuple(x.astype(jnp.bfloat16) for x in (attended, query_grad, key_grad, value_grad))


def views(block, at, width):
    return [block.at[:, pl.ds(pl.multiple_of(i * INNER + at, HEAD), width)] for i in range(2)]


def run_copies(copies):
    for copy in copies:
        copy.start()
    for copy in copies:
        copy.wait()


def load_kernel(kept, role_ref, block, *rest):
    *chunks, sems = rest
    at = (role_ref[0] if kept else 1 - role_ref[0]) * KEPT
    copies = []
    for i, chunk in enumerate(chunks):
        for j, view in enumerate(views(block, at, chunk.shape[-1])):
            copies.append(pltpu.make_async_copy(view, chunk.at[j], sems.at[i, j]))
        at = at + chunk.shape[-1]
    run_copies(copies)


def work_kernel(width, role_ref, own, received, kept, back):
    role = role_ref[0]

    def run(decoder):
        query_side, key_side = (own, received) if decoder else (received, own)
        front, rear = (kept, back) if decoder else (back, kept)
        for h in range(width // HEAD):
            cols = slice(h * HEAD, (h + 1) * HEAD)
            attended, query_grad, key_grad, value_grad = head_work(
                query_side[0, :, cols], query_side[1, :, cols], key_side[0, :, cols], key_side[1, :, cols]
            )
            front[0, :, cols] = attended
            front[1, :, cols] = query_grad
            rear[0, :, cols] = key_grad
            rear[1, :, cols] = value_grad

    pl.when(role == 1)(lambda: run(True))
    pl.when(role == 0)(lambda: run(False))


def place_kernel(kept, firsts, aliased, role_ref, *rest):
    *chunks, out, sems = rest
    if aliased:
        chunks = chunks[:-1]
    at = (role_ref[0] if kept else 1 - role_ref[0]) * KEPT
    copies = []
    for i, (first, chunk) in enumerate(zip(firsts, chunks)):
        for j, view in enumerate(views(out, at + first, chunk.shape[-1])):
            copies.append(pltpu.make_async_copy(chunk.at[j], view, sems.at[i, j]))
    run_copies(copies)


def chunk_shape(rows, width):
    return jax.ShapeDtypeStruct((2, rows, width), jnp.bfloat16)


def cost(moved, flops=0, exps=0):
    return pl.CostEstimate(flops=flops, bytes_accessed=moved, transcendentals=exps)


def local(operands):
    rows, both = operands.shape[2:]
    block = operands.reshape(rows, both)
    role = lax.axis_index("group").astype(jnp.int32).reshape(1)
    count = lax.axis_size("dp")
    pairs = [(i, (i + count) % (2 * count)) for i in range(2 * count)]
    widths = [n * HEAD for n in CHUNKS]
    firsts = [sum(widths[:i]) for i in range(len(widths))]
    n = len(widths)

    def load(kept):
        return pl.pallas_call(
            functools.partial(load_kernel, kept),
            out_shape=[chunk_shape(rows, w) for w in widths],
            in_specs=[SMEM, ANY],
            out_specs=[VMEM] * n,
            scratch_shapes=[pltpu.SemaphoreType.DMA((n, 2))],
            compiler_params=PARAMS,
            cost_estimate=cost(rows * both),
            name="keep" if kept else "pack",
        )(role, block)

    def work(width, own, received):
        return pl.pallas_call(
            functools.partial(work_kernel, width),
            out_shape=[chunk_shape(rows, width)] * 2,
            in_specs=[SMEM, VMEM, VMEM],
            out_specs=[VMEM, VMEM],
            compiler_params=PARAMS,
            cost_estimate=cost(0, flops=12 * rows * rows * width, exps=rows * width),
            name="work",
        )(role, own, received)

    def place(kept, at, chunks, out=None):
        extra = [] if out is None else [out]
        return pl.pallas_call(
            functools.partial(place_kernel, kept, at, bool(extra)),
            out_shape=jax.ShapeDtypeStruct((rows, both), jnp.bfloat16),
            in_specs=[SMEM] + [VMEM] * len(chunks) + [ANY] * len(extra),
            out_specs=ANY,
            scratch_shapes=[pltpu.SemaphoreType.DMA((len(chunks), 2))],
            input_output_aliases={1 + len(chunks): 0} if extra else {},
            compiler_params=PARAMS,
            cost_estimate=cost(0),
            name="place",
        )(role, *chunks, *extra)

    sent = load(False)
    received = [lax.ppermute(c, ("group", "dp"), pairs) for c in sent]
    own = load(True)
    done, returned = [], []
    for i in range(n):
        kept, back = work(widths[i], own[i], received[i])
        done.append(kept)
        returned.append(lax.ppermute(back, ("group", "dp"), pairs))
    out = place(True, firsts, done)
    for i in range(n):
        out = place(False, [firsts[i]], [returned[i]], out)
    return out.reshape(operands.shape)


def solution(mesh):
    spec = P("group", "dp", None, None)
    return jax.shard_map(local, mesh=mesh, in_specs=(spec,), out_specs=spec, check_vma=False)
```

time: 127 us -> 53.7 us (0.42); the launches traced: 125 us -> 53.3 us
  Pallas kernels: 86.1 us -> 7.99 us
  waiting for transfers between devices: 3.46 us -> 12.3 us
  local copies, waits for them, and re-layouts: 5.54 us -> 1.59 us
  starting transfers between devices: 29.4 us -> 31.3 us
    pallas_call x9 -> x11, Pallas kernels: 86.1 us -> 7.99 us  [the longest x5 3.89 us: place(): pl.pallas_call(functools.partial(place_kernel, kept, at, bool(extra)), ou...]
    ppermute x4, waiting for transfers between devices: 3.45 us -> 12.3 us  [local(): returned.append(lax.ppermute(back, ('group', 'dp'), pairs))]
    unnamed x20 -> x2, local copies, waits for them, and re-layouts: 5.54 us -> 1.59 us
    ppermute x4, starting transfers between devices: 14.7 us -> 16.6 us  [local(): returned.append(lax.ppermute(back, ('group', 'dp'), pairs))]
  transfers between devices with their start and end apart: 8 -> 8, of which waited for: 1 -> 3; matrix products, arithmetic and copies ran while one was open for 0% -> 0% of each run, Pallas kernels for 35% -> 13%
where the time goes in v2:
time: 53.7 us; the launch traced here: 53.3 us
  starting transfers between devices  31.3 us (58%)
  waiting for transfers between devices  12.3 us (23%)
  Pallas kernels  7.99 us (15%)
  local copies, waits for them, and re-layouts  1.59 us (3%)
    ppermute x4, starting transfers between devices, local(): returned.append(lax.ppermute(back, ('group', 'dp'), pairs))  16.6 us
    ppermute x4, starting transfers between devices, local(): received = [lax.ppermute(c, ('group', 'dp'), pairs) for c in sent]  14.7 us
    ppermute x4, waiting for transfers between devices, local(): returned.append(lax.ppermute(back, ('group', 'dp'), pairs))  12.3 us
    pallas_call x5, Pallas kernels, place(): pl.pallas_call(functools.partial(place_kernel, kept, at, bool(extra)), ou...  3.89 us
    pallas_call x4, Pallas kernels, work(): pl.pallas_call(functools.partial(work_kernel, width), out_shape=[chunk_sh...  3.61 us
    unnamed x2, local copies, waits for them, and re-layouts  1.59 us
  transfers between devices with their start and end apart: 8, of which 3 were waited for; matrix products, arithmetic and copies ran while one was open for 0% of the time, Pallas kernels for 13%

profile of v2, /device:TPU:56, one launch (start us, length us, event | category | flops | bytes accessed | tf_op | source)
XLA Modules:
  0.0 53.3 jit_solution(2961281610252220862)
XLA Ops:
  0.0 0.0 copy-start
  0.0 1.6 %copy-done = bf16[1,1,256,4096]{3,2,1,0:T(8,128)(2,1)S(1)} copy-done((bf16[1,1,256,4096]{3,2,1,0:T(8,128)(2,1)S(1)}, bf16[1,1,256,4096]{3,2,1,0:T(8,128)(2,1)}, u32[]{:S(2)}) %copy-start) | copy-done | bytes 2097176
  1.6 0.2 pack.1
  1.8 4.9 %collective-permute-start.6 = (bf16[2,256,256]{2,1,0:T(8,128)(2,1)S(1)}, bf16[2,256,256]{2,1,0:T(8,128)(2,1)S(1)}, u32[]{:S(2)}, u32[]{:S(2)}) collective-permute-start(bf16[2,256,256]{2,1,0:T(8,128)(2,1)S(1)} %get-tuple-element.31), channel_id=1, source_target_pairs={{0,256},{1,257},{2,258},{3,259},{4,260},{5,261},{6,262},{7,263},{8... | collective-permute-start | bytes 786440 | tf_op jit(solution)/shard_map/ppermute | solution.py:152
  6.8 2.4 %collective-permute-start.4 = (bf16[2,256,256]{2,1,0:T(8,128)(2,1)S(1)}, bf16[2,256,256]{2,1,0:T(8,128)(2,1)S(1)}, u32[]{:S(2)}, u32[]{:S(2)}) collective-permute-start(bf16[2,256,256]{2,1,0:T(8,128)(2,1)S(1)} %get-tuple-element.28), channel_id=1, source_target_pairs={{0,256},{1,257},{2,258},{3,259},{4,260},{5,261},{6,262},{7,263},{8... | collective-permute-start | bytes 786440 | tf_op jit(solution)/shard_map/ppermute | solution.py:152
  9.2 4.9 %collective-permute-start.2 = (bf16[2,256,256]{2,1,0:T(8,128)(2,1)S(1)}, bf16[2,256,256]{2,1,0:T(8,128)(2,1)S(1)}, u32[]{:S(2)}, u32[]{:S(2)}) collective-permute-start(bf16[2,256,256]{2,1,0:T(8,128)(2,1)S(1)} %get-tuple-element.25), channel_id=1, source_target_pairs={{0,256},{1,257},{2,258},{3,259},{4,260},{5,261},{6,262},{7,263},{8... | collective-permute-start | bytes 786440 | tf_op jit(solution)/shard_map/ppermute | solution.py:152
  14.1 2.4 %collective-permute-start = (bf16[2,256,256]{2,1,0:T(8,128)(2,1)S(1)}, bf16[2,256,256]{2,1,0:T(8,128)(2,1)S(1)}, u32[]{:S(2)}, u32[]{:S(2)}) collective-permute-start(bf16[2,256,256]{2,1,0:T(8,128)(2,1)S(1)} %get-tuple-element.22), channel_id=1, source_target_pairs={{0,256},{1,257},{2,258},{3,259},{4,260},{5,261},{6,262},{7,263},{8... | collective-permute-start | bytes 786440 | tf_op jit(solution)/shard_map/ppermute | solution.py:152
  16.6 0.2 keep.1
  16.8 0.0 collective-permute-done.6.received
  16.8 0.9 %work.7 = (bf16[2,256,256]{2,1,0:T(8,128)(2,1)S(1)}, bf16[2,256,256]{2,1,0:T(8,128)(2,1)S(1)}) custom-call(s32[1]{0:T(128)} %bitcast.role_ref, bf16[2,256,256]{2,1,0:T(8,128)(2,1)S(1)} %get-tuple-element.30.own, bf16[2,256,256]{2,1,0:T(8,128)(2,1)S(1)} %collective-permute-done.6.received), custom_call_target="tpu_custom_call" | custom-call | flops 201326592 | tf_op jit(solution)/shard_map/work/pallas_call | solution.py:127
  17.7 4.9 %collective-permute-start.7 = (bf16[2,256,256]{2,1,0:T(8,128)(2,1)S(1)}, bf16[2,256,256]{2,1,0:T(8,128)(2,1)S(1)}, u32[]{:S(2)}, u32[]{:S(2)}) collective-permute-start(bf16[2,256,256]{2,1,0:T(8,128)(2,1)S(1)} %get-tuple-element.32), channel_id=1, source_target_pairs={{0,256},{1,257},{2,258},{3,259},{4,260},{5,261},{6,262},{7,263},{8... | collective-permute-start | bytes 786440 | tf_op jit(solution)/shard_map/ppermute | solution.py:158
  22.7 0.0 collective-permute-done.4.received
  22.7 0.9 %work.6 = (bf16[2,256,256]{2,1,0:T(8,128)(2,1)S(1)}, bf16[2,256,256]{2,1,0:T(8,128)(2,1)S(1)}) custom-call(s32[1]{0:T(128)} %bitcast.role_ref, bf16[2,256,256]{2,1,0:T(8,128)(2,1)S(1)} %get-tuple-element.27.own, bf16[2,256,256]{2,1,0:T(8,128)(2,1)S(1)} %collective-permute-done.4.received), custom_call_target="tpu_custom_call" | custom-call | flops 201326592 | tf_op jit(solution)/shard_map/work/pallas_call | solution.py:127
  23.6 2.4 %collective-permute-start.5 = (bf16[2,256,256]{2,1,0:T(8,128)(2,1)S(1)}, bf16[2,256,256]{2,1,0:T(8,128)(2,1)S(1)}, u32[]{:S(2)}, u32[]{:S(2)}) collective-permute-start(bf16[2,256,256]{2,1,0:T(8,128)(2,1)S(1)} %get-tuple-element.29), channel_id=1, source_target_pairs={{0,256},{1,257},{2,258},{3,259},{4,260},{5,261},{6,262},{7,263},{8... | collective-permute-start | bytes 786440 | tf_op jit(solution)/shard_map/ppermute | solution.py:158
  26.0 0.0 collective-permute-done.2.received
  26.0 0.9 %work.5 = (bf16[2,256,256]{2,1,0:T(8,128)(2,1)S(1)}, bf16[2,256,256]{2,1,0:T(8,128)(2,1)S(1)}) custom-call(s32[1]{0:T(128)} %bitcast.role_ref, bf16[2,256,256]{2,1,0:T(8,128)(2,1)S(1)} %get-tuple-element.24.own, bf16[2,256,256]{2,1,0:T(8,128)(2,1)S(1)} %collective-permute-done.2.received), custom_call_target="tpu_custom_call" | custom-call | flops 201326592 | tf_op jit(solution)/shard_map/work/pallas_call | solution.py:127
  26.9 4.9 %collective-permute-start.3 = (bf16[2,256,256]{2,1,0:T(8,128)(2,1)S(1)}, bf16[2,256,256]{2,1,0:T(8,128)(2,1)S(1)}, u32[]{:S(2)}, u32[]{:S(2)}) collective-permute-start(bf16[2,256,256]{2,1,0:T(8,128)(2,1)S(1)} %get-tuple-element.26), channel_id=1, source_target_pairs={{0,256},{1,257},{2,258},{3,259},{4,260},{5,261},{6,262},{7,263},{8... | collective-permute-start | bytes 786440 | tf_op jit(solution)/shard_map/ppermute | solution.py:158
  31.9 0.0 collective-permute-done.received
  31.9 0.9 %work.4 = (bf16[2,256,256]{2,1,0:T(8,128)(2,1)S(1)}, bf16[2,256,256]{2,1,0:T(8,128)(2,1)S(1)}) custom-call(s32[1]{0:T(128)} %bitcast.role_ref, bf16[2,256,256]{2,1,0:T(8,128)(2,1)S(1)} %get-tuple-element.21.own, bf16[2,256,256]{2,1,0:T(8,128)(2,1)S(1)} %collective-permute-done.received), custom_call_target="tpu_custom_call" | custom-call | flops 201326592 | tf_op jit(solution)/shard_map/work/pallas_call | solution.py:127
  32.8 4.3 %collective-permute-start.1 = (bf16[2,256,256]{2,1,0:T(8,128)(2,1)S(1)}, bf16[2,256,256]{2,1,0:T(8,128)(2,1)S(1)}, u32[]{:S(2)}, u32[]{:S(2)}) collective-permute-start(bf16[2,256,256]{2,1,0:T(8,128)(2,1)S(1)} %get-tuple-element.23), channel_id=1, source_target_pairs={{0,256},{1,257},{2,258},{3,259},{4,260},{5,261},{6,262},{7,263},{8... | collective-permute-start | bytes 786440 | tf_op jit(solution)/shard_map/ppermute | solution.py:158
  37.1 1.0 %place.5.rest_1_ = bf16[256,4096]{1,0:T(8,128)(2,1)} custom-call(s32[1]{0:T(128)} %bitcast.role_ref, bf16[2,256,256]{2,1,0:T(8,128)(2,1)S(1)} %get-tuple-element.33.rest_0_, bf16[2,256,256]{2,1,0:T(8,128)(2,1)S(1)} %get-tuple-element.34.rest_1_, bf16[2,256,256]{2,1,0:T(8,128)(2,1)S(1)} %get-tuple-element.35.rest_2_, ...), custom_call_target="tpu_custom_call" | custom-call | tf_op jit(solution)/shard_map/place/pallas_call | solution.py:139
  38.2 0.0 collective-permute-done.7.rest_0_
  38.2 0.7 %place.6.rest_1_ = bf16[256,4096]{1,0:T(8,128)(2,1)} custom-call(s32[1]{0:T(128)} %bitcast.role_ref, bf16[2,256,256]{2,1,0:T(8,128)(2,1)S(1)} %collective-permute-done.7.rest_0_, bf16[256,4096]{1,0:T(8,128)(2,1)} %place.5.rest_1_), custom_call_target="tpu_custom_call", output_to_operand_aliasing={{}: (2, {})} | custom-call | tf_op jit(solution)/shard_map/place/pallas_call | solution.py:139
  38.9 3.4 %collective-permute-done.5.rest_0_ = bf16[2,256,256]{2,1,0:T(8,128)(2,1)S(1)} collective-permute-done((bf16[2,256,256]{2,1,0:T(8,128)(2,1)S(1)}, bf16[2,256,256]{2,1,0:T(8,128)(2,1)S(1)}, u32[]{:S(2)}, u32[]{:S(2)}) %collective-permute-start.5) | collective-permute-done | bytes 262176 | tf_op jit(solution)/shard_map/ppermute | solution.py:158
  42.3 0.7 %place.7.rest_1_ = bf16[256,4096]{1,0:T(8,128)(2,1)} custom-call(s32[1]{0:T(128)} %bitcast.role_ref, bf16[2,256,256]{2,1,0:T(8,128)(2,1)S(1)} %collective-permute-done.5.rest_0_, bf16[256,4096]{1,0:T(8,128)(2,1)} %place.6.rest_1_), custom_call_target="tpu_custom_call", output_to_operand_aliasing={{}: (2, {})} | custom-call | tf_op jit(solution)/shard_map/place/pallas_call | solution.py:139
  43.0 4.9 %collective-permute-done.3.rest_0_ = bf16[2,256,256]{2,1,0:T(8,128)(2,1)S(1)} collective-permute-done((bf16[2,256,256]{2,1,0:T(8,128)(2,1)S(1)}, bf16[2,256,256]{2,1,0:T(8,128)(2,1)S(1)}, u32[]{:S(2)}, u32[]{:S(2)}) %collective-permute-start.3) | collective-permute-done | bytes 262176 | tf_op jit(solution)/shard_map/ppermute | solution.py:158
  47.9 0.7 %place.8.rest_1_ = bf16[256,4096]{1,0:T(8,128)(2,1)} custom-call(s32[1]{0:T(128)} %bitcast.role_ref, bf16[2,256,256]{2,1,0:T(8,128)(2,1)S(1)} %collective-permute-done.3.rest_0_, bf16[256,4096]{1,0:T(8,128)(2,1)} %place.7.rest_1_), custom_call_target="tpu_custom_call", output_to_operand_aliasing={{}: (2, {})} | custom-call | tf_op jit(solution)/shard_map/place/pallas_call | solution.py:139
  48.6 4.0 %collective-permute-done.1.rest_0_ = bf16[2,256,256]{2,1,0:T(8,128)(2,1)S(1)} collective-permute-done((bf16[2,256,256]{2,1,0:T(8,128)(2,1)S(1)}, bf16[2,256,256]{2,1,0:T(8,128)(2,1)S(1)}, u32[]{:S(2)}, u32[]{:S(2)}) %collective-permute-start.1) | collective-permute-done | bytes 262176 | tf_op jit(solution)/shard_map/ppermute | solution.py:158
  52.6 0.7 %place.9 = bf16[256,4096]{1,0:T(8,128)(2,1)} custom-call(s32[1]{0:T(128)} %bitcast.role_ref, bf16[2,256,256]{2,1,0:T(8,128)(2,1)S(1)} %collective-permute-done.1.rest_0_, bf16[256,4096]{1,0:T(8,128)(2,1)} %place.8.rest_1_), custom_call_target="tpu_custom_call", output_to_operand_aliasing={{}: (2, {})} | custom-call | tf_op jit(solution)/shard_map/place/pallas_call | solution.py:139
Async XLA Ops:
  0.0 1.6 %copy-start = (bf16[1,1,256,4096]{3,2,1,0:T(8,128)(2,1)S(1)}, bf16[1,1,256,4096]{3,2,1,0:T(8,128)(2,1)}, u32[]{:S(2)}) copy-start(bf16[1,1,256,4096]{3,2,1,0:T(8,128)(2,1)} %param.1) | copy-start | bytes 6291460
  1.8 15.0 %collective-permute-start.6 = (bf16[2,256,256]{2,1,0:T(8,128)(2,1)S(1)}, bf16[2,256,256]{2,1,0:T(8,128)(2,1)S(1)}, u32[]{:S(2)}, u32[]{:S(2)}) collective-permute-start(bf16[2,256,256]{2,1,0:T(8,128)(2,1)S(1)} %get-tuple-element.31), channel_id=1, source_target_pairs={{0,256},{1,257},{2,258},{3,259},{4,260},{5,261},{6,262},{7,263},{8... | collective-permute-start | bytes 786440 | tf_op jit(solution)/shard_map/ppermute | solution.py:152
  6.8 15.9 %collective-permute-start.4 = (bf16[2,256,256]{2,1,0:T(8,128)(2,1)S(1)}, bf16[2,256,256]{2,1,0:T(8,128)(2,1)S(1)}, u32[]{:S(2)}, u32[]{:S(2)}) collective-permute-start(bf16[2,256,256]{2,1,0:T(8,128)(2,1)S(1)} %get-tuple-element.28), channel_id=1, source_target_pairs={{0,256},{1,257},{2,258},{3,259},{4,260},{5,261},{6,262},{7,263},{8... | collective-permute-start | bytes 786440 | tf_op jit(solution)/shard_map/ppermute | solution.py:152
  9.2 16.8 %collective-permute-start.2 = (bf16[2,256,256]{2,1,0:T(8,128)(2,1)S(1)}, bf16[2,256,256]{2,1,0:T(8,128)(2,1)S(1)}, u32[]{:S(2)}, u32[]{:S(2)}) collective-permute-start(bf16[2,256,256]{2,1,0:T(8,128)(2,1)S(1)} %get-tuple-element.25), channel_id=1, source_target_pairs={{0,256},{1,257},{2,258},{3,259},{4,260},{5,261},{6,262},{7,263},{8... | collective-permute-start | bytes 786440 | tf_op jit(solution)/shard_map/ppermute | solution.py:152
  14.1 17.7 %collective-permute-start = (bf16[2,256,256]{2,1,0:T(8,128)(2,1)S(1)}, bf16[2,256,256]{2,1,0:T(8,128)(2,1)S(1)}, u32[]{:S(2)}, u32[]{:S(2)}) collective-permute-start(bf16[2,256,256]{2,1,0:T(8,128)(2,1)S(1)} %get-tuple-element.22), channel_id=1, source_target_pairs={{0,256},{1,257},{2,258},{3,259},{4,260},{5,261},{6,262},{7,263},{8... | collective-permute-start | bytes 786440 | tf_op jit(solution)/shard_map/ppermute | solution.py:152
  17.7 20.4 %collective-permute-start.7 = (bf16[2,256,256]{2,1,0:T(8,128)(2,1)S(1)}, bf16[2,256,256]{2,1,0:T(8,128)(2,1)S(1)}, u32[]{:S(2)}, u32[]{:S(2)}) collective-permute-start(bf16[2,256,256]{2,1,0:T(8,128)(2,1)S(1)} %get-tuple-element.32), channel_id=1, source_target_pairs={{0,256},{1,257},{2,258},{3,259},{4,260},{5,261},{6,262},{7,263},{8... | collective-permute-start | bytes 786440 | tf_op jit(solution)/shard_map/ppermute | solution.py:158
  23.6 18.7 %collective-permute-start.5 = (bf16[2,256,256]{2,1,0:T(8,128)(2,1)S(1)}, bf16[2,256,256]{2,1,0:T(8,128)(2,1)S(1)}, u32[]{:S(2)}, u32[]{:S(2)}) collective-permute-start(bf16[2,256,256]{2,1,0:T(8,128)(2,1)S(1)} %get-tuple-element.29), channel_id=1, source_target_pairs={{0,256},{1,257},{2,258},{3,259},{4,260},{5,261},{6,262},{7,263},{8... | collective-permute-start | bytes 786440 | tf_op jit(solution)/shard_map/ppermute | solution.py:158
  26.9 20.9 %collective-permute-start.3 = (bf16[2,256,256]{2,1,0:T(8,128)(2,1)S(1)}, bf16[2,256,256]{2,1,0:T(8,128)(2,1)S(1)}, u32[]{:S(2)}, u32[]{:S(2)}) collective-permute-start(bf16[2,256,256]{2,1,0:T(8,128)(2,1)S(1)} %get-tuple-element.26), channel_id=1, source_target_pairs={{0,256},{1,257},{2,258},{3,259},{4,260},{5,261},{6,262},{7,263},{8... | collective-permute-start | bytes 786440 | tf_op jit(solution)/shard_map/ppermute | solution.py:158
  32.8 19.8 %collective-permute-start.1 = (bf16[2,256,256]{2,1,0:T(8,128)(2,1)S(1)}, bf16[2,256,256]{2,1,0:T(8,128)(2,1)S(1)}, u32[]{:S(2)}, u32[]{:S(2)}) collective-permute-start(bf16[2,256,256]{2,1,0:T(8,128)(2,1)S(1)} %get-tuple-element.23), channel_id=1, source_target_pairs={{0,256},{1,257},{2,258},{3,259},{4,260},{5,261},{6,262},{7,263},{8... | collective-permute-start | bytes 786440 | tf_op jit(solution)/shard_map/ppermute | solution.py:158

commit v3 on v2

--- a/solution.py
+++ b/solution.py
@@ -11,12 +11,13 @@
 INNER = 2048
 KEPT = INNER // 2
 CHUNKS = (1, 1, 1, 1)
+EARLY = 2
 FACTOR = HEAD ** (-0.5)
 VMEM_LIMIT = 12 * 1024 * 1024
 
-SMEM = pl.BlockSpec(memory_space=pltpu.SMEM)
 VMEM = pl.BlockSpec(memory_space=pltpu.VMEM)
 ANY = pl.BlockSpec(memory_space=pl.ANY)
+HBM = pl.BlockSpec(memory_space=pltpu.HBM)
 PARAMS = pltpu.CompilerParams(vmem_limit_bytes=VMEM_LIMIT)
 
 
@@ -43,6 +44,11 @@
     return [block.at[:, pl.ds(pl.multiple_of(i * INNER + at, HEAD), width)] for i in range(2)]
 
 
+def side(kept):
+    role = lax.axis_index("group")
+    return role if kept else 1 - role
+
+
 def run_copies(copies):
     for copy in copies:
         copy.start()
@@ -50,19 +56,18 @@
         copy.wait()
 
 
-def load_kernel(kept, role_ref, block, *rest):
+def load_kernel(parts, block, *rest):
     *chunks, sems = rest
-    at = (role_ref[0] if kept else 1 - role_ref[0]) * KEPT
     copies = []
-    for i, chunk in enumerate(chunks):
+    for i, ((kept, first), chunk) in enumerate(zip(parts, chunks)):
+        at = side(kept) * KEPT + first
         for j, view in enumerate(views(block, at, chunk.shape[-1])):
             copies.append(pltpu.make_async_copy(view, chunk.at[j], sems.at[i, j]))
-        at = at + chunk.shape[-1]
     run_copies(copies)
 
 
-def work_kernel(width, role_ref, own, received, kept, back):
-    role = role_ref[0]
+def work_kernel(width, own, received, kept, back):
+    role = lax.axis_index("group")
 
     def run(decoder):
         query_side, key_side = (own, received) if decoder else (received, own)
@@ -81,11 +86,11 @@
     pl.when(role == 0)(lambda: run(False))
 
 
-def place_kernel(kept, firsts, aliased, role_ref, *rest):
+def place_kernel(kept, firsts, aliased, *rest):
     *chunks, out, sems = rest
     if aliased:
         chunks = chunks[:-1]
-    at = (role_ref[0] if kept else 1 - role_ref[0]) * KEPT
+    at = side(kept) * KEPT
     copies = []
     for i, (first, chunk) in enumerate(zip(firsts, chunks)):
         for j, view in enumerate(views(out, at + first, chunk.shape[-1])):
@@ -103,54 +108,54 @@
 
 def local(operands):
     rows, both = operands.shape[2:]
-    block = operands.reshape(rows, both)
-    role = lax.axis_index("group").astype(jnp.int32).reshape(1)
     count = lax.axis_size("dp")
     pairs = [(i, (i + count) % (2 * count)) for i in range(2 * count)]
     widths = [n * HEAD for n in CHUNKS]
     firsts = [sum(widths[:i]) for i in range(len(widths))]
     n = len(widths)
 
-    def load(kept):
+    def load(parts, block):
         return pl.pallas_call(
-            functools.partial(load_kernel, kept),
-            out_shape=[chunk_shape(rows, w) for w in widths],
-            in_specs=[SMEM, ANY],
-            out_specs=[VMEM] * n,
-            scratch_shapes=[pltpu.SemaphoreType.DMA((n, 2))],
+            functools.partial(load_kernel, [(kept, firsts[i]) for kept, i in parts]),
+            out_shape=[pltpu.VMEM((2, rows, widths[i]), jnp.bfloat16) for _, i in parts],
+            in_specs=[HBM],
+            out_specs=[VMEM] * len(parts),
+            scratch_shapes=[pltpu.SemaphoreType.DMA((len(parts), 2))],
             compiler_params=PARAMS,
-            cost_estimate=cost(rows * both),
-            name="keep" if kept else "pack",
-        )(role, block)
+            cost_estimate=cost(0),
+            name="load",
+        )(block)
 
     def work(width, own, received):
         return pl.pallas_call(
             functools.partial(work_kernel, width),
             out_shape=[chunk_shape(rows, width)] * 2,
-            in_specs=[SMEM, VMEM, VMEM],
+            in_specs=[VMEM, VMEM],
             out_specs=[VMEM, VMEM],
             compiler_params=PARAMS,
             cost_estimate=cost(0, flops=12 * rows * rows * width, exps=rows * width),
             name="work",
-        )(role, own, received)
+        )(own, received)
 
     def place(kept, at, chunks, out=None):
         extra = [] if out is None else [out]
         return pl.pallas_call(
             functools.partial(place_kernel, kept, at, bool(extra)),
             out_shape=jax.ShapeDtypeStruct((rows, both), jnp.bfloat16),
-            in_specs=[SMEM] + [VMEM] * len(chunks) + [ANY] * len(extra),
+            in_specs=[VMEM] * len(chunks) + [ANY] * len(extra),
             out_specs=ANY,
             scratch_shapes=[pltpu.SemaphoreType.DMA((len(chunks), 2))],
-            input_output_aliases={1 + len(chunks): 0} if extra else {},
+            input_output_aliases={len(chunks): 0} if extra else {},
             compiler_params=PARAMS,
             cost_estimate=cost(0),
             name="place",
-        )(role, *chunks, *extra)
+        )(*chunks, *extra)
 
-    sent = load(False)
+    block = pltpu.with_memory_space_constraint(operands.reshape(rows, both), pltpu.HBM)
+    sent = load([(False, i) for i in range(EARLY)], block)
+    rest = load([(False, i) for i in range(EARLY, n)] + [(True, i) for i in range(n)], block)
+    sent, own = sent + rest[: n - EARLY], rest[n - EARLY :]
     received = [lax.ppermute(c, ("group", "dp"), pairs) for c in sent]
-    own = load(True)
     done, returned = [], []
     for i in range(n):
         kept, back = work(widths[i], own[i], received[i])

time: 53.7 us -> 53 us (0.987)
  Pallas kernels: 7.99 us -> 10.3 us
  local copies, waits for them, and re-layouts: 1.59 us -> 0 us
  starting transfers between devices: 31.3 us -> 29.9 us
    pallas_call x2, Pallas kernels: 0.48 us -> 2.71 us  [load(): pl.pallas_call(functools.partial(load_kernel, [(kept, firsts[i]) for kept...]
    unnamed x2 -> x0, local copies, waits for them, and re-layouts: 1.59 us -> none
    ppermute x4, starting transfers between devices: 16.6 us -> 15.2 us  [local(): returned.append(lax.ppermute(back, ('group', 'dp'), pairs))]
  transfers between devices with their start and end apart: 8 -> 8, of which waited for: 3 -> 3; matrix products, arithmetic and copies ran while one was open for 0% -> 0% of each run, Pallas kernels for 13% -> 16%
where the time goes in v3:
time: 53 us; the launch traced here: 52.6 us
  starting transfers between devices  29.9 us (56%)
  waiting for transfers between devices  12.3 us (23%)
  Pallas kernels  10.3 us (19%)
    ppermute x4, starting transfers between devices, local(): returned.append(lax.ppermute(back, ('group', 'dp'), pairs))  15.2 us
    ppermute x4, starting transfers between devices, local(): received = [lax.ppermute(c, ('group', 'dp'), pairs) for c in sent]  14.7 us
    ppermute x4, waiting for transfers between devices, local(): returned.append(lax.ppermute(back, ('group', 'dp'), pairs))  12.2 us
    pallas_call x5, Pallas kernels, place(): pl.pallas_call(functools.partial(place_kernel, kept, at, bool(extra)), ou...  3.91 us
    pallas_call x4, Pallas kernels, work(): pl.pallas_call(functools.partial(work_kernel, width), out_shape=[chunk_sh...  3.63 us
    pallas_call x2, Pallas kernels, load(): pl.pallas_call(functools.partial(load_kernel, [(kept, firsts[i]) for kept...  2.71 us
  transfers between devices with their start and end apart: 8, of which 3 were waited for; matrix products, arithmetic and copies ran while one was open for 0% of the time, Pallas kernels for 16%

profile of v3, /device:TPU:56, one launch (start us, length us, event | category | flops | bytes accessed | tf_op | source)
XLA Modules:
  0.0 52.6 jit_solution(17098743299949833961)
XLA Ops:
  0.0 1.1 %load.3 = (bf16[2,256,256]{2,1,0:T(8,128)(2,1)S(1)}, bf16[2,256,256]{2,1,0:T(8,128)(2,1)S(1)}) custom-call(bf16[256,4096]{1,0:T(8,128)(2,1)} %bitcast.2), custom_call_target="tpu_custom_call" | custom-call | tf_op jit(solution)/shard_map/load/pallas_call | solution.py:118
  1.1 4.9 %collective-permute-start.6 = (bf16[2,256,256]{2,1,0:T(8,128)(2,1)S(1)}, bf16[2,256,256]{2,1,0:T(8,128)(2,1)S(1)}, u32[]{:S(2)}, u32[]{:S(2)}) collective-permute-start(bf16[2,256,256]{2,1,0:T(8,128)(2,1)S(1)} %get-tuple-element.31), channel_id=1, source_target_pairs={{0,256},{1,257},{2,258},{3,259},{4,260},{5,261},{6,262},{7,263},{8... | collective-permute-start | bytes 786440 | tf_op jit(solution)/shard_map/ppermute | solution.py:158
  6.1 2.4 %collective-permute-start.4 = (bf16[2,256,256]{2,1,0:T(8,128)(2,1)S(1)}, bf16[2,256,256]{2,1,0:T(8,128)(2,1)S(1)}, u32[]{:S(2)}, u32[]{:S(2)}) collective-permute-start(bf16[2,256,256]{2,1,0:T(8,128)(2,1)S(1)} %get-tuple-element.28), channel_id=1, source_target_pairs={{0,256},{1,257},{2,258},{3,259},{4,260},{5,261},{6,262},{7,263},{8... | collective-permute-start | bytes 786440 | tf_op jit(solution)/shard_map/ppermute | solution.py:158
  8.5 1.6 %load.2 = (bf16[2,256,256]{2,1,0:T(8,128)(2,1)S(1)}, bf16[2,256,256]{2,1,0:T(8,128)(2,1)S(1)}, bf16[2,256,256]{2,1,0:T(8,128)(2,1)S(1)}, bf16[2,256,256]{2,1,0:T...) custom-call(bf16[256,4096]{1,0:T(8,128)(2,1)} %bitcast.3), custom_call_target="tpu_custom_call" | custom-call | tf_op jit(solution)/shard_map/load/pallas_call | solution.py:118
  10.1 4.9 %collective-permute-start.2 = (bf16[2,256,256]{2,1,0:T(8,128)(2,1)S(1)}, bf16[2,256,256]{2,1,0:T(8,128)(2,1)S(1)}, u32[]{:S(2)}, u32[]{:S(2)}) collective-permute-start(bf16[2,256,256]{2,1,0:T(8,128)(2,1)S(1)} %get-tuple-element.25), channel_id=1, source_target_pairs={{0,256},{1,257},{2,258},{3,259},{4,260},{5,261},{6,262},{7,263},{8... | collective-permute-start | bytes 786440 | tf_op jit(solution)/shard_map/ppermute | solution.py:158
  15.0 2.4 %collective-permute-start = (bf16[2,256,256]{2,1,0:T(8,128)(2,1)S(1)}, bf16[2,256,256]{2,1,0:T(8,128)(2,1)S(1)}, u32[]{:S(2)}, u32[]{:S(2)}) collective-permute-start(bf16[2,256,256]{2,1,0:T(8,128)(2,1)S(1)} %get-tuple-element.22), channel_id=1, source_target_pairs={{0,256},{1,257},{2,258},{3,259},{4,260},{5,261},{6,262},{7,263},{8... | collective-permute-start | bytes 786440 | tf_op jit(solution)/shard_map/ppermute | solution.py:158
  17.5 0.0 collective-permute-done.6.received
  17.5 0.9 %work.7 = (bf16[2,256,256]{2,1,0:T(8,128)(2,1)S(1)}, bf16[2,256,256]{2,1,0:T(8,128)(2,1)S(1)}) custom-call(bf16[2,256,256]{2,1,0:T(8,128)(2,1)S(1)} %get-tuple-element.30.own, bf16[2,256,256]{2,1,0:T(8,128)(2,1)S(1)} %collective-permute-done.6.received), custom_call_target="tpu_custom_call" | custom-call | flops 201326592 | tf_op jit(solution)/shard_map/work/pallas_call | solution.py:130
  18.4 4.9 %collective-permute-start.7 = (bf16[2,256,256]{2,1,0:T(8,128)(2,1)S(1)}, bf16[2,256,256]{2,1,0:T(8,128)(2,1)S(1)}, u32[]{:S(2)}, u32[]{:S(2)}) collective-permute-start(bf16[2,256,256]{2,1,0:T(8,128)(2,1)S(1)} %get-tuple-element.32), channel_id=1, source_target_pairs={{0,256},{1,257},{2,258},{3,259},{4,260},{5,261},{6,262},{7,263},{8... | collective-permute-start | bytes 786440 | tf_op jit(solution)/shard_map/ppermute | solution.py:163
  23.3 0.0 collective-permute-done.4.received
  23.3 0.9 %work.6 = (bf16[2,256,256]{2,1,0:T(8,128)(2,1)S(1)}, bf16[2,256,256]{2,1,0:T(8,128)(2,1)S(1)}) custom-call(bf16[2,256,256]{2,1,0:T(8,128)(2,1)S(1)} %get-tuple-element.27.own, bf16[2,256,256]{2,1,0:T(8,128)(2,1)S(1)} %collective-permute-done.4.received), custom_call_target="tpu_custom_call" | custom-call | flops 201326592 | tf_op jit(solution)/shard_map/work/pallas_call | solution.py:130
  24.3 2.4 %collective-permute-start.5 = (bf16[2,256,256]{2,1,0:T(8,128)(2,1)S(1)}, bf16[2,256,256]{2,1,0:T(8,128)(2,1)S(1)}, u32[]{:S(2)}, u32[]{:S(2)}) collective-permute-start(bf16[2,256,256]{2,1,0:T(8,128)(2,1)S(1)} %get-tuple-element.29), channel_id=1, source_target_pairs={{0,256},{1,257},{2,258},{3,259},{4,260},{5,261},{6,262},{7,263},{8... | collective-permute-start | bytes 786440 | tf_op jit(solution)/shard_map/ppermute | solution.py:163
  26.7 0.0 collective-permute-done.2.received
  26.7 0.9 %work.5 = (bf16[2,256,256]{2,1,0:T(8,128)(2,1)S(1)}, bf16[2,256,256]{2,1,0:T(8,128)(2,1)S(1)}) custom-call(bf16[2,256,256]{2,1,0:T(8,128)(2,1)S(1)} %get-tuple-element.24.own, bf16[2,256,256]{2,1,0:T(8,128)(2,1)S(1)} %collective-permute-done.2.received), custom_call_target="tpu_custom_call" | custom-call | flops 201326592 | tf_op jit(solution)/shard_map/work/pallas_call | solution.py:130
  27.6 4.9 %collective-permute-start.3 = (bf16[2,256,256]{2,1,0:T(8,128)(2,1)S(1)}, bf16[2,256,256]{2,1,0:T(8,128)(2,1)S(1)}, u32[]{:S(2)}, u32[]{:S(2)}) collective-permute-start(bf16[2,256,256]{2,1,0:T(8,128)(2,1)S(1)} %get-tuple-element.26), channel_id=1, source_target_pairs={{0,256},{1,257},{2,258},{3,259},{4,260},{5,261},{6,262},{7,263},{8... | collective-permute-start | bytes 786440 | tf_op jit(solution)/shard_map/ppermute | solution.py:163
  32.5 0.0 collective-permute-done.received
  32.6 0.9 %work.4 = (bf16[2,256,256]{2,1,0:T(8,128)(2,1)S(1)}, bf16[2,256,256]{2,1,0:T(8,128)(2,1)S(1)}) custom-call(bf16[2,256,256]{2,1,0:T(8,128)(2,1)S(1)} %get-tuple-element.21.own, bf16[2,256,256]{2,1,0:T(8,128)(2,1)S(1)} %collective-permute-done.received), custom_call_target="tpu_custom_call" | custom-call | flops 201326592 | tf_op jit(solution)/shard_map/work/pallas_call | solution.py:130
  33.5 3.0 %collective-permute-start.1 = (bf16[2,256,256]{2,1,0:T(8,128)(2,1)S(1)}, bf16[2,256,256]{2,1,0:T(8,128)(2,1)S(1)}, u32[]{:S(2)}, u32[]{:S(2)}) collective-permute-start(bf16[2,256,256]{2,1,0:T(8,128)(2,1)S(1)} %get-tuple-element.23), channel_id=1, source_target_pairs={{0,256},{1,257},{2,258},{3,259},{4,260},{5,261},{6,262},{7,263},{8... | collective-permute-start | bytes 786440 | tf_op jit(solution)/shard_map/ppermute | solution.py:163
  36.4 1.0 %place.5.rest_1_ = bf16[256,4096]{1,0:T(8,128)(2,1)} custom-call(bf16[2,256,256]{2,1,0:T(8,128)(2,1)S(1)} %get-tuple-element.33.rest_0_, bf16[2,256,256]{2,1,0:T(8,128)(2,1)S(1)} %get-tuple-element.34.rest_1_, bf16[2,256,256]{2,1,0:T(8,128)(2,1)S(1)} %get-tuple-element.35.rest_2_, bf16[2,256,256]{2,1,0:T(8,128)(2,1)S(1)} %get-tuple-element.36.rest_3_), custom_call_target="tpu_custom_call" | custom-call | tf_op jit(solution)/shard_map/place/pallas_call | solution.py:142
  37.5 0.0 collective-permute-done.7.rest_0_
  37.5 0.7 %place.6.rest_1_ = bf16[256,4096]{1,0:T(8,128)(2,1)} custom-call(bf16[2,256,256]{2,1,0:T(8,128)(2,1)S(1)} %collective-permute-done.7.rest_0_, bf16[256,4096]{1,0:T(8,128)(2,1)} %place.5.rest_1_), custom_call_target="tpu_custom_call", output_to_operand_aliasing={{}: (1, {})} | custom-call | tf_op jit(solution)/shard_map/place/pallas_call | solution.py:142
  38.2 3.3 %collective-permute-done.5.rest_0_ = bf16[2,256,256]{2,1,0:T(8,128)(2,1)S(1)} collective-permute-done((bf16[2,256,256]{2,1,0:T(8,128)(2,1)S(1)}, bf16[2,256,256]{2,1,0:T(8,128)(2,1)S(1)}, u32[]{:S(2)}, u32[]{:S(2)}) %collective-permute-start.5) | collective-permute-done | bytes 262176 | tf_op jit(solution)/shard_map/ppermute | solution.py:163
  41.6 0.7 %place.7.rest_1_ = bf16[256,4096]{1,0:T(8,128)(2,1)} custom-call(bf16[2,256,256]{2,1,0:T(8,128)(2,1)S(1)} %collective-permute-done.5.rest_0_, bf16[256,4096]{1,0:T(8,128)(2,1)} %place.6.rest_1_), custom_call_target="tpu_custom_call", output_to_operand_aliasing={{}: (1, {})} | custom-call | tf_op jit(solution)/shard_map/place/pallas_call | solution.py:142
  42.3 4.9 %collective-permute-done.3.rest_0_ = bf16[2,256,256]{2,1,0:T(8,128)(2,1)S(1)} collective-permute-done((bf16[2,256,256]{2,1,0:T(8,128)(2,1)S(1)}, bf16[2,256,256]{2,1,0:T(8,128)(2,1)S(1)}, u32[]{:S(2)}, u32[]{:S(2)}) %collective-permute-start.3) | collective-permute-done | bytes 262176 | tf_op jit(solution)/shard_map/ppermute | solution.py:163
  47.2 0.7 %place.8.rest_1_ = bf16[256,4096]{1,0:T(8,128)(2,1)} custom-call(bf16[2,256,256]{2,1,0:T(8,128)(2,1)S(1)} %collective-permute-done.3.rest_0_, bf16[256,4096]{1,0:T(8,128)(2,1)} %place.7.rest_1_), custom_call_target="tpu_custom_call", output_to_operand_aliasing={{}: (1, {})} | custom-call | tf_op jit(solution)/shard_map/place/pallas_call | solution.py:142
  47.9 4.0 %collective-permute-done.1.rest_0_ = bf16[2,256,256]{2,1,0:T(8,128)(2,1)S(1)} collective-permute-done((bf16[2,256,256]{2,1,0:T(8,128)(2,1)S(1)}, bf16[2,256,256]{2,1,0:T(8,128)(2,1)S(1)}, u32[]{:S(2)}, u32[]{:S(2)}) %collective-permute-start.1) | collective-permute-done | bytes 262176 | tf_op jit(solution)/shard_map/ppermute | solution.py:163
  51.9 0.7 %place.9 = bf16[256,4096]{1,0:T(8,128)(2,1)} custom-call(bf16[2,256,256]{2,1,0:T(8,128)(2,1)S(1)} %collective-permute-done.1.rest_0_, bf16[256,4096]{1,0:T(8,128)(2,1)} %place.8.rest_1_), custom_call_target="tpu_custom_call", output_to_operand_aliasing={{}: (1, {})} | custom-call | tf_op jit(solution)/shard_map/place/pallas_call | solution.py:142
Async XLA Ops:
  1.1 16.3 %collective-permute-start.6 = (bf16[2,256,256]{2,1,0:T(8,128)(2,1)S(1)}, bf16[2,256,256]{2,1,0:T(8,128)(2,1)S(1)}, u32[]{:S(2)}, u32[]{:S(2)}) collective-permute-start(bf16[2,256,256]{2,1,0:T(8,128)(2,1)S(1)} %get-tuple-element.31), channel_id=1, source_target_pairs={{0,256},{1,257},{2,258},{3,259},{4,260},{5,261},{6,262},{7,263},{8... | collective-permute-start | bytes 786440 | tf_op jit(solution)/shard_map/ppermute | solution.py:158
  6.1 17.2 %collective-permute-start.4 = (bf16[2,256,256]{2,1,0:T(8,128)(2,1)S(1)}, bf16[2,256,256]{2,1,0:T(8,128)(2,1)S(1)}, u32[]{:S(2)}, u32[]{:S(2)}) collective-permute-start(bf16[2,256,256]{2,1,0:T(8,128)(2,1)S(1)} %get-tuple-element.28), channel_id=1, source_target_pairs={{0,256},{1,257},{2,258},{3,259},{4,260},{5,261},{6,262},{7,263},{8... | collective-permute-start | bytes 786440 | tf_op jit(solution)/shard_map/ppermute | solution.py:158
  10.1 16.6 %collective-permute-start.2 = (bf16[2,256,256]{2,1,0:T(8,128)(2,1)S(1)}, bf16[2,256,256]{2,1,0:T(8,128)(2,1)S(1)}, u32[]{:S(2)}, u32[]{:S(2)}) collective-permute-start(bf16[2,256,256]{2,1,0:T(8,128)(2,1)S(1)} %get-tuple-element.25), channel_id=1, source_target_pairs={{0,256},{1,257},{2,258},{3,259},{4,260},{5,261},{6,262},{7,263},{8... | collective-permute-start | bytes 786440 | tf_op jit(solution)/shard_map/ppermute | solution.py:158
  15.0 17.5 %collective-permute-start = (bf16[2,256,256]{2,1,0:T(8,128)(2,1)S(1)}, bf16[2,256,256]{2,1,0:T(8,128)(2,1)S(1)}, u32[]{:S(2)}, u32[]{:S(2)}) collective-permute-start(bf16[2,256,256]{2,1,0:T(8,128)(2,1)S(1)} %get-tuple-element.22), channel_id=1, source_target_pairs={{0,256},{1,257},{2,258},{3,259},{4,260},{5,261},{6,262},{7,263},{8... | collective-permute-start | bytes 786440 | tf_op jit(solution)/shard_map/ppermute | solution.py:158
  18.4 19.1 %collective-permute-start.7 = (bf16[2,256,256]{2,1,0:T(8,128)(2,1)S(1)}, bf16[2,256,256]{2,1,0:T(8,128)(2,1)S(1)}, u32[]{:S(2)}, u32[]{:S(2)}) collective-permute-start(bf16[2,256,256]{2,1,0:T(8,128)(2,1)S(1)} %get-tuple-element.32), channel_id=1, source_target_pairs={{0,256},{1,257},{2,258},{3,259},{4,260},{5,261},{6,262},{7,263},{8... | collective-permute-start | bytes 786440 | tf_op jit(solution)/shard_map/ppermute | solution.py:163
  24.3 17.3 %collective-permute-start.5 = (bf16[2,256,256]{2,1,0:T(8,128)(2,1)S(1)}, bf16[2,256,256]{2,1,0:T(8,128)(2,1)S(1)}, u32[]{:S(2)}, u32[]{:S(2)}) collective-permute-start(bf16[2,256,256]{2,1,0:T(8,128)(2,1)S(1)} %get-tuple-element.29), channel_id=1, source_target_pairs={{0,256},{1,257},{2,258},{3,259},{4,260},{5,261},{6,262},{7,263},{8... | collective-permute-start | bytes 786440 | tf_op jit(solution)/shard_map/ppermute | solution.py:163
  27.6 19.6 %collective-permute-start.3 = (bf16[2,256,256]{2,1,0:T(8,128)(2,1)S(1)}, bf16[2,256,256]{2,1,0:T(8,128)(2,1)S(1)}, u32[]{:S(2)}, u32[]{:S(2)}) collective-permute-start(bf16[2,256,256]{2,1,0:T(8,128)(2,1)S(1)} %get-tuple-element.26), channel_id=1, source_target_pairs={{0,256},{1,257},{2,258},{3,259},{4,260},{5,261},{6,262},{7,263},{8... | collective-permute-start | bytes 786440 | tf_op jit(solution)/shard_map/ppermute | solution.py:163
  33.5 18.4 %collective-permute-start.1 = (bf16[2,256,256]{2,1,0:T(8,128)(2,1)S(1)}, bf16[2,256,256]{2,1,0:T(8,128)(2,1)S(1)}, u32[]{:S(2)}, u32[]{:S(2)}) collective-permute-start(bf16[2,256,256]{2,1,0:T(8,128)(2,1)S(1)} %get-tuple-element.23), channel_id=1, source_target_pairs={{0,256},{1,257},{2,258},{3,259},{4,260},{5,261},{6,262},{7,263},{8... | collective-permute-start | bytes 786440 | tf_op jit(solution)/shard_map/ppermute | solution.py:163

commit v4 on v3

--- a/solution.py
+++ b/solution.py
@@ -10,8 +10,8 @@
 HEAD = 256
 INNER = 2048
 KEPT = INNER // 2
-CHUNKS = (1, 1, 1, 1)
-EARLY = 2
+CHUNKS = (2, 1, 1)
+EARLY = 1
 FACTOR = HEAD ** (-0.5)
 VMEM_LIMIT = 12 * 1024 * 1024
 

time: 53 us -> 52.8 us (level)
  waiting for transfers between devices: 12.3 us -> 18.7 us
  starting transfers between devices: 29.9 us -> 24.6 us
  Pallas kernels: 10.3 us -> 9.15 us
    ppermute x4 -> x3, waiting for transfers between devices: 0.01 us -> 9.13 us  [local(): received = [lax.ppermute(c, ('group', 'dp'), pairs) for c in sent]]
    ppermute x4 -> x3, starting transfers between devices: 15.2 us -> 12.3 us  [local(): returned.append(lax.ppermute(back, ('group', 'dp'), pairs))]
    ppermute x4 -> x3, waiting for transfers between devices: 12.2 us -> 9.57 us  [local(): returned.append(lax.ppermute(back, ('group', 'dp'), pairs))]
    ppermute x4 -> x3, starting transfers between devices: 14.7 us -> 12.3 us  [local(): received = [lax.ppermute(c, ('group', 'dp'), pairs) for c in sent]]
    pallas_call x5 -> x4, Pallas kernels: 3.91 us -> 3.25 us  [place(): pl.pallas_call(functools.partial(place_kernel, kept, at, bool(extra)), ou...]
    pallas_call x4 -> x3, Pallas kernels: 3.63 us -> 3.29 us  [work(): pl.pallas_call(functools.partial(work_kernel, width), out_shape=[chunk_sh...]
  transfers between devices with their start and end apart: 8 -> 6, of which waited for: 3 -> 5; matrix products, arithmetic and copies ran while one was open for 0% -> 0% of each run, Pallas kernels for 16% -> 14%
where the time goes in v4:
time: 52.8 us; the launch traced here: 52.5 us
  starting transfers between devices  24.6 us (47%)
  waiting for transfers between devices  18.7 us (35%)
  Pallas kernels  9.15 us (17%)
    ppermute x3, starting transfers between devices, local(): returned.append(lax.ppermute(back, ('group', 'dp'), pairs))  12.3 us
    ppermute x3, starting transfers between devices, local(): received = [lax.ppermute(c, ('group', 'dp'), pairs) for c in sent]  12.3 us
    ppermute x3, waiting for transfers between devices, local(): returned.append(lax.ppermute(back, ('group', 'dp'), pairs))  9.57 us
    ppermute x3, waiting for transfers between devices, local(): received = [lax.ppermute(c, ('group', 'dp'), pairs) for c in sent]  9.13 us
    pallas_call x3, Pallas kernels, work(): pl.pallas_call(functools.partial(work_kernel, width), out_shape=[chunk_sh...  3.29 us
    pallas_call x4, Pallas kernels, place(): pl.pallas_call(functools.partial(place_kernel, kept, at, bool(extra)), ou...  3.25 us
    pallas_call x2, Pallas kernels, load(): pl.pallas_call(functools.partial(load_kernel, [(kept, firsts[i]) for kept...  2.61 us
  transfers between devices with their start and end apart: 6, of which 5 were waited for; matrix products, arithmetic and copies ran while one was open for 0% of the time, Pallas kernels for 14%

profile of v4, /device:TPU:56, one launch (start us, length us, event | category | flops | bytes accessed | tf_op | source)
XLA Modules:
  0.0 52.5 jit_solution(14941634304108138383)
XLA Ops:
  0.0 1.0 %load.3 = bf16[2,256,512]{2,1,0:T(8,128)(2,1)S(1)} custom-call(bf16[256,4096]{1,0:T(8,128)(2,1)} %bitcast.2), custom_call_target="tpu_custom_call" | custom-call | tf_op jit(solution)/shard_map/load/pallas_call | solution.py:118
  1.1 4.9 %collective-permute-start.4 = (bf16[2,256,512]{2,1,0:T(8,128)(2,1)S(1)}, bf16[2,256,512]{2,1,0:T(8,128)(2,1)S(1)}, u32[]{:S(2)}, u32[]{:S(2)}) collective-permute-start(bf16[2,256,512]{2,1,0:T(8,128)(2,1)S(1)} %load.3), channel_id=1, source_target_pairs={{0,256},{1,257},{2,258},{3,259},{4,260},{5,261},{6,262},{7,263},{8... | collective-permute-start | bytes 1572872 | tf_op jit(solution)/shard_map/ppermute | solution.py:158
  6.0 1.6 %load.2 = (bf16[2,256,256]{2,1,0:T(8,128)(2,1)S(1)}, bf16[2,256,256]{2,1,0:T(8,128)(2,1)S(1)}, bf16[2,256,512]{2,1,0:T(8,128)(2,1)S(1)}, bf16[2,256,256]{2,1,0:T(8,128)(2,1)S(1)}, bf16[2,256,256]{2,1,0:T(8,128)(2,1)S(1)}) custom-call(bf16[256,4096]{1,0:T(8,128)(2,1)} %bitcast.3), custom_call_target="tpu_custom_call" | custom-call | tf_op jit(solution)/shard_map/load/pallas_call | solution.py:118
  7.6 2.4 %collective-permute-start = (bf16[2,256,256]{2,1,0:T(8,128)(2,1)S(1)}, bf16[2,256,256]{2,1,0:T(8,128)(2,1)S(1)}, u32[]{:S(2)}, u32[]{:S(2)}) collective-permute-start(bf16[2,256,256]{2,1,0:T(8,128)(2,1)S(1)} %get-tuple-element.17), channel_id=1, source_target_pairs={{0,256},{1,257},{2,258},{3,259},{4,260},{5,261},{6,262},{7,263},{8... | collective-permute-start | bytes 786440 | tf_op jit(solution)/shard_map/ppermute | solution.py:158
  10.0 4.9 %collective-permute-start.2 = (bf16[2,256,256]{2,1,0:T(8,128)(2,1)S(1)}, bf16[2,256,256]{2,1,0:T(8,128)(2,1)S(1)}, u32[]{:S(2)}, u32[]{:S(2)}) collective-permute-start(bf16[2,256,256]{2,1,0:T(8,128)(2,1)S(1)} %get-tuple-element.20), channel_id=1, source_target_pairs={{0,256},{1,257},{2,258},{3,259},{4,260},{5,261},{6,262},{7,263},{8... | collective-permute-start | bytes 786440 | tf_op jit(solution)/shard_map/ppermute | solution.py:158
  14.9 4.3 %collective-permute-done.4.received = bf16[2,256,512]{2,1,0:T(8,128)(2,1)S(1)} collective-permute-done((bf16[2,256,512]{2,1,0:T(8,128)(2,1)S(1)}, bf16[2,256,512]{2,1,0:T(8,128)(2,1)S(1)}, u32[]{:S(2)}, u32[]{:S(2)}) %collective-permute-start.4) | collective-permute-done | bytes 524320 | tf_op jit(solution)/shard_map/ppermute | solution.py:158
  19.3 1.5 %work.5 = (bf16[2,256,512]{2,1,0:T(8,128)(2,1)S(1)}, bf16[2,256,512]{2,1,0:T(8,128)(2,1)S(1)}) custom-call(bf16[2,256,512]{2,1,0:T(8,128)(2,1)S(1)} %get-tuple-element.22.own, bf16[2,256,512]{2,1,0:T(8,128)(2,1)S(1)} %collective-permute-done.4.received), custom_call_target="tpu_custom_call" | custom-call | flops 402653184 | tf_op jit(solution)/shard_map/work/pallas_call | solution.py:130
  20.8 4.9 %collective-permute-start.5 = (bf16[2,256,512]{2,1,0:T(8,128)(2,1)S(1)}, bf16[2,256,512]{2,1,0:T(8,128)(2,1)S(1)}, u32[]{:S(2)}, u32[]{:S(2)}) collective-permute-start(bf16[2,256,512]{2,1,0:T(8,128)(2,1)S(1)} %get-tuple-element.23), channel_id=1, source_target_pairs={{0,256},{1,257},{2,258},{3,259},{4,260},{5,261},{6,262},{7,263},{8... | collective-permute-start | bytes 1572872 | tf_op jit(solution)/shard_map/ppermute | solution.py:163
  25.7 4.8 %collective-permute-done.2.received = bf16[2,256,256]{2,1,0:T(8,128)(2,1)S(1)} collective-permute-done((bf16[2,256,256]{2,1,0:T(8,128)(2,1)S(1)}, bf16[2,256,256]{2,1,0:T(8,128)(2,1)S(1)}, u32[]{:S(2)}, u32[]{:S(2)}) %collective-permute-start.2) | collective-permute-done | bytes 262176 | tf_op jit(solution)/shard_map/ppermute | solution.py:158
  30.5 0.9 %work.4 = (bf16[2,256,256]{2,1,0:T(8,128)(2,1)S(1)}, bf16[2,256,256]{2,1,0:T(8,128)(2,1)S(1)}) custom-call(bf16[2,256,256]{2,1,0:T(8,128)(2,1)S(1)} %get-tuple-element.19.own, bf16[2,256,256]{2,1,0:T(8,128)(2,1)S(1)} %collective-permute-done.2.received), custom_call_target="tpu_custom_call" | custom-call | flops 201326592 | tf_op jit(solution)/shard_map/work/pallas_call | solution.py:130
  31.4 4.9 %collective-permute-start.3 = (bf16[2,256,256]{2,1,0:T(8,128)(2,1)S(1)}, bf16[2,256,256]{2,1,0:T(8,128)(2,1)S(1)}, u32[]{:S(2)}, u32[]{:S(2)}) collective-permute-start(bf16[2,256,256]{2,1,0:T(8,128)(2,1)S(1)} %get-tuple-element.21), channel_id=1, source_target_pairs={{0,256},{1,257},{2,258},{3,259},{4,260},{5,261},{6,262},{7,263},{8... | collective-permute-start | bytes 786440 | tf_op jit(solution)/shard_map/ppermute | solution.py:163
  36.3 0.0 collective-permute-done.received
  36.4 0.9 %work.3 = (bf16[2,256,256]{2,1,0:T(8,128)(2,1)S(1)}, bf16[2,256,256]{2,1,0:T(8,128)(2,1)S(1)}) custom-call(bf16[2,256,256]{2,1,0:T(8,128)(2,1)S(1)} %get-tuple-element.16.own, bf16[2,256,256]{2,1,0:T(8,128)(2,1)S(1)} %collective-permute-done.received), custom_call_target="tpu_custom_call" | custom-call | flops 201326592 | tf_op jit(solution)/shard_map/work/pallas_call | solution.py:130
  37.3 2.4 %collective-permute-start.1 = (bf16[2,256,256]{2,1,0:T(8,128)(2,1)S(1)}, bf16[2,256,256]{2,1,0:T(8,128)(2,1)S(1)}, u32[]{:S(2)}, u32[]{:S(2)}) collective-permute-start(bf16[2,256,256]{2,1,0:T(8,128)(2,1)S(1)} %get-tuple-element.18), channel_id=1, source_target_pairs={{0,256},{1,257},{2,258},{3,259},{4,260},{5,261},{6,262},{7,263},{8... | collective-permute-start | bytes 786440 | tf_op jit(solution)/shard_map/ppermute | solution.py:163
  39.7 1.0 %place.4.rest_1_ = bf16[256,4096]{1,0:T(8,128)(2,1)} custom-call(bf16[2,256,512]{2,1,0:T(8,128)(2,1)S(1)} %get-tuple-element.24.rest_0_, bf16[2,256,256]{2,1,0:T(8,128)(2,1)S(1)} %get-tuple-element.25.rest_1_, bf16[2,256,256]{2,1,0:T(8,128)(2,1)S(1)} %get-tuple-element.26.rest_2_), custom_call_target="tpu_custom_call" | custom-call | tf_op jit(solution)/shard_map/place/pallas_call | solution.py:142
  40.7 1.0 %collective-permute-done.5.rest_0_ = bf16[2,256,512]{2,1,0:T(8,128)(2,1)S(1)} collective-permute-done((bf16[2,256,512]{2,1,0:T(8,128)(2,1)S(1)}, bf16[2,256,512]{2,1,0:T(8,128)(2,1)S(1)}, u32[]{:S(2)}, u32[]{:S(2)}) %collective-permute-start.5) | collective-permute-done | bytes 524320 | tf_op jit(solution)/shard_map/ppermute | solution.py:163
  41.7 0.8 %place.5.rest_1_ = bf16[256,4096]{1,0:T(8,128)(2,1)} custom-call(bf16[2,256,512]{2,1,0:T(8,128)(2,1)S(1)} %collective-permute-done.5.rest_0_, bf16[256,4096]{1,0:T(8,128)(2,1)} %place.4.rest_1_), custom_call_target="tpu_custom_call", output_to_operand_aliasing={{}: (1, {})} | custom-call | tf_op jit(solution)/shard_map/place/pallas_call | solution.py:142
  42.5 4.8 %collective-permute-done.3.rest_0_ = bf16[2,256,256]{2,1,0:T(8,128)(2,1)S(1)} collective-permute-done((bf16[2,256,256]{2,1,0:T(8,128)(2,1)S(1)}, bf16[2,256,256]{2,1,0:T(8,128)(2,1)S(1)}, u32[]{:S(2)}, u32[]{:S(2)}) %collective-permute-start.3) | collective-permute-done | bytes 262176 | tf_op jit(solution)/shard_map/ppermute | solution.py:163
  47.4 0.7 %place.6.rest_1_ = bf16[256,4096]{1,0:T(8,128)(2,1)} custom-call(bf16[2,256,256]{2,1,0:T(8,128)(2,1)S(1)} %collective-permute-done.3.rest_0_, bf16[256,4096]{1,0:T(8,128)(2,1)} %place.5.rest_1_), custom_call_target="tpu_custom_call", output_to_operand_aliasing={{}: (1, {})} | custom-call | tf_op jit(solution)/shard_map/place/pallas_call | solution.py:142
  48.1 3.7 %collective-permute-done.1.rest_0_ = bf16[2,256,256]{2,1,0:T(8,128)(2,1)S(1)} collective-permute-done((bf16[2,256,256]{2,1,0:T(8,128)(2,1)S(1)}, bf16[2,256,256]{2,1,0:T(8,128)(2,1)S(1)}, u32[]{:S(2)}, u32[]{:S(2)}) %collective-permute-start.1) | collective-permute-done | bytes 262176 | tf_op jit(solution)/shard_map/ppermute | solution.py:163
  51.8 0.7 %place.7 = bf16[256,4096]{1,0:T(8,128)(2,1)} custom-call(bf16[2,256,256]{2,1,0:T(8,128)(2,1)S(1)} %collective-permute-done.1.rest_0_, bf16[256,4096]{1,0:T(8,128)(2,1)} %place.6.rest_1_), custom_call_target="tpu_custom_call", output_to_operand_aliasing={{}: (1, {})} | custom-call | tf_op jit(solution)/shard_map/place/pallas_call | solution.py:142
Async XLA Ops:
  1.1 18.2 %collective-permute-start.4 = (bf16[2,256,512]{2,1,0:T(8,128)(2,1)S(1)}, bf16[2,256,512]{2,1,0:T(8,128)(2,1)S(1)}, u32[]{:S(2)}, u32[]{:S(2)}) collective-permute-start(bf16[2,256,512]{2,1,0:T(8,128)(2,1)S(1)} %load.3), channel_id=1, source_target_pairs={{0,256},{1,257},{2,258},{3,259},{4,260},{5,261},{6,262},{7,263},{8... | collective-permute-start | bytes 1572872 | tf_op jit(solution)/shard_map/ppermute | solution.py:158
  7.6 28.8 %collective-permute-start = (bf16[2,256,256]{2,1,0:T(8,128)(2,1)S(1)}, bf16[2,256,256]{2,1,0:T(8,128)(2,1)S(1)}, u32[]{:S(2)}, u32[]{:S(2)}) collective-permute-start(bf16[2,256,256]{2,1,0:T(8,128)(2,1)S(1)} %get-tuple-element.17), channel_id=1, source_target_pairs={{0,256},{1,257},{2,258},{3,259},{4,260},{5,261},{6,262},{7,263},{8... | collective-permute-start | bytes 786440 | tf_op jit(solution)/shard_map/ppermute | solution.py:158
  10.0 20.5 %collective-permute-start.2 = (bf16[2,256,256]{2,1,0:T(8,128)(2,1)S(1)}, bf16[2,256,256]{2,1,0:T(8,128)(2,1)S(1)}, u32[]{:S(2)}, u32[]{:S(2)}) collective-permute-start(bf16[2,256,256]{2,1,0:T(8,128)(2,1)S(1)} %get-tuple-element.20), channel_id=1, source_target_pairs={{0,256},{1,257},{2,258},{3,259},{4,260},{5,261},{6,262},{7,263},{8... | collective-permute-start | bytes 786440 | tf_op jit(solution)/shard_map/ppermute | solution.py:158
  20.8 21.0 %collective-permute-start.5 = (bf16[2,256,512]{2,1,0:T(8,128)(2,1)S(1)}, bf16[2,256,512]{2,1,0:T(8,128)(2,1)S(1)}, u32[]{:S(2)}, u32[]{:S(2)}) collective-permute-start(bf16[2,256,512]{2,1,0:T(8,128)(2,1)S(1)} %get-tuple-element.23), channel_id=1, source_target_pairs={{0,256},{1,257},{2,258},{3,259},{4,260},{5,261},{6,262},{7,263},{8... | collective-permute-start | bytes 1572872 | tf_op jit(solution)/shard_map/ppermute | solution.py:163
  31.4 16.0 %collective-permute-start.3 = (bf16[2,256,256]{2,1,0:T(8,128)(2,1)S(1)}, bf16[2,256,256]{2,1,0:T(8,128)(2,1)S(1)}, u32[]{:S(2)}, u32[]{:S(2)}) collective-permute-start(bf16[2,256,256]{2,1,0:T(8,128)(2,1)S(1)} %get-tuple-element.21), channel_id=1, source_target_pairs={{0,256},{1,257},{2,258},{3,259},{4,260},{5,261},{6,262},{7,263},{8... | collective-permute-start | bytes 786440 | tf_op jit(solution)/shard_map/ppermute | solution.py:163
  37.3 14.6 %collective-permute-start.1 = (bf16[2,256,256]{2,1,0:T(8,128)(2,1)S(1)}, bf16[2,256,256]{2,1,0:T(8,128)(2,1)S(1)}, u32[]{:S(2)}, u32[]{:S(2)}) collective-permute-start(bf16[2,256,256]{2,1,0:T(8,128)(2,1)S(1)} %get-tuple-element.18), channel_id=1, source_target_pairs={{0,256},{1,257},{2,258},{3,259},{4,260},{5,261},{6,262},{7,263},{8... | collective-permute-start | bytes 786440 | tf_op jit(solution)/shard_map/ppermute | solution.py:163

commit v5 on v3

v5 whole, which is shorter than its diff:
```python
import functools

import jax
import jax.numpy as jnp
from jax import lax
from jax.experimental import pallas as pl
from jax.experimental.pallas import tpu as pltpu
from jax.sharding import PartitionSpec as P

HEAD = 256
HEADS = 8
INNER = HEAD * HEADS
KEPT = INNER // 2
CHUNKS = (1, 1, 1, 1)
LOAD_GROUPS = 3
FACTOR = HEAD ** (-0.5)
PARAMS = pltpu.CompilerParams(vmem_limit_bytes=12 * 1024 * 1024)

VMEM = pl.BlockSpec(memory_space=pltpu.VMEM)
ANY = pl.BlockSpec(memory_space=pl.ANY)
HBM = pl.BlockSpec(memory_space=pltpu.HBM)


def dot(a, b, dims):
    return lax.dot_general(a, b, (dims, ((), ())), preferred_element_type=jnp.float32)


def softmax(scores, axis):
    exponent = jnp.exp(scores - jnp.max(scores, axis=axis, keepdims=True))
    return exponent / jnp.sum(exponent, axis=axis, keepdims=True)


def decoder_half(query, out_grad, key, value):
    weights = softmax(dot(query, key, ((1,), (1,))) * FACTOR, -1)
    grad_weights = dot(out_grad, value, ((1,), (1,)))
    weights_b = weights.astype(jnp.bfloat16)
    attended = dot(weights_b, value, ((1,), (0,)))
    row_delta = jnp.sum(out_grad.astype(jnp.float32) * attended, axis=-1, keepdims=True)
    grad_scores = (weights * (grad_weights - row_delta) * FACTOR).astype(jnp.bfloat16)
    query_grad = dot(grad_scores, key, ((1,), (0,)))
    return attended.astype(jnp.bfloat16), query_grad.astype(jnp.bfloat16), weights_b, grad_scores


def encoder_half(query, out_grad, key, value):
    weights = softmax(dot(key, query, ((1,), (1,))) * FACTOR, 0)
    grad_weights = dot(value, out_grad, ((1,), (1,)))
    weights_b = weights.astype(jnp.bfloat16)
    row_delta = jnp.sum(weights_b.astype(jnp.float32) * grad_weights, axis=0, keepdims=True)
    grad_scores = (weights * (grad_weights - row_delta) * FACTOR).astype(jnp.bfloat16)
    key_grad = dot(grad_scores, query, ((1,), (0,)))
    value_grad = dot(weights_b, out_grad, ((1,), (0,)))
    return key_grad.astype(jnp.bfloat16), value_grad.astype(jnp.bfloat16)


def head_work(query, out_grad, key, value):
    attended, query_grad, weights_b, grad_scores = decoder_half(query, out_grad, key, value)
    key_grad = dot(grad_scores, query, ((0,), (0,))).astype(jnp.bfloat16)
    value_grad = dot(weights_b, out_grad, ((0,), (0,))).astype(jnp.bfloat16)
    return attended, query_grad, key_grad, value_grad


def on_decoder():
    return lax.axis_index("group") == 1


def in_split_plan():
    return lax.rem(lax.axis_index("dp"), 2) == 0


def side(kept):
    role = lax.axis_index("group")
    return role if kept else 1 - role


def views(block, at, width):
    return [block.at[:, pl.ds(pl.multiple_of(i * INNER + at, HEAD), width)] for i in range(2)]


def run_copies(copies):
    for copy in copies:
        copy.start()
    for copy in copies:
        copy.wait()


def load_kernel(parts, groups, block, *rest):
    *chunks, whole, sems = rest

    def split():
        copies = []
        for i, ((kept, first), chunk) in enumerate(zip(parts, chunks)):
            for j, view in enumerate(views(block, side(kept) * KEPT + first, chunk.shape[-1])):
                copies.append(pltpu.make_async_copy(view, chunk.at[j], sems.at[i, j]))
        size = -(-len(copies) // groups)
        for i in range(0, len(copies), size):
            run_copies(copies[i : i + size])

    def all_of_it():
        run_copies([pltpu.make_async_copy(block, whole, sems.at[0, 0])])

    pl.when(in_split_plan())(split)
    pl.when(jnp.logical_not(in_split_plan()))(all_of_it)


def work_kernel(width, own, received, kept, back):
    def run(decoder):
        query_side, key_side = (own, received) if decoder else (received, own)
        front, rear = (kept, back) if decoder else (back, kept)
        for h in range(width // HEAD):
            cols = slice(h * HEAD, (h + 1) * HEAD)
            attended, query_grad, key_grad, value_grad = head_work(
                query_side[0, :, cols], query_side[1, :, cols], key_side[0, :, cols], key_side[1, :, cols]
            )
            front[0, :, cols] = attended
            front[1, :, cols] = query_grad
            rear[0, :, cols] = key_grad
            rear[1, :, cols] = value_grad

    split = in_split_plan()
    pl.when(jnp.logical_and(split, on_decoder()))(lambda: run(True))
    pl.when(jnp.logical_and(split, jnp.logical_not(on_decoder())))(lambda: run(False))


def whole_kernel(own, received, _, out, stage, sems):
    def run(decoder):
        query_side, key_side = (own, received) if decoder else (received, own)
        copies = []
        for h in range(HEADS):
            cols = [slice(i * INNER + h * HEAD, i * INNER + (h + 1) * HEAD) for i in range(2)]
            operands = [ref[:, c] for ref in (query_side, key_side) for c in cols]
            results = (decoder_half if decoder else encoder_half)(*operands)[:2]
            for i, result in enumerate(results):
                stage[h, i] = result
                copies.append(pltpu.make_async_copy(stage.at[h, i], out.at[:, cols[i]], sems.at[h, i]))
                copies[-1].start()
        for copy in copies:
            copy.wait()

    whole = jnp.logical_not(in_split_plan())
    pl.when(jnp.logical_and(whole, on_decoder()))(lambda: run(True))
    pl.when(jnp.logical_and(whole, jnp.logical_not(on_decoder())))(lambda: run(False))


def place_kernel(kept, firsts, aliased, *rest):
    *chunks, out, sems = rest
    if aliased:
        chunks = chunks[:-1]

    def run():
        copies = []
        for i, (first, chunk) in enumerate(zip(firsts, chunks)):
            for j, view in enumerate(views(out, side(kept) * KEPT + first, chunk.shape[-1])):
                copies.append(pltpu.make_async_copy(chunk.at[j], view, sems.at[i, j]))
        run_copies(copies)

    pl.when(in_split_plan())(run)


def cost(moved, flops=0, exps=0):
    return pl.CostEstimate(flops=flops, bytes_accessed=moved, transcendentals=exps)


def local(operands):
    rows, both = operands.shape[2:]
    count = lax.axis_size("dp")
    swaps = [(i, (i + count) % (2 * count)) for i in range(2 * count)]
    split_swaps = [p for p in swaps if p[0] % 2 == 0]
    whole_swaps = [p for p in swaps if p[0] % 2 == 1]
    widths = [n * HEAD for n in CHUNKS]
    firsts = [sum(widths[:i]) for i in range(len(widths))]
    n = len(widths)

    def load(block, parts):
        return pl.pallas_call(
            functools.partial(load_kernel, [(kept, firsts[i]) for kept, i in parts], LOAD_GROUPS),
            out_shape=[pltpu.VMEM((2, rows, widths[i]), jnp.bfloat16) for _, i in parts]
            + [pltpu.VMEM((rows, both), jnp.bfloat16)],
            in_specs=[HBM],
            out_specs=[VMEM] * (len(parts) + 1),
            scratch_shapes=[pltpu.SemaphoreType.DMA((len(parts), 2))],
            compiler_params=PARAMS,
            cost_estimate=cost(0),
            name="load",
        )(block)

    def work(width, own, received):
        return pl.pallas_call(
            functools.partial(work_kernel, width),
            out_shape=[jax.ShapeDtypeStruct((2, rows, width), jnp.bfloat16)] * 2,
            in_specs=[VMEM, VMEM],
            out_specs=[VMEM, VMEM],
            compiler_params=PARAMS,
            cost_estimate=cost(0, flops=12 * rows * rows * width, exps=rows * width),
            name="work",
        )(own, received)

    def place(kept, at, chunks, out=None):
        extra = [] if out is None else [out]
        return pl.pallas_call(
            functools.partial(place_kernel, kept, at, bool(extra)),
            out_shape=jax.ShapeDtypeStruct((rows, both), jnp.bfloat16),
            in_specs=[VMEM] * len(chunks) + [ANY] * len(extra),
            out_specs=ANY,
            scratch_shapes=[pltpu.SemaphoreType.DMA((len(chunks), 2))],
            input_output_aliases={len(chunks): 0} if extra else {},
            compiler_params=PARAMS,
            cost_estimate=cost(0),
            name="place",
        )(*chunks, *extra)

    def whole(own, received, out):
        return pl.pallas_call(
            whole_kernel,
            out_shape=jax.ShapeDtypeStruct((rows, both), jnp.bfloat16),
            in_specs=[VMEM, VMEM, ANY],
            out_specs=ANY,
            scratch_shapes=[
                pltpu.VMEM((HEADS, 2, rows, HEAD), jnp.bfloat16),
                pltpu.SemaphoreType.DMA((HEADS, 2)),
            ],
            input_output_aliases={2: 0},
            compiler_params=PARAMS,
            cost_estimate=cost(0),
            name="whole",
        )(own, received, out)

    whole_received = lax.ppermute(operands, ("group", "dp"), whole_swaps)
    block = pltpu.with_memory_space_constraint(operands.reshape(rows, both), pltpu.HBM)
    *chunks, own_block = load(block, [(True, i) for i in range(n)] + [(False, i) for i in range(n)])
    own, sent = chunks[:n], chunks[n:]
    received = [lax.ppermute(c, ("group", "dp"), split_swaps) for c in sent]
    done, returned = [], []
    for i in range(n):
        kept, back = work(widths[i], own[i], received[i])
        done.append(kept)
        returned.append(lax.ppermute(back, ("group", "dp"), split_swaps))
    out = place(True, firsts, done)
    for i in range(n):
        if i == n - 1:
            out = whole(own_block, whole_received.reshape(rows, both), out)
        out = place(False, [firsts[i]], [returned[i]], out)
    return out.reshape(operands.shape)


def solution(mesh):
    spec = P("group", "dp", None, None)
    return jax.shard_map(local, mesh=mesh, in_specs=(spec,), out_specs=spec, check_vma=False)
```

time: 53 us -> 52.1 us (0.983)
  waiting for transfers between devices: 12.3 us -> 7.71 us
  starting transfers between devices: 29.9 us -> 32.3 us
  Pallas kernels: 10.3 us -> 11.5 us
    ppermute x8 -> x9, waiting for transfers between devices: 12.3 us -> 7.71 us  [the longest x4 7.7 us: local(): returned.append(lax.ppermute(back, ('group', 'dp'), split_swaps))]
    ppermute x8 -> x9, starting transfers between devices: 29.9 us -> 32.3 us  [the longest x4 16.8 us: local(): returned.append(lax.ppermute(back, ('group', 'dp'), split_swaps))]
    pallas_call x2 -> x1, Pallas kernels: 2.71 us -> 3.68 us  [load(): pl.pallas_call(functools.partial(load_kernel, [(kept, firsts[i]) for kept...]
    pallas_call x4 -> x5, Pallas kernels: 3.63 us -> 3.89 us  [the longest x4 3.72 us: work(): pl.pallas_call(functools.partial(work_kernel, width), out_shape=[jax.Shap...]
  transfers between devices with their start and end apart: 8 -> 9, of which waited for: 3 -> 3; matrix products, arithmetic and copies ran while one was open for 0% -> 0% of each run, Pallas kernels for 16% -> 21%
where the time goes in v5:
time: 52.1 us; the launch traced here: 51.7 us
  starting transfers between devices  32.3 us (62%)
  Pallas kernels  11.5 us (22%)
  waiting for transfers between devices  7.71 us (15%)
    ppermute x4, starting transfers between devices, local(): returned.append(lax.ppermute(back, ('group', 'dp'), split_swaps))  16.8 us
    ppermute x4, starting transfers between devices, local(): received = [lax.ppermute(c, ('group', 'dp'), split_swaps) for c in sent]  14.7 us
    ppermute x4, waiting for transfers between devices, local(): returned.append(lax.ppermute(back, ('group', 'dp'), split_swaps))  7.7 us
    pallas_call x5, Pallas kernels, place(): pl.pallas_call(functools.partial(place_kernel, kept, at, bool(extra)), ou...  3.91 us
    pallas_call x4, Pallas kernels, work(): pl.pallas_call(functools.partial(work_kernel, width), out_shape=[jax.Shap...  3.72 us
    pallas_call x1, Pallas kernels, load(): pl.pallas_call(functools.partial(load_kernel, [(kept, firsts[i]) for kept...  3.68 us
  transfers between devices with their start and end apart: 9, of which 3 were waited for; matrix products, arithmetic and copies ran while one was open for 0% of the time, Pallas kernels for 21%

profile of v5, /device:TPU:56, one launch (start us, length us, event | category | flops | bytes accessed | tf_op | source)
XLA Modules:
  0.0 51.7 jit_solution(3012134423810698352)
XLA Ops:
  0.0 0.8 %collective-permute-start.2 = (bf16[1,1,256,4096]{3,2,1,0:T(8,128)(2,1)}, bf16[1,1,256,4096]{3,2,1,0:T(8,128)(2,1)S(1)}, u32[]{:S(2)}, u32[]{:S(2)}) collective-permute-start(bf16[1,1,256,4096]{3,2,1,0:T(8,128)(2,1)} %param.1), channel_id=1, source_target_pairs={{1,257},{3,259},{5,261},{7,263},{9,265},{11,267},{13,269},{15,271}... | collective-permute-start | bytes 6291464 | tf_op jit(solution)/shard_map/ppermute | solution.py:227
  0.8 3.7 %load.1 = (bf16[2,256,256]{2,1,0:T(8,128)(2,1)S(1)}, bf16[2,256,256]{2,1,0:T(8,128)(2,1)S(1)}, bf16[2,256,256]{2,1,0:T(8,128)(2,1)S(1)}, bf16[2,256,256]{2,1,0:T...) custom-call(bf16[256,4096]{1,0:T(8,128)(2,1)} %bitcast.4), custom_call_target="tpu_custom_call" | custom-call | tf_op jit(solution)/shard_map/load/pallas_call | solution.py:174
  4.5 4.9 %collective-permute-start.7 = (bf16[2,256,256]{2,1,0:T(8,128)(2,1)S(1)}, bf16[2,256,256]{2,1,0:T(8,128)(2,1)S(1)}, u32[]{:S(2)}, u32[]{:S(2)}) collective-permute-start(bf16[2,256,256]{2,1,0:T(8,128)(2,1)S(1)} %get-tuple-element.33), channel_id=1, source_target_pairs={{0,256},{2,258},{4,260},{6,262},{8,264},{10,266},{12,268},{14,270}... | collective-permute-start | bytes 786440 | tf_op jit(solution)/shard_map/ppermute | solution.py:231
  9.4 2.4 %collective-permute-start.5 = (bf16[2,256,256]{2,1,0:T(8,128)(2,1)S(1)}, bf16[2,256,256]{2,1,0:T(8,128)(2,1)S(1)}, u32[]{:S(2)}, u32[]{:S(2)}) collective-permute-start(bf16[2,256,256]{2,1,0:T(8,128)(2,1)S(1)} %get-tuple-element.30), channel_id=1, source_target_pairs={{0,256},{2,258},{4,260},{6,262},{8,264},{10,266},{12,268},{14,270}... | collective-permute-start | bytes 786440 | tf_op jit(solution)/shard_map/ppermute | solution.py:231
  11.8 4.9 %collective-permute-start.3 = (bf16[2,256,256]{2,1,0:T(8,128)(2,1)S(1)}, bf16[2,256,256]{2,1,0:T(8,128)(2,1)S(1)}, u32[]{:S(2)}, u32[]{:S(2)}) collective-permute-start(bf16[2,256,256]{2,1,0:T(8,128)(2,1)S(1)} %get-tuple-element.27), channel_id=1, source_target_pairs={{0,256},{2,258},{4,260},{6,262},{8,264},{10,266},{12,268},{14,270}... | collective-permute-start | bytes 786440 | tf_op jit(solution)/shard_map/ppermute | solution.py:231
  16.8 2.4 %collective-permute-start = (bf16[2,256,256]{2,1,0:T(8,128)(2,1)S(1)}, bf16[2,256,256]{2,1,0:T(8,128)(2,1)S(1)}, u32[]{:S(2)}, u32[]{:S(2)}) collective-permute-start(bf16[2,256,256]{2,1,0:T(8,128)(2,1)S(1)} %get-tuple-element.23), channel_id=1, source_target_pairs={{0,256},{2,258},{4,260},{6,262},{8,264},{10,266},{12,268},{14,270}... | collective-permute-start | bytes 786440 | tf_op jit(solution)/shard_map/ppermute | solution.py:231
  19.2 0.0 collective-permute-done.7.received
  19.2 0.9 %work.7 = (bf16[2,256,256]{2,1,0:T(8,128)(2,1)S(1)}, bf16[2,256,256]{2,1,0:T(8,128)(2,1)S(1)}) custom-call(bf16[2,256,256]{2,1,0:T(8,128)(2,1)S(1)} %get-tuple-element.32.own, bf16[2,256,256]{2,1,0:T(8,128)(2,1)S(1)} %collective-permute-done.7.received), custom_call_target="tpu_custom_call" | custom-call | flops 201326592 | tf_op jit(solution)/shard_map/work/pallas_call | solution.py:187
  20.2 4.9 %collective-permute-start.8 = (bf16[2,256,256]{2,1,0:T(8,128)(2,1)S(1)}, bf16[2,256,256]{2,1,0:T(8,128)(2,1)S(1)}, u32[]{:S(2)}, u32[]{:S(2)}) collective-permute-start(bf16[2,256,256]{2,1,0:T(8,128)(2,1)S(1)} %get-tuple-element.34), channel_id=1, source_target_pairs={{0,256},{2,258},{4,260},{6,262},{8,264},{10,266},{12,268},{14,270}... | collective-permute-start | bytes 786440 | tf_op jit(solution)/shard_map/ppermute | solution.py:236
  25.1 0.0 collective-permute-done.5.received
  25.1 0.9 %work.6 = (bf16[2,256,256]{2,1,0:T(8,128)(2,1)S(1)}, bf16[2,256,256]{2,1,0:T(8,128)(2,1)S(1)}) custom-call(bf16[2,256,256]{2,1,0:T(8,128)(2,1)S(1)} %get-tuple-element.29.own, bf16[2,256,256]{2,1,0:T(8,128)(2,1)S(1)} %collective-permute-done.5.received), custom_call_target="tpu_custom_call" | custom-call | flops 201326592 | tf_op jit(solution)/shard_map/work/pallas_call | solution.py:187
  26.0 2.6 %collective-permute-start.6 = (bf16[2,256,256]{2,1,0:T(8,128)(2,1)S(1)}, bf16[2,256,256]{2,1,0:T(8,128)(2,1)S(1)}, u32[]{:S(2)}, u32[]{:S(2)}) collective-permute-start(bf16[2,256,256]{2,1,0:T(8,128)(2,1)S(1)} %get-tuple-element.31), channel_id=1, source_target_pairs={{0,256},{2,258},{4,260},{6,262},{8,264},{10,266},{12,268},{14,270}... | collective-permute-start | bytes 786440 | tf_op jit(solution)/shard_map/ppermute | solution.py:236
  28.6 0.0 collective-permute-done.3.received
  28.6 0.9 %work.5 = (bf16[2,256,256]{2,1,0:T(8,128)(2,1)S(1)}, bf16[2,256,256]{2,1,0:T(8,128)(2,1)S(1)}) custom-call(bf16[2,256,256]{2,1,0:T(8,128)(2,1)S(1)} %get-tuple-element.26.own, bf16[2,256,256]{2,1,0:T(8,128)(2,1)S(1)} %collective-permute-done.3.received), custom_call_target="tpu_custom_call" | custom-call | flops 201326592 | tf_op jit(solution)/shard_map/work/pallas_call | solution.py:187
  29.6 4.8 %collective-permute-start.4 = (bf16[2,256,256]{2,1,0:T(8,128)(2,1)S(1)}, bf16[2,256,256]{2,1,0:T(8,128)(2,1)S(1)}, u32[]{:S(2)}, u32[]{:S(2)}) collective-permute-start(bf16[2,256,256]{2,1,0:T(8,128)(2,1)S(1)} %get-tuple-element.28), channel_id=1, source_target_pairs={{0,256},{2,258},{4,260},{6,262},{8,264},{10,266},{12,268},{14,270}... | collective-permute-start | bytes 786440 | tf_op jit(solution)/shard_map/ppermute | solution.py:236
  34.3 0.0 collective-permute-done.received
  34.4 0.9 %work.4 = (bf16[2,256,256]{2,1,0:T(8,128)(2,1)S(1)}, bf16[2,256,256]{2,1,0:T(8,128)(2,1)S(1)}) custom-call(bf16[2,256,256]{2,1,0:T(8,128)(2,1)S(1)} %get-tuple-element.22.own, bf16[2,256,256]{2,1,0:T(8,128)(2,1)S(1)} %collective-permute-done.received), custom_call_target="tpu_custom_call" | custom-call | flops 201326592 | tf_op jit(solution)/shard_map/work/pallas_call | solution.py:187
  35.3 4.5 %collective-permute-start.1 = (bf16[2,256,256]{2,1,0:T(8,128)(2,1)S(1)}, bf16[2,256,256]{2,1,0:T(8,128)(2,1)S(1)}, u32[]{:S(2)}, u32[]{:S(2)}) collective-permute-start(bf16[2,256,256]{2,1,0:T(8,128)(2,1)S(1)} %get-tuple-element.24), channel_id=1, source_target_pairs={{0,256},{2,258},{4,260},{6,262},{8,264},{10,266},{12,268},{14,270}... | collective-permute-start | bytes 786440 | tf_op jit(solution)/shard_map/ppermute | solution.py:236
  39.8 1.0 %place.5.rest_1_ = bf16[256,4096]{1,0:T(8,128)(2,1)} custom-call(bf16[2,256,256]{2,1,0:T(8,128)(2,1)S(1)} %get-tuple-element.35.rest_0_, bf16[2,256,256]{2,1,0:T(8,128)(2,1)S(1)} %get-tuple-element.36.rest_1_, bf16[2,256,256]{2,1,0:T(8,128)(2,1)S(1)} %get-tuple-element.37.rest_2_, bf16[2,256,256]{2,1,0:T(8,128)(2,1)S(1)} %get-tuple-element.38.rest_3_), custom_call_target="tpu_custom_call" | custom-call | tf_op jit(solution)/shard_map/place/pallas_call | solution.py:199
  40.9 0.0 collective-permute-done.8.rest_0_
  40.9 0.7 %place.6.rest_1_ = bf16[256,4096]{1,0:T(8,128)(2,1)} custom-call(bf16[2,256,256]{2,1,0:T(8,128)(2,1)S(1)} %collective-permute-done.8.rest_0_, bf16[256,4096]{1,0:T(8,128)(2,1)} %place.5.rest_1_), custom_call_target="tpu_custom_call", output_to_operand_aliasing={{}: (1, {})} | custom-call | tf_op jit(solution)/shard_map/place/pallas_call | solution.py:199
  41.6 3.6 %collective-permute-done.6.rest_0_ = bf16[2,256,256]{2,1,0:T(8,128)(2,1)S(1)} collective-permute-done((bf16[2,256,256]{2,1,0:T(8,128)(2,1)S(1)}, bf16[2,256,256]{2,1,0:T(8,128)(2,1)S(1)}, u32[]{:S(2)}, u32[]{:S(2)}) %collective-permute-start.6) | collective-permute-done | bytes 262176 | tf_op jit(solution)/shard_map/ppermute | solution.py:236
  45.2 0.7 %place.7.rest_1_ = bf16[256,4096]{1,0:T(8,128)(2,1)} custom-call(bf16[2,256,256]{2,1,0:T(8,128)(2,1)S(1)} %collective-permute-done.6.rest_0_, bf16[256,4096]{1,0:T(8,128)(2,1)} %place.6.rest_1_), custom_call_target="tpu_custom_call", output_to_operand_aliasing={{}: (1, {})} | custom-call | tf_op jit(solution)/shard_map/place/pallas_call | solution.py:199
  45.9 2.2 %collective-permute-done.4.rest_0_ = bf16[2,256,256]{2,1,0:T(8,128)(2,1)S(1)} collective-permute-done((bf16[2,256,256]{2,1,0:T(8,128)(2,1)S(1)}, bf16[2,256,256]{2,1,0:T(8,128)(2,1)S(1)}, u32[]{:S(2)}, u32[]{:S(2)}) %collective-permute-start.4) | collective-permute-done | bytes 262176 | tf_op jit(solution)/shard_map/ppermute | solution.py:236
  48.2 0.7 %place.8._ = bf16[256,4096]{1,0:T(8,128)(2,1)} custom-call(bf16[2,256,256]{2,1,0:T(8,128)(2,1)S(1)} %collective-permute-done.4.rest_0_, bf16[256,4096]{1,0:T(8,128)(2,1)} %place.7.rest_1_), custom_call_target="tpu_custom_call", output_to_operand_aliasing={{}: (1, {})} | custom-call | tf_op jit(solution)/shard_map/place/pallas_call | solution.py:199
  48.9 0.0 collective-permute-done.2
  48.9 0.2 whole.1.rest_1_
  49.1 1.9 %collective-permute-done.1.rest_0_ = bf16[2,256,256]{2,1,0:T(8,128)(2,1)S(1)} collective-permute-done((bf16[2,256,256]{2,1,0:T(8,128)(2,1)S(1)}, bf16[2,256,256]{2,1,0:T(8,128)(2,1)S(1)}, u32[]{:S(2)}, u32[]{:S(2)}) %collective-permute-start.1) | collective-permute-done | bytes 262176 | tf_op jit(solution)/shard_map/ppermute | solution.py:236
  51.0 0.7 %place.9 = bf16[256,4096]{1,0:T(8,128)(2,1)} custom-call(bf16[2,256,256]{2,1,0:T(8,128)(2,1)S(1)} %collective-permute-done.1.rest_0_, bf16[256,4096]{1,0:T(8,128)(2,1)} %whole.1.rest_1_), custom_call_target="tpu_custom_call", output_to_operand_aliasing={{}: (1, {})} | custom-call | tf_op jit(solution)/shard_map/place/pallas_call | solution.py:199
Async XLA Ops:
  0.0 48.9 %collective-permute-start.2 = (bf16[1,1,256,4096]{3,2,1,0:T(8,128)(2,1)}, bf16[1,1,256,4096]{3,2,1,0:T(8,128)(2,1)S(1)}, u32[]{:S(2)}, u32[]{:S(2)}) collective-permute-start(bf16[1,1,256,4096]{3,2,1,0:T(8,128)(2,1)} %param.1), channel_id=1, source_target_pairs={{1,257},{3,259},{5,261},{7,263},{9,265},{11,267},{13,269},{15,271}... | collective-permute-start | bytes 6291464 | tf_op jit(solution)/shard_map/ppermute | solution.py:227
  4.5 14.7 %collective-permute-start.7 = (bf16[2,256,256]{2,1,0:T(8,128)(2,1)S(1)}, bf16[2,256,256]{2,1,0:T(8,128)(2,1)S(1)}, u32[]{:S(2)}, u32[]{:S(2)}) collective-permute-start(bf16[2,256,256]{2,1,0:T(8,128)(2,1)S(1)} %get-tuple-element.33), channel_id=1, source_target_pairs={{0,256},{2,258},{4,260},{6,262},{8,264},{10,266},{12,268},{14,270}... | collective-permute-start | bytes 786440 | tf_op jit(solution)/shard_map/ppermute | solution.py:231
  9.4 15.7 %collective-permute-start.5 = (bf16[2,256,256]{2,1,0:T(8,128)(2,1)S(1)}, bf16[2,256,256]{2,1,0:T(8,128)(2,1)S(1)}, u32[]{:S(2)}, u32[]{:S(2)}) collective-permute-start(bf16[2,256,256]{2,1,0:T(8,128)(2,1)S(1)} %get-tuple-element.30), channel_id=1, source_target_pairs={{0,256},{2,258},{4,260},{6,262},{8,264},{10,266},{12,268},{14,270}... | collective-permute-start | bytes 786440 | tf_op jit(solution)/shard_map/ppermute | solution.py:231
  11.8 16.8 %collective-permute-start.3 = (bf16[2,256,256]{2,1,0:T(8,128)(2,1)S(1)}, bf16[2,256,256]{2,1,0:T(8,128)(2,1)S(1)}, u32[]{:S(2)}, u32[]{:S(2)}) collective-permute-start(bf16[2,256,256]{2,1,0:T(8,128)(2,1)S(1)} %get-tuple-element.27), channel_id=1, source_target_pairs={{0,256},{2,258},{4,260},{6,262},{8,264},{10,266},{12,268},{14,270}... | collective-permute-start | bytes 786440 | tf_op jit(solution)/shard_map/ppermute | solution.py:231
  16.8 17.6 %collective-permute-start = (bf16[2,256,256]{2,1,0:T(8,128)(2,1)S(1)}, bf16[2,256,256]{2,1,0:T(8,128)(2,1)S(1)}, u32[]{:S(2)}, u32[]{:S(2)}) collective-permute-start(bf16[2,256,256]{2,1,0:T(8,128)(2,1)S(1)} %get-tuple-element.23), channel_id=1, source_target_pairs={{0,256},{2,258},{4,260},{6,262},{8,264},{10,266},{12,268},{14,270}... | collective-permute-start | bytes 786440 | tf_op jit(solution)/shard_map/ppermute | solution.py:231
  20.2 20.7 %collective-permute-start.8 = (bf16[2,256,256]{2,1,0:T(8,128)(2,1)S(1)}, bf16[2,256,256]{2,1,0:T(8,128)(2,1)S(1)}, u32[]{:S(2)}, u32[]{:S(2)}) collective-permute-start(bf16[2,256,256]{2,1,0:T(8,128)(2,1)S(1)} %get-tuple-element.34), channel_id=1, source_target_pairs={{0,256},{2,258},{4,260},{6,262},{8,264},{10,266},{12,268},{14,270}... | collective-permute-start | bytes 786440 | tf_op jit(solution)/shard_map/ppermute | solution.py:236
  26.0 19.2 %collective-permute-start.6 = (bf16[2,256,256]{2,1,0:T(8,128)(2,1)S(1)}, bf16[2,256,256]{2,1,0:T(8,128)(2,1)S(1)}, u32[]{:S(2)}, u32[]{:S(2)}) collective-permute-start(bf16[2,256,256]{2,1,0:T(8,128)(2,1)S(1)} %get-tuple-element.31), channel_id=1, source_target_pairs={{0,256},{2,258},{4,260},{6,262},{8,264},{10,266},{12,268},{14,270}... | collective-permute-start | bytes 786440 | tf_op jit(solution)/shard_map/ppermute | solution.py:236
  29.6 18.6 %collective-permute-start.4 = (bf16[2,256,256]{2,1,0:T(8,128)(2,1)S(1)}, bf16[2,256,256]{2,1,0:T(8,128)(2,1)S(1)}, u32[]{:S(2)}, u32[]{:S(2)}) collective-permute-start(bf16[2,256,256]{2,1,0:T(8,128)(2,1)S(1)} %get-tuple-element.28), channel_id=1, source_target_pairs={{0,256},{2,258},{4,260},{6,262},{8,264},{10,266},{12,268},{14,270}... | collective-permute-start | bytes 786440 | tf_op jit(solution)/shard_map/ppermute | solution.py:236
  35.3 15.7 %collective-permute-start.1 = (bf16[2,256,256]{2,1,0:T(8,128)(2,1)S(1)}, bf16[2,256,256]{2,1,0:T(8,128)(2,1)S(1)}, u32[]{:S(2)}, u32[]{:S(2)}) collective-permute-start(bf16[2,256,256]{2,1,0:T(8,128)(2,1)S(1)} %get-tuple-element.24), channel_id=1, source_target_pairs={{0,256},{2,258},{4,260},{6,262},{8,264},{10,266},{12,268},{14,270}... | collective-permute-start | bytes 786440 | tf_op jit(solution)/shard_map/ppermute | solution.py:236

commit v6 on v5

--- a/solution.py
+++ b/solution.py
@@ -12,7 +12,7 @@
 INNER = HEAD * HEADS
 KEPT = INNER // 2
 CHUNKS = (1, 1, 1, 1)
-LOAD_GROUPS = 3
+TOGETHER = 4
 FACTOR = HEAD ** (-0.5)
 PARAMS = pltpu.CompilerParams(vmem_limit_bytes=12 * 1024 * 1024)
 
@@ -31,32 +31,55 @@
 
 
 def decoder_half(query, out_grad, key, value):
-    weights = softmax(dot(query, key, ((1,), (1,))) * FACTOR, -1)
+    scores = dot(query, key, ((1,), (1,))) * FACTOR
     grad_weights = dot(out_grad, value, ((1,), (1,)))
+    yield
+    weights = softmax(scores, -1)
     weights_b = weights.astype(jnp.bfloat16)
+    yield
     attended = dot(weights_b, value, ((1,), (0,)))
+    yield
     row_delta = jnp.sum(out_grad.astype(jnp.float32) * attended, axis=-1, keepdims=True)
     grad_scores = (weights * (grad_weights - row_delta) * FACTOR).astype(jnp.bfloat16)
+    yield
     query_grad = dot(grad_scores, key, ((1,), (0,)))
     return attended.astype(jnp.bfloat16), query_grad.astype(jnp.bfloat16), weights_b, grad_scores
 
 
 def encoder_half(query, out_grad, key, value):
-    weights = softmax(dot(key, query, ((1,), (1,))) * FACTOR, 0)
+    scores = dot(key, query, ((1,), (1,))) * FACTOR
     grad_weights = dot(value, out_grad, ((1,), (1,)))
+    yield
+    weights = softmax(scores, 0)
     weights_b = weights.astype(jnp.bfloat16)
+    yield
+    value_grad = dot(weights_b, out_grad, ((1,), (0,)))
     row_delta = jnp.sum(weights_b.astype(jnp.float32) * grad_weights, axis=0, keepdims=True)
     grad_scores = (weights * (grad_weights - row_delta) * FACTOR).astype(jnp.bfloat16)
+    yield
     key_grad = dot(grad_scores, query, ((1,), (0,)))
-    value_grad = dot(weights_b, out_grad, ((1,), (0,)))
     return key_grad.astype(jnp.bfloat16), value_grad.astype(jnp.bfloat16)
 
 
 def head_work(query, out_grad, key, value):
-    attended, query_grad, weights_b, grad_scores = decoder_half(query, out_grad, key, value)
+    attended, query_grad, weights_b, grad_scores = yield from decoder_half(query, out_grad, key, value)
+    yield
     key_grad = dot(grad_scores, query, ((0,), (0,))).astype(jnp.bfloat16)
     value_grad = dot(weights_b, out_grad, ((0,), (0,))).astype(jnp.bfloat16)
     return attended, query_grad, key_grad, value_grad
+
+
+def side_by_side(heads):
+    results = [None] * len(heads)
+    left = list(range(len(heads)))
+    while left:
+        for i in list(left):
+            try:
+                next(heads[i])
+            except StopIteration as end:
+                results[i] = end.value
+                left.remove(i)
+    return results
 
 
 def on_decoder():
@@ -83,7 +106,7 @@
         copy.wait()
 
 
-def load_kernel(parts, groups, block, *rest):
+def load_kernel(parts, block, *rest):
     *chunks, whole, sems = rest
 
     def split():
@@ -91,9 +114,7 @@
         for i, ((kept, first), chunk) in enumerate(zip(parts, chunks)):
             for j, view in enumerate(views(block, side(kept) * KEPT + first, chunk.shape[-1])):
                 copies.append(pltpu.make_async_copy(view, chunk.at[j], sems.at[i, j]))
-        size = -(-len(copies) // groups)
-        for i in range(0, len(copies), size):
-            run_copies(copies[i : i + size])
+        run_copies(copies)
 
     def all_of_it():
         run_copies([pltpu.make_async_copy(block, whole, sems.at[0, 0])])
@@ -106,15 +127,15 @@
     def run(decoder):
         query_side, key_side = (own, received) if decoder else (received, own)
         front, rear = (kept, back) if decoder else (back, kept)
-        for h in range(width // HEAD):
-            cols = slice(h * HEAD, (h + 1) * HEAD)
-            attended, query_grad, key_grad, value_grad = head_work(
-                query_side[0, :, cols], query_side[1, :, cols], key_side[0, :, cols], key_side[1, :, cols]
-            )
-            front[0, :, cols] = attended
-            front[1, :, cols] = query_grad
-            rear[0, :, cols] = key_grad
-            rear[1, :, cols] = value_grad
+        cols = [slice(h * HEAD, (h + 1) * HEAD) for h in range(width // HEAD)]
+        heads = [
+            head_work(query_side[0, :, c], query_side[1, :, c], key_side[0, :, c], key_side[1, :, c]) for c in cols
+        ]
+        for c, (attended, query_grad, key_grad, value_grad) in zip(cols, side_by_side(heads)):
+            front[0, :, c] = attended
+            front[1, :, c] = query_grad
+            rear[0, :, c] = key_grad
+            rear[1, :, c] = value_grad
 
     split = in_split_plan()
     pl.when(jnp.logical_and(split, on_decoder()))(lambda: run(True))
@@ -125,14 +146,16 @@
     def run(decoder):
         query_side, key_side = (own, received) if decoder else (received, own)
         copies = []
-        for h in range(HEADS):
-            cols = [slice(i * INNER + h * HEAD, i * INNER + (h + 1) * HEAD) for i in range(2)]
-            operands = [ref[:, c] for ref in (query_side, key_side) for c in cols]
-            results = (decoder_half if decoder else encoder_half)(*operands)[:2]
-            for i, result in enumerate(results):
-                stage[h, i] = result
-                copies.append(pltpu.make_async_copy(stage.at[h, i], out.at[:, cols[i]], sems.at[h, i]))
-                copies[-1].start()
+        for start in range(0, HEADS, TOGETHER):
+            heads = range(start, start + TOGETHER)
+            cols = {h: [slice(i * INNER + h * HEAD, i * INNER + (h + 1) * HEAD) for i in range(2)] for h in heads}
+            work = decoder_half if decoder else encoder_half
+            results = side_by_side([work(*[ref[:, c] for ref in (query_side, key_side) for c in cols[h]]) for h in heads])
+            for h, result in zip(heads, results):
+                for i in range(2):
+                    stage[h, i] = result[i]
+                    copies.append(pltpu.make_async_copy(stage.at[h, i], out.at[:, cols[h][i]], sems.at[h, i]))
+                    copies[-1].start()
         for copy in copies:
             copy.wait()
 
@@ -172,7 +195,7 @@
 
     def load(block, parts):
         return pl.pallas_call(
-            functools.partial(load_kernel, [(kept, firsts[i]) for kept, i in parts], LOAD_GROUPS),
+            functools.partial(load_kernel, [(kept, firsts[i]) for kept, i in parts]),
             out_shape=[pltpu.VMEM((2, rows, widths[i]), jnp.bfloat16) for _, i in parts]
             + [pltpu.VMEM((rows, both), jnp.bfloat16)],
             in_specs=[HBM],

time: 52.1 us -> 52 us (level)
  Pallas kernels: 11.5 us -> 9.58 us
  waiting for transfers between devices: 7.71 us -> 9.61 us
    ppermute x4, waiting for transfers between devices: 7.7 us -> 9.6 us  [local(): returned.append(lax.ppermute(back, ('group', 'dp'), split_swaps))]
    pallas_call x1, Pallas kernels: 3.68 us -> 1.79 us  [load(): pl.pallas_call(functools.partial(load_kernel, [(kept, firsts[i]) for kept...]
  transfers between devices with their start and end apart: 9 -> 9, of which waited for: 3 -> 3; matrix products, arithmetic and copies ran while one was open for 0% -> 0% of each run, Pallas kernels for 21% -> 17%
where the time goes in v6:
time: 52 us; the launch traced here: 51.7 us
  starting transfers between devices  32.3 us (62%)
  waiting for transfers between devices  9.61 us (18%)
  Pallas kernels  9.58 us (18%)
    ppermute x4, starting transfers between devices, local(): returned.append(lax.ppermute(back, ('group', 'dp'), split_swaps))  16.8 us
    ppermute x4, starting transfers between devices, local(): received = [lax.ppermute(c, ('group', 'dp'), split_swaps) for c in sent]  14.7 us
    ppermute x4, waiting for transfers between devices, local(): returned.append(lax.ppermute(back, ('group', 'dp'), split_swaps))  9.6 us
    pallas_call x5, Pallas kernels, place(): pl.pallas_call(functools.partial(place_kernel, kept, at, bool(extra)), ou...  3.91 us
    pallas_call x4, Pallas kernels, work(): pl.pallas_call(functools.partial(work_kernel, width), out_shape=[jax.Shap...  3.71 us
    pallas_call x1, Pallas kernels, load(): pl.pallas_call(functools.partial(load_kernel, [(kept, firsts[i]) for kept...  1.79 us
  transfers between devices with their start and end apart: 9, of which 3 were waited for; matrix products, arithmetic and copies ran while one was open for 0% of the time, Pallas kernels for 17%

profile of v6, /device:TPU:56, one launch (start us, length us, event | category | flops | bytes accessed | tf_op | source)
XLA Modules:
  0.0 51.7 jit_solution(11662008723156532490)
XLA Ops:
  0.0 0.8 %collective-permute-start.2 = (bf16[1,1,256,4096]{3,2,1,0:T(8,128)(2,1)}, bf16[1,1,256,4096]{3,2,1,0:T(8,128)(2,1)S(1)}, u32[]{:S(2)}, u32[]{:S(2)}) collective-permute-start(bf16[1,1,256,4096]{3,2,1,0:T(8,128)(2,1)} %param.1), channel_id=1, source_target_pairs={{1,257},{3,259},{5,261},{7,263},{9,265},{11,267},{13,269},{15,271}... | collective-permute-start | bytes 6291464 | tf_op jit(solution)/shard_map/ppermute | solution.py:250
  0.8 1.8 %load.1 = (bf16[2,256,256]{2,1,0:T(8,128)(2,1)S(1)}, bf16[2,256,256]{2,1,0:T(8,128)(2,1)S(1)}, bf16[2,256,256]{2,1,0:T(8,128)(2,1)S(1)}, bf16[2,256,256]{2,1,0:T...) custom-call(bf16[256,4096]{1,0:T(8,128)(2,1)} %bitcast.4), custom_call_target="tpu_custom_call" | custom-call | tf_op jit(solution)/shard_map/load/pallas_call | solution.py:197
  2.6 4.9 %collective-permute-start.7 = (bf16[2,256,256]{2,1,0:T(8,128)(2,1)S(1)}, bf16[2,256,256]{2,1,0:T(8,128)(2,1)S(1)}, u32[]{:S(2)}, u32[]{:S(2)}) collective-permute-start(bf16[2,256,256]{2,1,0:T(8,128)(2,1)S(1)} %get-tuple-element.33), channel_id=1, source_target_pairs={{0,256},{2,258},{4,260},{6,262},{8,264},{10,266},{12,268},{14,270}... | collective-permute-start | bytes 786440 | tf_op jit(solution)/shard_map/ppermute | solution.py:254
  7.5 2.4 %collective-permute-start.5 = (bf16[2,256,256]{2,1,0:T(8,128)(2,1)S(1)}, bf16[2,256,256]{2,1,0:T(8,128)(2,1)S(1)}, u32[]{:S(2)}, u32[]{:S(2)}) collective-permute-start(bf16[2,256,256]{2,1,0:T(8,128)(2,1)S(1)} %get-tuple-element.30), channel_id=1, source_target_pairs={{0,256},{2,258},{4,260},{6,262},{8,264},{10,266},{12,268},{14,270}... | collective-permute-start | bytes 786440 | tf_op jit(solution)/shard_map/ppermute | solution.py:254
  10.0 4.9 %collective-permute-start.3 = (bf16[2,256,256]{2,1,0:T(8,128)(2,1)S(1)}, bf16[2,256,256]{2,1,0:T(8,128)(2,1)S(1)}, u32[]{:S(2)}, u32[]{:S(2)}) collective-permute-start(bf16[2,256,256]{2,1,0:T(8,128)(2,1)S(1)} %get-tuple-element.27), channel_id=1, source_target_pairs={{0,256},{2,258},{4,260},{6,262},{8,264},{10,266},{12,268},{14,270}... | collective-permute-start | bytes 786440 | tf_op jit(solution)/shard_map/ppermute | solution.py:254
  14.9 2.4 %collective-permute-start = (bf16[2,256,256]{2,1,0:T(8,128)(2,1)S(1)}, bf16[2,256,256]{2,1,0:T(8,128)(2,1)S(1)}, u32[]{:S(2)}, u32[]{:S(2)}) collective-permute-start(bf16[2,256,256]{2,1,0:T(8,128)(2,1)S(1)} %get-tuple-element.23), channel_id=1, source_target_pairs={{0,256},{2,258},{4,260},{6,262},{8,264},{10,266},{12,268},{14,270}... | collective-permute-start | bytes 786440 | tf_op jit(solution)/shard_map/ppermute | solution.py:254
  17.3 0.0 collective-permute-done.7.received
  17.3 0.9 %work.7 = (bf16[2,256,256]{2,1,0:T(8,128)(2,1)S(1)}, bf16[2,256,256]{2,1,0:T(8,128)(2,1)S(1)}) custom-call(bf16[2,256,256]{2,1,0:T(8,128)(2,1)S(1)} %get-tuple-element.32.own, bf16[2,256,256]{2,1,0:T(8,128)(2,1)S(1)} %collective-permute-done.7.received), custom_call_target="tpu_custom_call" | custom-call | flops 201326592 | tf_op jit(solution)/shard_map/work/pallas_call | solution.py:210
  18.3 4.9 %collective-permute-start.8 = (bf16[2,256,256]{2,1,0:T(8,128)(2,1)S(1)}, bf16[2,256,256]{2,1,0:T(8,128)(2,1)S(1)}, u32[]{:S(2)}, u32[]{:S(2)}) collective-permute-start(bf16[2,256,256]{2,1,0:T(8,128)(2,1)S(1)} %get-tuple-element.34), channel_id=1, source_target_pairs={{0,256},{2,258},{4,260},{6,262},{8,264},{10,266},{12,268},{14,270}... | collective-permute-start | bytes 786440 | tf_op jit(solution)/shard_map/ppermute | solution.py:259
  23.2 0.0 collective-permute-done.5.received
  23.2 0.9 %work.6 = (bf16[2,256,256]{2,1,0:T(8,128)(2,1)S(1)}, bf16[2,256,256]{2,1,0:T(8,128)(2,1)S(1)}) custom-call(bf16[2,256,256]{2,1,0:T(8,128)(2,1)S(1)} %get-tuple-element.29.own, bf16[2,256,256]{2,1,0:T(8,128)(2,1)S(1)} %collective-permute-done.5.received), custom_call_target="tpu_custom_call" | custom-call | flops 201326592 | tf_op jit(solution)/shard_map/work/pallas_call | solution.py:210
  24.1 2.6 %collective-permute-start.6 = (bf16[2,256,256]{2,1,0:T(8,128)(2,1)S(1)}, bf16[2,256,256]{2,1,0:T(8,128)(2,1)S(1)}, u32[]{:S(2)}, u32[]{:S(2)}) collective-permute-start(bf16[2,256,256]{2,1,0:T(8,128)(2,1)S(1)} %get-tuple-element.31), channel_id=1, source_target_pairs={{0,256},{2,258},{4,260},{6,262},{8,264},{10,266},{12,268},{14,270}... | collective-permute-start | bytes 786440 | tf_op jit(solution)/shard_map/ppermute | solution.py:259
  26.7 0.0 collective-permute-done.3.received
  26.7 0.9 %work.5 = (bf16[2,256,256]{2,1,0:T(8,128)(2,1)S(1)}, bf16[2,256,256]{2,1,0:T(8,128)(2,1)S(1)}) custom-call(bf16[2,256,256]{2,1,0:T(8,128)(2,1)S(1)} %get-tuple-element.26.own, bf16[2,256,256]{2,1,0:T(8,128)(2,1)S(1)} %collective-permute-done.3.received), custom_call_target="tpu_custom_call" | custom-call | flops 201326592 | tf_op jit(solution)/shard_map/work/pallas_call | solution.py:210
  27.7 4.8 %collective-permute-start.4 = (bf16[2,256,256]{2,1,0:T(8,128)(2,1)S(1)}, bf16[2,256,256]{2,1,0:T(8,128)(2,1)S(1)}, u32[]{:S(2)}, u32[]{:S(2)}) collective-permute-start(bf16[2,256,256]{2,1,0:T(8,128)(2,1)S(1)} %get-tuple-element.28), channel_id=1, source_target_pairs={{0,256},{2,258},{4,260},{6,262},{8,264},{10,266},{12,268},{14,270}... | collective-permute-start | bytes 786440 | tf_op jit(solution)/shard_map/ppermute | solution.py:259
  32.5 0.0 collective-permute-done.received
  32.5 0.9 %work.4 = (bf16[2,256,256]{2,1,0:T(8,128)(2,1)S(1)}, bf16[2,256,256]{2,1,0:T(8,128)(2,1)S(1)}) custom-call(bf16[2,256,256]{2,1,0:T(8,128)(2,1)S(1)} %get-tuple-element.22.own, bf16[2,256,256]{2,1,0:T(8,128)(2,1)S(1)} %collective-permute-done.received), custom_call_target="tpu_custom_call" | custom-call | flops 201326592 | tf_op jit(solution)/shard_map/work/pallas_call | solution.py:210
  33.4 4.5 %collective-permute-start.1 = (bf16[2,256,256]{2,1,0:T(8,128)(2,1)S(1)}, bf16[2,256,256]{2,1,0:T(8,128)(2,1)S(1)}, u32[]{:S(2)}, u32[]{:S(2)}) collective-permute-start(bf16[2,256,256]{2,1,0:T(8,128)(2,1)S(1)} %get-tuple-element.24), channel_id=1, source_target_pairs={{0,256},{2,258},{4,260},{6,262},{8,264},{10,266},{12,268},{14,270}... | collective-permute-start | bytes 786440 | tf_op jit(solution)/shard_map/ppermute | solution.py:259
  37.9 1.0 %place.5.rest_1_ = bf16[256,4096]{1,0:T(8,128)(2,1)} custom-call(bf16[2,256,256]{2,1,0:T(8,128)(2,1)S(1)} %get-tuple-element.35.rest_0_, bf16[2,256,256]{2,1,0:T(8,128)(2,1)S(1)} %get-tuple-element.36.rest_1_, bf16[2,256,256]{2,1,0:T(8,128)(2,1)S(1)} %get-tuple-element.37.rest_2_, bf16[2,256,256]{2,1,0:T(8,128)(2,1)S(1)} %get-tuple-element.38.rest_3_), custom_call_target="tpu_custom_call" | custom-call | tf_op jit(solution)/shard_map/place/pallas_call | solution.py:222
  39.0 0.0 collective-permute-done.8.rest_0_
  39.0 0.7 %place.6.rest_1_ = bf16[256,4096]{1,0:T(8,128)(2,1)} custom-call(bf16[2,256,256]{2,1,0:T(8,128)(2,1)S(1)} %collective-permute-done.8.rest_0_, bf16[256,4096]{1,0:T(8,128)(2,1)} %place.5.rest_1_), custom_call_target="tpu_custom_call", output_to_operand_aliasing={{}: (1, {})} | custom-call | tf_op jit(solution)/shard_map/place/pallas_call | solution.py:222
  39.7 3.6 %collective-permute-done.6.rest_0_ = bf16[2,256,256]{2,1,0:T(8,128)(2,1)S(1)} collective-permute-done((bf16[2,256,256]{2,1,0:T(8,128)(2,1)S(1)}, bf16[2,256,256]{2,1,0:T(8,128)(2,1)S(1)}, u32[]{:S(2)}, u32[]{:S(2)}) %collective-permute-start.6) | collective-permute-done | bytes 262176 | tf_op jit(solution)/shard_map/ppermute | solution.py:259
  43.3 0.7 %place.7.rest_1_ = bf16[256,4096]{1,0:T(8,128)(2,1)} custom-call(bf16[2,256,256]{2,1,0:T(8,128)(2,1)S(1)} %collective-permute-done.6.rest_0_, bf16[256,4096]{1,0:T(8,128)(2,1)} %place.6.rest_1_), custom_call_target="tpu_custom_call", output_to_operand_aliasing={{}: (1, {})} | custom-call | tf_op jit(solution)/shard_map/place/pallas_call | solution.py:222
  44.0 4.1 %collective-permute-done.4.rest_0_ = bf16[2,256,256]{2,1,0:T(8,128)(2,1)S(1)} collective-permute-done((bf16[2,256,256]{2,1,0:T(8,128)(2,1)S(1)}, bf16[2,256,256]{2,1,0:T(8,128)(2,1)S(1)}, u32[]{:S(2)}, u32[]{:S(2)}) %collective-permute-start.4) | collective-permute-done | bytes 262176 | tf_op jit(solution)/shard_map/ppermute | solution.py:259
  48.2 0.7 %place.8._ = bf16[256,4096]{1,0:T(8,128)(2,1)} custom-call(bf16[2,256,256]{2,1,0:T(8,128)(2,1)S(1)} %collective-permute-done.4.rest_0_, bf16[256,4096]{1,0:T(8,128)(2,1)} %place.7.rest_1_), custom_call_target="tpu_custom_call", output_to_operand_aliasing={{}: (1, {})} | custom-call | tf_op jit(solution)/shard_map/place/pallas_call | solution.py:222
  48.9 0.0 collective-permute-done.2
  48.9 0.2 whole.1.rest_1_
  49.1 1.9 %collective-permute-done.1.rest_0_ = bf16[2,256,256]{2,1,0:T(8,128)(2,1)S(1)} collective-permute-done((bf16[2,256,256]{2,1,0:T(8,128)(2,1)S(1)}, bf16[2,256,256]{2,1,0:T(8,128)(2,1)S(1)}, u32[]{:S(2)}, u32[]{:S(2)}) %collective-permute-start.1) | collective-permute-done | bytes 262176 | tf_op jit(solution)/shard_map/ppermute | solution.py:259
  51.0 0.7 %place.9 = bf16[256,4096]{1,0:T(8,128)(2,1)} custom-call(bf16[2,256,256]{2,1,0:T(8,128)(2,1)S(1)} %collective-permute-done.1.rest_0_, bf16[256,4096]{1,0:T(8,128)(2,1)} %whole.1.rest_1_), custom_call_target="tpu_custom_call", output_to_operand_aliasing={{}: (1, {})} | custom-call | tf_op jit(solution)/shard_map/place/pallas_call | solution.py:222
Async XLA Ops:
  0.0 48.9 %collective-permute-start.2 = (bf16[1,1,256,4096]{3,2,1,0:T(8,128)(2,1)}, bf16[1,1,256,4096]{3,2,1,0:T(8,128)(2,1)S(1)}, u32[]{:S(2)}, u32[]{:S(2)}) collective-permute-start(bf16[1,1,256,4096]{3,2,1,0:T(8,128)(2,1)} %param.1), channel_id=1, source_target_pairs={{1,257},{3,259},{5,261},{7,263},{9,265},{11,267},{13,269},{15,271}... | collective-permute-start | bytes 6291464 | tf_op jit(solution)/shard_map/ppermute | solution.py:250
  2.6 14.7 %collective-permute-start.7 = (bf16[2,256,256]{2,1,0:T(8,128)(2,1)S(1)}, bf16[2,256,256]{2,1,0:T(8,128)(2,1)S(1)}, u32[]{:S(2)}, u32[]{:S(2)}) collective-permute-start(bf16[2,256,256]{2,1,0:T(8,128)(2,1)S(1)} %get-tuple-element.33), channel_id=1, source_target_pairs={{0,256},{2,258},{4,260},{6,262},{8,264},{10,266},{12,268},{14,270}... | collective-permute-start | bytes 786440 | tf_op jit(solution)/shard_map/ppermute | solution.py:254
  7.5 15.7 %collective-permute-start.5 = (bf16[2,256,256]{2,1,0:T(8,128)(2,1)S(1)}, bf16[2,256,256]{2,1,0:T(8,128)(2,1)S(1)}, u32[]{:S(2)}, u32[]{:S(2)}) collective-permute-start(bf16[2,256,256]{2,1,0:T(8,128)(2,1)S(1)} %get-tuple-element.30), channel_id=1, source_target_pairs={{0,256},{2,258},{4,260},{6,262},{8,264},{10,266},{12,268},{14,270}... | collective-permute-start | bytes 786440 | tf_op jit(solution)/shard_map/ppermute | solution.py:254
  10.0 16.8 %collective-permute-start.3 = (bf16[2,256,256]{2,1,0:T(8,128)(2,1)S(1)}, bf16[2,256,256]{2,1,0:T(8,128)(2,1)S(1)}, u32[]{:S(2)}, u32[]{:S(2)}) collective-permute-start(bf16[2,256,256]{2,1,0:T(8,128)(2,1)S(1)} %get-tuple-element.27), channel_id=1, source_target_pairs={{0,256},{2,258},{4,260},{6,262},{8,264},{10,266},{12,268},{14,270}... | collective-permute-start | bytes 786440 | tf_op jit(solution)/shard_map/ppermute | solution.py:254
  14.9 17.6 %collective-permute-start = (bf16[2,256,256]{2,1,0:T(8,128)(2,1)S(1)}, bf16[2,256,256]{2,1,0:T(8,128)(2,1)S(1)}, u32[]{:S(2)}, u32[]{:S(2)}) collective-permute-start(bf16[2,256,256]{2,1,0:T(8,128)(2,1)S(1)} %get-tuple-element.23), channel_id=1, source_target_pairs={{0,256},{2,258},{4,260},{6,262},{8,264},{10,266},{12,268},{14,270}... | collective-permute-start | bytes 786440 | tf_op jit(solution)/shard_map/ppermute | solution.py:254
  18.3 20.7 %collective-permute-start.8 = (bf16[2,256,256]{2,1,0:T(8,128)(2,1)S(1)}, bf16[2,256,256]{2,1,0:T(8,128)(2,1)S(1)}, u32[]{:S(2)}, u32[]{:S(2)}) collective-permute-start(bf16[2,256,256]{2,1,0:T(8,128)(2,1)S(1)} %get-tuple-element.34), channel_id=1, source_target_pairs={{0,256},{2,258},{4,260},{6,262},{8,264},{10,266},{12,268},{14,270}... | collective-permute-start | bytes 786440 | tf_op jit(solution)/shard_map/ppermute | solution.py:259
  24.1 19.2 %collective-permute-start.6 = (bf16[2,256,256]{2,1,0:T(8,128)(2,1)S(1)}, bf16[2,256,256]{2,1,0:T(8,128)(2,1)S(1)}, u32[]{:S(2)}, u32[]{:S(2)}) collective-permute-start(bf16[2,256,256]{2,1,0:T(8,128)(2,1)S(1)} %get-tuple-element.31), channel_id=1, source_target_pairs={{0,256},{2,258},{4,260},{6,262},{8,264},{10,266},{12,268},{14,270}... | collective-permute-start | bytes 786440 | tf_op jit(solution)/shard_map/ppermute | solution.py:259
  27.7 20.5 %collective-permute-start.4 = (bf16[2,256,256]{2,1,0:T(8,128)(2,1)S(1)}, bf16[2,256,256]{2,1,0:T(8,128)(2,1)S(1)}, u32[]{:S(2)}, u32[]{:S(2)}) collective-permute-start(bf16[2,256,256]{2,1,0:T(8,128)(2,1)S(1)} %get-tuple-element.28), channel_id=1, source_target_pairs={{0,256},{2,258},{4,260},{6,262},{8,264},{10,266},{12,268},{14,270}... | collective-permute-start | bytes 786440 | tf_op jit(solution)/shard_map/ppermute | solution.py:259
  33.4 17.6 %collective-permute-start.1 = (bf16[2,256,256]{2,1,0:T(8,128)(2,1)S(1)}, bf16[2,256,256]{2,1,0:T(8,128)(2,1)S(1)}, u32[]{:S(2)}, u32[]{:S(2)}) collective-permute-start(bf16[2,256,256]{2,1,0:T(8,128)(2,1)S(1)} %get-tuple-element.24), channel_id=1, source_target_pairs={{0,256},{2,258},{4,260},{6,262},{8,264},{10,266},{12,268},{14,270}... | collective-permute-start | bytes 786440 | tf_op jit(solution)/shard_map/ppermute | solution.py:259

commit v7 on v6

--- a/solution.py
+++ b/solution.py
@@ -11,7 +11,7 @@
 HEADS = 8
 INNER = HEAD * HEADS
 KEPT = INNER // 2
-CHUNKS = (1, 1, 1, 1)
+CHUNKS = (3, 1)
 TOGETHER = 4
 FACTOR = HEAD ** (-0.5)
 PARAMS = pltpu.CompilerParams(vmem_limit_bytes=12 * 1024 * 1024)
@@ -106,51 +106,65 @@
         copy.wait()
 
 
-def load_kernel(parts, block, *rest):
-    *chunks, whole, sems = rest
-
-    def split():
-        copies = []
-        for i, ((kept, first), chunk) in enumerate(zip(parts, chunks)):
-            for j, view in enumerate(views(block, side(kept) * KEPT + first, chunk.shape[-1])):
-                copies.append(pltpu.make_async_copy(view, chunk.at[j], sems.at[i, j]))
-        run_copies(copies)
-
-    def all_of_it():
-        run_copies([pltpu.make_async_copy(block, whole, sems.at[0, 0])])
-
-    pl.when(in_split_plan())(split)
-    pl.when(jnp.logical_not(in_split_plan()))(all_of_it)
-
-
-def work_kernel(width, own, received, kept, back):
+def half_copies(block, at, chunk, sems):
+    parts = views(block, at, chunk.shape[-1])
+    return [pltpu.make_async_copy(view, chunk.at[j], sems.at[j]) for j, view in enumerate(parts)]
+
+
+def first_kernel(block, head, sent, sems):
+    split = in_split_plan()
+    pl.when(split)(lambda: run_copies(half_copies(block, side(False) * KEPT, sent, sems)))
+    pl.when(jnp.logical_not(split))(lambda: run_copies(half_copies(block, 0, head, sems)))
+
+
+def second_kernel(block, _, others, own_block, kept, sems):
+    split = in_split_plan()
+
+    def whole():
+        copies = half_copies(block, HEAD, others, sems)
+        run_copies(copies + [pltpu.make_async_copy(block, own_block, sems.at[2])])
+
+    pl.when(split)(lambda: run_copies(half_copies(block, side(True) * KEPT, kept, sems)))
+    pl.when(jnp.logical_not(split))(whole)
+
+
+def work_kernel(own, received, kept, *backs):
     def run(decoder):
         query_side, key_side = (own, received) if decoder else (received, own)
-        front, rear = (kept, back) if decoder else (back, kept)
-        cols = [slice(h * HEAD, (h + 1) * HEAD) for h in range(width // HEAD)]
+        cols = [slice(h * HEAD, (h + 1) * HEAD) for h in range(HEADS // 2)]
         heads = [
             head_work(query_side[0, :, c], query_side[1, :, c], key_side[0, :, c], key_side[1, :, c]) for c in cols
         ]
-        for c, (attended, query_grad, key_grad, value_grad) in zip(cols, side_by_side(heads)):
-            front[0, :, c] = attended
-            front[1, :, c] = query_grad
-            rear[0, :, c] = key_grad
-            rear[1, :, c] = value_grad
+        places = [(back, i) for back in backs for i in range(back.shape[-1] // HEAD)]
+        for c, (back, i), result in zip(cols, places, side_by_side(heads)):
+            front, rear = result[:2], result[2:]
+            stay, go = (front, rear) if decoder else (rear, front)
+            for j in range(2):
+                kept[j, :, c] = stay[j]
+                back[j, :, i * HEAD : (i + 1) * HEAD] = go[j]
 
     split = in_split_plan()
     pl.when(jnp.logical_and(split, on_decoder()))(lambda: run(True))
     pl.when(jnp.logical_and(split, jnp.logical_not(on_decoder())))(lambda: run(False))
 
 
-def whole_kernel(own, received, _, out, stage, sems):
+def whole_kernel(first, own, received, _, out, stage, sems):
     def run(decoder):
-        query_side, key_side = (own, received) if decoder else (received, own)
+        def partner(h, i):
+            if first:
+                return received[0 if decoder else 1, i]
+            return received[i, :, (h - 1) * HEAD : h * HEAD]
+
         copies = []
-        for start in range(0, HEADS, TOGETHER):
-            heads = range(start, start + TOGETHER)
+        todo = range(1) if first else range(1, HEADS)
+        for start in range(0, len(todo), TOGETHER):
+            heads = todo[start : start + TOGETHER]
             cols = {h: [slice(i * INNER + h * HEAD, i * INNER + (h + 1) * HEAD) for i in range(2)] for h in heads}
             work = decoder_half if decoder else encoder_half
-            results = side_by_side([work(*[ref[:, c] for ref in (query_side, key_side) for c in cols[h]]) for h in heads])
+            mine = {h: [own[:, c] for c in cols[h]] for h in heads}
+            theirs = {h: [partner(h, i) for i in range(2)] for h in heads}
+            sides = (mine, theirs) if decoder else (theirs, mine)
+            results = side_by_side([work(*sides[0][h], *sides[1][h]) for h in heads])
             for h, result in zip(heads, results):
                 for i in range(2):
                     stage[h, i] = result[i]
@@ -192,28 +206,38 @@
     widths = [n * HEAD for n in CHUNKS]
     firsts = [sum(widths[:i]) for i in range(len(widths))]
     n = len(widths)
-
-    def load(block, parts):
-        return pl.pallas_call(
-            functools.partial(load_kernel, [(kept, firsts[i]) for kept, i in parts]),
-            out_shape=[pltpu.VMEM((2, rows, widths[i]), jnp.bfloat16) for _, i in parts]
-            + [pltpu.VMEM((rows, both), jnp.bfloat16)],
-            in_specs=[HBM],
-            out_specs=[VMEM] * (len(parts) + 1),
-            scratch_shapes=[pltpu.SemaphoreType.DMA((len(parts), 2))],
-            compiler_params=PARAMS,
-            cost_estimate=cost(0),
-            name="load",
-        )(block)
-
-    def work(width, own, received):
-        return pl.pallas_call(
-            functools.partial(work_kernel, width),
-            out_shape=[jax.ShapeDtypeStruct((2, rows, width), jnp.bfloat16)] * 2,
+    half, head, others = (2, rows, KEPT), (2, rows, HEAD), (2, rows, INNER - HEAD)
+
+    def nothing(shape):
+        return pl.pallas_call(
+            lambda out: None,
+            out_shape=pltpu.VMEM(shape, jnp.bfloat16),
+            out_specs=VMEM,
+            compiler_params=PARAMS,
+            cost_estimate=cost(0),
+            name="nothing",
+        )()
+
+    def load(kernel, shapes, name, *after):
+        return pl.pallas_call(
+            kernel,
+            out_shape=[pltpu.VMEM(shape, jnp.bfloat16) for shape in shapes],
+            in_specs=[HBM] + [ANY] * len(after),
+            out_specs=[VMEM] * len(shapes),
+            scratch_shapes=[pltpu.SemaphoreType.DMA((3,))],
+            compiler_params=PARAMS,
+            cost_estimate=cost(0),
+            name=name,
+        )(block, *after)
+
+    def work(own, received):
+        return pl.pallas_call(
+            work_kernel,
+            out_shape=[jax.ShapeDtypeStruct((2, rows, width), jnp.bfloat16) for width in [KEPT, *widths]],
             in_specs=[VMEM, VMEM],
-            out_specs=[VMEM, VMEM],
-            compiler_params=PARAMS,
-            cost_estimate=cost(0, flops=12 * rows * rows * width, exps=rows * width),
+            out_specs=[VMEM] * (1 + n),
+            compiler_params=PARAMS,
+            cost_estimate=cost(0, flops=12 * rows * rows * KEPT, exps=rows * KEPT),
             name="work",
         )(own, received)
 
@@ -231,9 +255,9 @@
             name="place",
         )(*chunks, *extra)
 
-    def whole(own, received, out):
-        return pl.pallas_call(
-            whole_kernel,
+    def whole(first, own, received, out):
+        return pl.pallas_call(
+            functools.partial(whole_kernel, first),
             out_shape=jax.ShapeDtypeStruct((rows, both), jnp.bfloat16),
             in_specs=[VMEM, VMEM, ANY],
             out_specs=ANY,
@@ -247,20 +271,25 @@
             name="whole",
         )(own, received, out)
 
-    whole_received = lax.ppermute(operands, ("group", "dp"), whole_swaps)
     block = pltpu.with_memory_space_constraint(operands.reshape(rows, both), pltpu.HBM)
-    *chunks, own_block = load(block, [(True, i) for i in range(n)] + [(False, i) for i in range(n)])
-    own, sent = chunks[:n], chunks[n:]
-    received = [lax.ppermute(c, ("group", "dp"), split_swaps) for c in sent]
-    done, returned = [], []
-    for i in range(n):
-        kept, back = work(widths[i], own[i], received[i])
-        done.append(kept)
-        returned.append(lax.ppermute(back, ("group", "dp"), split_swaps))
-    out = place(True, firsts, done)
+    first_head, sent = load(first_kernel, [head, half], "first")
+    gathered = lax.cond(
+        in_split_plan(),
+        lambda chunk: nothing((2, *head)),
+        lambda chunk: lax.all_gather(chunk, "group"),
+        first_head,
+    )
+    gathered, sent = lax.optimization_barrier((gathered, sent))
+    received = lax.ppermute(sent, ("group", "dp"), split_swaps)
+    other_heads, own_block, own = load(second_kernel, [others, (rows, both), half], "second", gathered)
+    whole_received = lax.ppermute(other_heads, ("group", "dp"), whole_swaps)
+    kept, *backs = work(own, received)
+    returned = [lax.ppermute(back, ("group", "dp"), split_swaps) for back in backs]
+    out = place(True, [0], [kept])
+    out = whole(True, own_block, gathered, out)
     for i in range(n):
         if i == n - 1:
-            out = whole(own_block, whole_received.reshape(rows, both), out)
+            out = whole(False, own_block, whole_received, out)
         out = place(False, [firsts[i]], [returned[i]], out)
     return out.reshape(operands.shape)
 

time: 52 us -> 53.7 us (1.033)
  the two profiles are of different devices: /device:TPU:56 before, /device:TPU:4 now
where the time goes in v7:
time: 53.7 us; the launch traced here: 53.4 us
  waiting for transfers between devices  30.2 us (56%)
  starting transfers between devices  16.4 us (31%)
  Pallas kernels  6.75 us (13%)
    ppermute x1, waiting for transfers between devices, local(): received = lax.ppermute(sent, ('group', 'dp'), split_swaps)  18 us
    ppermute x2, waiting for transfers between devices, local(): lax.ppermute(back, ('group', 'dp'), split_swaps)  12.2 us
    ppermute x2, starting transfers between devices, local(): lax.ppermute(back, ('group', 'dp'), split_swaps)  7.81 us
    ppermute x1, starting transfers between devices, local(): received = lax.ppermute(sent, ('group', 'dp'), split_swaps)  7.79 us
    pallas_call x3, Pallas kernels, place(): pl.pallas_call(functools.partial(place_kernel, kept, at, bool(extra)), ou...  2.6 us
    pallas_call x2, Pallas kernels, load(): pl.pallas_call(kernel, out_shape=[pltpu.VMEM(shape, jnp.bfloat16) for sha...  2.47 us
    pallas_call x1, Pallas kernels, work(): pl.pallas_call(work_kernel, out_shape=[jax.ShapeDtypeStruct((2, rows, wid...  1.35 us
  transfers between devices with their start and end apart: 4, of which 3 were waited for; matrix products, arithmetic and copies ran while one was open for 0% of the time, Pallas kernels for 9%

profile of v7, /device:TPU:4, one launch (start us, length us, event | category | flops | bytes accessed | tf_op | source)
XLA Modules:
  0.0 53.4 jit_solution(9945490030193319247)
XLA Ops:
  0.0 1.2 %first.1 = (bf16[2,256,256]{2,1,0:T(8,128)(2,1)S(1)}, bf16[2,256,1024]{2,1,0:T(8,128)(2,1)S(1)}) custom-call(bf16[256,4096]{1,0:T(8,128)(2,1)} %bitcast.4), custom_call_target="tpu_custom_call" | custom-call | tf_op jit(solution)/shard_map/first/pallas_call | solution.py:222
  1.3 7.8 %collective-permute-start = (bf16[2,256,1024]{2,1,0:T(8,128)(2,1)S(1)}, bf16[2,256,1024]{2,1,0:T(8,128)(2,1)S(1)}, u32[]{:S(2)}, u32[]{:S(2)}) collective-permute-start(bf16[2,256,1024]{2,1,0:T(8,128)(2,1)S(1)} %get-tuple-element.23), channel_id=1, source_target_pairs={{0,256},{2,258},{4,260},{6,262},{8,264},{10,266},{12,268},{14,270}... | collective-permute-start | bytes 3145736 | tf_op jit(solution)/shard_map/ppermute | solution.py:283
  9.1 1.2 %second.1 = (bf16[2,256,1792]{2,1,0:T(8,128)(2,1)S(1)}, bf16[256,4096]{1,0:T(8,128)(2,1)S(1)}, bf16[2,256,1024]{2,1,0:T(8,128)(2,1)S(1)}) custom-call(bf16[256,4096]{1,0:T(8,128)(2,1)} %bitcast.5, bf16[2,2,256,256]{3,2,1,0:T(8,128)(2,1)S(1)} %get-tuple-element.29._.received), custom_call_target="tpu_custom_call" | custom-call | tf_op jit(solution)/shard_map/second/pallas_call | solution.py:222
  10.3 0.8 %collective-permute-start.2 = (bf16[2,256,1792]{2,1,0:T(8,128)(2,1)S(1)}, bf16[2,256,1792]{2,1,0:T(8,128)(2,1)S(1)}, u32[]{:S(2)}, u32[]{:S(2)}) collective-permute-start(bf16[2,256,1792]{2,1,0:T(8,128)(2,1)S(1)} %get-tuple-element.26), channel_id=1, source_target_pairs={{1,257},{3,259},{5,261},{7,263},{9,265},{11,267},{13,269},{15,271}... | collective-permute-start | bytes 5505032 | tf_op jit(solution)/shard_map/ppermute | solution.py:285
  11.1 18.0 %collective-permute-done.received = bf16[2,256,1024]{2,1,0:T(8,128)(2,1)S(1)} collective-permute-done((bf16[2,256,1024]{2,1,0:T(8,128)(2,1)S(1)}, bf16[2,256,1024]{2,1,0:T(8,128)(2,1)S(1)}, u32[]{:S(2)}, u32[]{:S(2)}) %collective-permute-start) | collective-permute-done | bytes 1048608 | tf_op jit(solution)/shard_map/ppermute | solution.py:283
  29.1 1.3 %work.1 = (bf16[2,256,1024]{2,1,0:T(8,128)(2,1)S(1)}, bf16[2,256,768]{2,1,0:T(8,128)(2,1)S(1)}, bf16[2,256,256]{2,1,0:T(8,128)(2,1)S(1)}) custom-call(bf16[2,256,1024]{2,1,0:T(8,128)(2,1)S(1)} %get-tuple-element.22.own, bf16[2,256,1024]{2,1,0:T(8,128)(2,1)S(1)} %collective-permute-done.received), custom_call_target="tpu_custom_call" | custom-call | flops 805306368 | tf_op jit(solution)/shard_map/work/pallas_call | solution.py:234
  30.4 5.9 %collective-permute-start.3 = (bf16[2,256,768]{2,1,0:T(8,128)(2,1)S(1)}, bf16[2,256,768]{2,1,0:T(8,128)(2,1)S(1)}, u32[]{:S(2)}, u32[]{:S(2)}) collective-permute-start(bf16[2,256,768]{2,1,0:T(8,128)(2,1)S(1)} %get-tuple-element.27), channel_id=1, source_target_pairs={{0,256},{2,258},{4,260},{6,262},{8,264},{10,266},{12,268},{14,270}... | collective-permute-start | bytes 2359304 | tf_op jit(solution)/shard_map/ppermute | solution.py:287
  36.3 1.9 %collective-permute-start.1 = (bf16[2,256,256]{2,1,0:T(8,128)(2,1)S(1)}, bf16[2,256,256]{2,1,0:T(8,128)(2,1)S(1)}, u32[]{:S(2)}, u32[]{:S(2)}) collective-permute-start(bf16[2,256,256]{2,1,0:T(8,128)(2,1)S(1)} %get-tuple-element.24), channel_id=1, source_target_pairs={{0,256},{2,258},{4,260},{6,262},{8,264},{10,266},{12,268},{14,270}... | collective-permute-start | bytes 786440 | tf_op jit(solution)/shard_map/ppermute | solution.py:287
  38.2 1.0 %place.3._ = bf16[256,4096]{1,0:T(8,128)(2,1)} custom-call(bf16[2,256,1024]{2,1,0:T(8,128)(2,1)S(1)} %get-tuple-element.28.rest_0_), custom_call_target="tpu_custom_call" | custom-call | tf_op jit(solution)/shard_map/place/pallas_call | solution.py:246
  39.2 0.2 whole.2.rest_1_
  39.4 10.5 %collective-permute-done.3.rest_0_ = bf16[2,256,768]{2,1,0:T(8,128)(2,1)S(1)} collective-permute-done((bf16[2,256,768]{2,1,0:T(8,128)(2,1)S(1)}, bf16[2,256,768]{2,1,0:T(8,128)(2,1)S(1)}, u32[]{:S(2)}, u32[]{:S(2)}) %collective-permute-start.3) | collective-permute-done | bytes 786464 | tf_op jit(solution)/shard_map/ppermute | solution.py:287
  49.9 0.9 %place.4._ = bf16[256,4096]{1,0:T(8,128)(2,1)} custom-call(bf16[2,256,768]{2,1,0:T(8,128)(2,1)S(1)} %collective-permute-done.3.rest_0_, bf16[256,4096]{1,0:T(8,128)(2,1)} %whole.2.rest_1_), custom_call_target="tpu_custom_call", output_to_operand_aliasing={{}: (1, {})} | custom-call | tf_op jit(solution)/shard_map/place/pallas_call | solution.py:246
  50.8 0.0 collective-permute-done.2.received
  50.8 0.2 whole.3.rest_1_
  51.0 1.7 %collective-permute-done.1.rest_0_ = bf16[2,256,256]{2,1,0:T(8,128)(2,1)S(1)} collective-permute-done((bf16[2,256,256]{2,1,0:T(8,128)(2,1)S(1)}, bf16[2,256,256]{2,1,0:T(8,128)(2,1)S(1)}, u32[]{:S(2)}, u32[]{:S(2)}) %collective-permute-start.1) | collective-permute-done | bytes 262176 | tf_op jit(solution)/shard_map/ppermute | solution.py:287
  52.7 0.7 %place.5 = bf16[256,4096]{1,0:T(8,128)(2,1)} custom-call(bf16[2,256,256]{2,1,0:T(8,128)(2,1)S(1)} %collective-permute-done.1.rest_0_, bf16[256,4096]{1,0:T(8,128)(2,1)} %whole.3.rest_1_), custom_call_target="tpu_custom_call", output_to_operand_aliasing={{}: (1, {})} | custom-call | tf_op jit(solution)/shard_map/place/pallas_call | solution.py:246
  (2 shorter events, 0.0 us)
Async XLA Ops:
  1.3 27.8 %collective-permute-start = (bf16[2,256,1024]{2,1,0:T(8,128)(2,1)S(1)}, bf16[2,256,1024]{2,1,0:T(8,128)(2,1)S(1)}, u32[]{:S(2)}, u32[]{:S(2)}) collective-permute-start(bf16[2,256,1024]{2,1,0:T(8,128)(2,1)S(1)} %get-tuple-element.23), channel_id=1, source_target_pairs={{0,256},{2,258},{4,260},{6,262},{8,264},{10,266},{12,268},{14,270}... | collective-permute-start | bytes 3145736 | tf_op jit(solution)/shard_map/ppermute | solution.py:283
  10.3 40.5 %collective-permute-start.2 = (bf16[2,256,1792]{2,1,0:T(8,128)(2,1)S(1)}, bf16[2,256,1792]{2,1,0:T(8,128)(2,1)S(1)}, u32[]{:S(2)}, u32[]{:S(2)}) collective-permute-start(bf16[2,256,1792]{2,1,0:T(8,128)(2,1)S(1)} %get-tuple-element.26), channel_id=1, source_target_pairs={{1,257},{3,259},{5,261},{7,263},{9,265},{11,267},{13,269},{15,271}... | collective-permute-start | bytes 5505032 | tf_op jit(solution)/shard_map/ppermute | solution.py:285
  30.4 19.5 %collective-permute-start.3 = (bf16[2,256,768]{2,1,0:T(8,128)(2,1)S(1)}, bf16[2,256,768]{2,1,0:T(8,128)(2,1)S(1)}, u32[]{:S(2)}, u32[]{:S(2)}) collective-permute-start(bf16[2,256,768]{2,1,0:T(8,128)(2,1)S(1)} %get-tuple-element.27), channel_id=1, source_target_pairs={{0,256},{2,258},{4,260},{6,262},{8,264},{10,266},{12,268},{14,270}... | collective-permute-start | bytes 2359304 | tf_op jit(solution)/shard_map/ppermute | solution.py:287
  36.3 16.4 %collective-permute-start.1 = (bf16[2,256,256]{2,1,0:T(8,128)(2,1)S(1)}, bf16[2,256,256]{2,1,0:T(8,128)(2,1)S(1)}, u32[]{:S(2)}, u32[]{:S(2)}) collective-permute-start(bf16[2,256,256]{2,1,0:T(8,128)(2,1)S(1)} %get-tuple-element.24), channel_id=1, source_target_pairs={{0,256},{2,258},{4,260},{6,262},{8,264},{10,266},{12,268},{14,270}... | collective-permute-start | bytes 786440 | tf_op jit(solution)/shard_map/ppermute | solution.py:287

commit v8 on v7

--- a/solution.py
+++ b/solution.py
@@ -13,6 +13,7 @@
 KEPT = INNER // 2
 CHUNKS = (3, 1)
 TOGETHER = 4
+EARLY = (2 * HEAD, HEAD + HEAD // 2)
 FACTOR = HEAD ** (-0.5)
 PARAMS = pltpu.CompilerParams(vmem_limit_bytes=12 * 1024 * 1024)
 
@@ -111,24 +112,37 @@
     return [pltpu.make_async_copy(view, chunk.at[j], sems.at[j]) for j, view in enumerate(parts)]
 
 
-def first_kernel(block, head, sent, sems):
+def first_kernel(block, early, sent, sems):
     split = in_split_plan()
+
+    def whole():
+        copies = []
+        for i, (to, count) in enumerate(((0, EARLY[0]), (EARLY[0], EARLY[1]))):
+            part = block.at[:, i * INNER : i * INNER + count]
+            copies.append(pltpu.make_async_copy(part, early.at[:, to : to + count], sems.at[i]))
+        run_copies(copies)
+
     pl.when(split)(lambda: run_copies(half_copies(block, side(False) * KEPT, sent, sems)))
-    pl.when(jnp.logical_not(split))(lambda: run_copies(half_copies(block, 0, head, sems)))
+    pl.when(jnp.logical_not(split))(whole)
 
 
 def second_kernel(block, _, others, own_block, kept, sems):
     split = in_split_plan()
 
     def whole():
-        copies = half_copies(block, HEAD, others, sems)
-        run_copies(copies + [pltpu.make_async_copy(block, own_block, sems.at[2])])
+        copies = [pltpu.make_async_copy(block, own_block, sems.at[2])]
+        for i, to in enumerate((0, INNER - EARLY[0])):
+            part = block.at[:, i * INNER + EARLY[i] : (i + 1) * INNER]
+            copies.append(pltpu.make_async_copy(part, others.at[:, to : to + INNER - EARLY[i]], sems.at[i]))
+        run_copies(copies)
 
     pl.when(split)(lambda: run_copies(half_copies(block, side(True) * KEPT, kept, sems)))
     pl.when(jnp.logical_not(split))(whole)
 
 
-def work_kernel(own, received, kept, *backs):
+def work_kernel(own, received, out, *rest):
+    *backs, kept, sems = rest
+
     def run(decoder):
         query_side, key_side = (own, received) if decoder else (received, own)
         cols = [slice(h * HEAD, (h + 1) * HEAD) for h in range(HEADS // 2)]
@@ -142,18 +156,28 @@
             for j in range(2):
                 kept[j, :, c] = stay[j]
                 back[j, :, i * HEAD : (i + 1) * HEAD] = go[j]
+        parts = views(out, side(True) * KEPT, KEPT)
+        run_copies([pltpu.make_async_copy(kept.at[j], view, sems.at[j]) for j, view in enumerate(parts)])
 
     split = in_split_plan()
     pl.when(jnp.logical_and(split, on_decoder()))(lambda: run(True))
     pl.when(jnp.logical_and(split, jnp.logical_not(on_decoder())))(lambda: run(False))
 
 
-def whole_kernel(first, own, received, _, out, stage, sems):
+def whole_kernel(first, own, *rest):
+    gathered, *received, _, out, stage, sems = rest
+
     def run(decoder):
         def partner(h, i):
-            if first:
-                return received[0 if decoder else 1, i]
-            return received[i, :, (h - 1) * HEAD : h * HEAD]
+            start, end, early = h * HEAD, (h + 1) * HEAD, EARLY[i]
+            parts = []
+            if start < early:
+                at = i * EARLY[0]
+                parts.append(gathered[0 if decoder else 1, :, at + start : at + min(end, early)])
+            if end > early:
+                at = i * (INNER - EARLY[0]) - early
+                parts.append(received[0][:, at + max(start, early) : at + end])
+            return parts[0] if len(parts) == 1 else jnp.concatenate(parts, axis=1)
 
         copies = []
         todo = range(1) if first else range(1, HEADS)
@@ -178,17 +202,10 @@
     pl.when(jnp.logical_and(whole, jnp.logical_not(on_decoder())))(lambda: run(False))
 
 
-def place_kernel(kept, firsts, aliased, *rest):
-    *chunks, out, sems = rest
-    if aliased:
-        chunks = chunks[:-1]
-
+def place_kernel(first, chunk, _, out, sems):
     def run():
-        copies = []
-        for i, (first, chunk) in enumerate(zip(firsts, chunks)):
-            for j, view in enumerate(views(out, side(kept) * KEPT + first, chunk.shape[-1])):
-                copies.append(pltpu.make_async_copy(chunk.at[j], view, sems.at[i, j]))
-        run_copies(copies)
+        parts = views(out, side(False) * KEPT + first, chunk.shape[-1])
+        run_copies([pltpu.make_async_copy(chunk.at[j], view, sems.at[j]) for j, view in enumerate(parts)])
 
     pl.when(in_split_plan())(run)
 
@@ -206,7 +223,7 @@
     widths = [n * HEAD for n in CHUNKS]
     firsts = [sum(widths[:i]) for i in range(len(widths))]
     n = len(widths)
-    half, head, others = (2, rows, KEPT), (2, rows, HEAD), (2, rows, INNER - HEAD)
+    half, early, others = (2, rows, KEPT), (rows, sum(EARLY)), (rows, both - sum(EARLY))
 
     def nothing(shape):
         return pl.pallas_call(
@@ -233,64 +250,64 @@
     def work(own, received):
         return pl.pallas_call(
             work_kernel,
-            out_shape=[jax.ShapeDtypeStruct((2, rows, width), jnp.bfloat16) for width in [KEPT, *widths]],
+            out_shape=[jax.ShapeDtypeStruct((rows, both), jnp.bfloat16)]
+            + [jax.ShapeDtypeStruct((2, rows, width), jnp.bfloat16) for width in widths],
             in_specs=[VMEM, VMEM],
-            out_specs=[VMEM] * (1 + n),
+            out_specs=[ANY] + [VMEM] * n,
+            scratch_shapes=[pltpu.VMEM(half, jnp.bfloat16), pltpu.SemaphoreType.DMA((2,))],
             compiler_params=PARAMS,
             cost_estimate=cost(0, flops=12 * rows * rows * KEPT, exps=rows * KEPT),
             name="work",
         )(own, received)
 
-    def place(kept, at, chunks, out=None):
-        extra = [] if out is None else [out]
-        return pl.pallas_call(
-            functools.partial(place_kernel, kept, at, bool(extra)),
+    def place(first, chunk, out):
+        return pl.pallas_call(
+            functools.partial(place_kernel, first),
             out_shape=jax.ShapeDtypeStruct((rows, both), jnp.bfloat16),
-            in_specs=[VMEM] * len(chunks) + [ANY] * len(extra),
+            in_specs=[VMEM, ANY],
             out_specs=ANY,
-            scratch_shapes=[pltpu.SemaphoreType.DMA((len(chunks), 2))],
-            input_output_aliases={len(chunks): 0} if extra else {},
+            scratch_shapes=[pltpu.SemaphoreType.DMA((2,))],
+            input_output_aliases={1: 0},
             compiler_params=PARAMS,
             cost_estimate=cost(0),
             name="place",
-        )(*chunks, *extra)
+        )(chunk, out)
 
     def whole(first, own, received, out):
         return pl.pallas_call(
             functools.partial(whole_kernel, first),
             out_shape=jax.ShapeDtypeStruct((rows, both), jnp.bfloat16),
-            in_specs=[VMEM, VMEM, ANY],
+            in_specs=[VMEM] * (1 + len(received)) + [ANY],
             out_specs=ANY,
             scratch_shapes=[
                 pltpu.VMEM((HEADS, 2, rows, HEAD), jnp.bfloat16),
                 pltpu.SemaphoreType.DMA((HEADS, 2)),
             ],
-            input_output_aliases={2: 0},
+            input_output_aliases={1 + len(received): 0},
             compiler_params=PARAMS,
             cost_estimate=cost(0),
             name="whole",
-        )(own, received, out)
+        )(own, *received, out)
 
     block = pltpu.with_memory_space_constraint(operands.reshape(rows, both), pltpu.HBM)
-    first_head, sent = load(first_kernel, [head, half], "first")
+    first_columns, sent = load(first_kernel, [early, half], "first")
     gathered = lax.cond(
         in_split_plan(),
-        lambda chunk: nothing((2, *head)),
+        lambda chunk: nothing((2, *early)),
         lambda chunk: lax.all_gather(chunk, "group"),
-        first_head,
+        first_columns,
     )
     gathered, sent = lax.optimization_barrier((gathered, sent))
     received = lax.ppermute(sent, ("group", "dp"), split_swaps)
-    other_heads, own_block, own = load(second_kernel, [others, (rows, both), half], "second", gathered)
-    whole_received = lax.ppermute(other_heads, ("group", "dp"), whole_swaps)
-    kept, *backs = work(own, received)
+    other_columns, own_block, own = load(second_kernel, [others, (rows, both), half], "second", gathered)
+    whole_received = lax.ppermute(other_columns, ("group", "dp"), whole_swaps)
+    out, *backs = work(own, received)
     returned = [lax.ppermute(back, ("group", "dp"), split_swaps) for back in backs]
-    out = place(True, [0], [kept])
-    out = whole(True, own_block, gathered, out)
+    out = whole(True, own_block, [gathered], out)
     for i in range(n):
         if i == n - 1:
-            out = whole(False, own_block, whole_received, out)
-        out = place(False, [firsts[i]], [returned[i]], out)
+            out = whole(False, own_block, [gathered, whole_received], out)
+        out = place(firsts[i], returned[i], out)
     return out.reshape(operands.shape)
 
 

time: 53.7 us -> 51.7 us (0.963)
  the two profiles are of different devices: /device:TPU:4 before, /device:TPU:56 now
where the time goes in v8:
time: 51.7 us; the launch traced here: 51.4 us
  waiting for transfers between devices  31.5 us (61%)
  starting transfers between devices  13 us (25%)
  Pallas kernels  6.74 us (13%)
    ppermute x2, waiting for transfers between devices, local(): lax.ppermute(back, ('group', 'dp'), split_swaps)  18 us
    ppermute x1, waiting for transfers between devices, local(): received = lax.ppermute(sent, ('group', 'dp'), split_swaps)  13.6 us
    ppermute x2, starting transfers between devices, local(): lax.ppermute(back, ('group', 'dp'), split_swaps)  7.35 us
    ppermute x1, starting transfers between devices, local(): received = lax.ppermute(sent, ('group', 'dp'), split_swaps)  4.93 us
    pallas_call x2, Pallas kernels, load(): pl.pallas_call(kernel, out_shape=[pltpu.VMEM(shape, jnp.bfloat16) for sha...  2.47 us
    pallas_call x1, Pallas kernels, work(): pl.pallas_call(work_kernel, out_shape=[jax.ShapeDtypeStruct((rows, both),...  2.33 us
    pallas_call x2, Pallas kernels, place(): pl.pallas_call(functools.partial(place_kernel, first), out_shape=jax.Shap...  1.61 us
  transfers between devices with their start and end apart: 4, of which 3 were waited for; matrix products, arithmetic and copies ran while one was open for 0% of the time, Pallas kernels for 9%

profile of v8, /device:TPU:56, one launch (start us, length us, event | category | flops | bytes accessed | tf_op | source)
XLA Modules:
  0.0 51.4 jit_solution(10147352106211878942)
XLA Ops:
  0.0 1.2 %first.1 = (bf16[256,896]{1,0:T(8,128)(2,1)S(1)}, bf16[2,256,1024]{2,1,0:T(8,128)(2,1)S(1)}) custom-call(bf16[256,4096]{1,0:T(8,128)(2,1)} %bitcast.4), custom_call_target="tpu_custom_call" | custom-call | tf_op jit(solution)/shard_map/first/pallas_call | solution.py:239
  1.3 4.9 %collective-permute-start = (bf16[2,256,1024]{2,1,0:T(8,128)(2,1)S(1)}, bf16[2,256,1024]{2,1,0:T(8,128)(2,1)S(1)}, u32[]{:S(2)}, u32[]{:S(2)}) collective-permute-start(bf16[2,256,1024]{2,1,0:T(8,128)(2,1)S(1)} %get-tuple-element.23), channel_id=1, source_target_pairs={{0,256},{2,258},{4,260},{6,262},{8,264},{10,266},{12,268},{14,270}... | collective-permute-start | bytes 3145736 | tf_op jit(solution)/shard_map/ppermute | solution.py:301
  6.2 1.2 %second.1 = (bf16[256,3200]{1,0:T(8,128)(2,1)S(1)}, bf16[256,4096]{1,0:T(8,128)(2,1)S(1)}, bf16[2,256,1024]{2,1,0:T(8,128)(2,1)S(1)}) custom-call(bf16[256,4096]{1,0:T(8,128)(2,1)} %bitcast.5, bf16[2,256,896]{2,1,0:T(8,128)(2,1)S(1)} %get-tuple-element.29._.rest_0_), custom_call_target="tpu_custom_call" | custom-call | tf_op jit(solution)/shard_map/second/pallas_call | solution.py:239
  7.5 0.8 %collective-permute-start.2 = (bf16[256,3200]{1,0:T(8,128)(2,1)S(1)}, bf16[256,3200]{1,0:T(8,128)(2,1)S(1)}, u32[]{:S(2)}, u32[]{:S(2)}) collective-permute-start(bf16[256,3200]{1,0:T(8,128)(2,1)S(1)} %get-tuple-element.26), channel_id=1, source_target_pairs={{1,257},{3,259},{5,261},{7,263},{9,265},{11,267},{13,269},{15,271}... | collective-permute-start | bytes 4915208 | tf_op jit(solution)/shard_map/ppermute | solution.py:303
  8.2 13.6 %collective-permute-done.received = bf16[2,256,1024]{2,1,0:T(8,128)(2,1)S(1)} collective-permute-done((bf16[2,256,1024]{2,1,0:T(8,128)(2,1)S(1)}, bf16[2,256,1024]{2,1,0:T(8,128)(2,1)S(1)}, u32[]{:S(2)}, u32[]{:S(2)}) %collective-permute-start) | collective-permute-done | bytes 1048608 | tf_op jit(solution)/shard_map/ppermute | solution.py:301
  21.8 2.3 %work.1 = (bf16[256,4096]{1,0:T(8,128)(2,1)}, bf16[2,256,768]{2,1,0:T(8,128)(2,1)S(1)}, bf16[2,256,256]{2,1,0:T(8,128)(2,1)S(1)}) custom-call(bf16[2,256,1024]{2,1,0:T(8,128)(2,1)S(1)} %get-tuple-element.22.own, bf16[2,256,1024]{2,1,0:T(8,128)(2,1)S(1)} %collective-permute-done.received), custom_call_target="tpu_custom_call" | custom-call | flops 805306368 | tf_op jit(solution)/shard_map/work/pallas_call | solution.py:251
  24.1 4.6 %collective-permute-start.3 = (bf16[2,256,768]{2,1,0:T(8,128)(2,1)S(1)}, bf16[2,256,768]{2,1,0:T(8,128)(2,1)S(1)}, u32[]{:S(2)}, u32[]{:S(2)}) collective-permute-start(bf16[2,256,768]{2,1,0:T(8,128)(2,1)S(1)} %get-tuple-element.27), channel_id=1, source_target_pairs={{0,256},{2,258},{4,260},{6,262},{8,264},{10,266},{12,268},{14,270}... | collective-permute-start | bytes 2359304 | tf_op jit(solution)/shard_map/ppermute | solution.py:305
  28.8 2.7 %collective-permute-start.1 = (bf16[2,256,256]{2,1,0:T(8,128)(2,1)S(1)}, bf16[2,256,256]{2,1,0:T(8,128)(2,1)S(1)}, u32[]{:S(2)}, u32[]{:S(2)}) collective-permute-start(bf16[2,256,256]{2,1,0:T(8,128)(2,1)S(1)} %get-tuple-element.24), channel_id=1, source_target_pairs={{0,256},{2,258},{4,260},{6,262},{8,264},{10,266},{12,268},{14,270}... | collective-permute-start | bytes 786440 | tf_op jit(solution)/shard_map/ppermute | solution.py:305
  31.5 0.2 whole.2._
  31.7 16.2 %collective-permute-done.3.chunk = bf16[2,256,768]{2,1,0:T(8,128)(2,1)S(1)} collective-permute-done((bf16[2,256,768]{2,1,0:T(8,128)(2,1)S(1)}, bf16[2,256,768]{2,1,0:T(8,128)(2,1)S(1)}, u32[]{:S(2)}, u32[]{:S(2)}) %collective-permute-start.3) | collective-permute-done | bytes 786464 | tf_op jit(solution)/shard_map/ppermute | solution.py:305
  47.9 0.9 %place.2.rest_2_ = bf16[256,4096]{1,0:T(8,128)(2,1)} custom-call(bf16[2,256,768]{2,1,0:T(8,128)(2,1)S(1)} %collective-permute-done.3.chunk, bf16[256,4096]{1,0:T(8,128)(2,1)} %whole.2._), custom_call_target="tpu_custom_call", output_to_operand_aliasing={{}: (1, {})} | custom-call | tf_op jit(solution)/shard_map/place/pallas_call | solution.py:264
  48.8 0.0 collective-permute-done.2.rest_1_
  48.8 0.2 whole.3._
  49.0 1.7 %collective-permute-done.1.chunk = bf16[2,256,256]{2,1,0:T(8,128)(2,1)S(1)} collective-permute-done((bf16[2,256,256]{2,1,0:T(8,128)(2,1)S(1)}, bf16[2,256,256]{2,1,0:T(8,128)(2,1)S(1)}, u32[]{:S(2)}, u32[]{:S(2)}) %collective-permute-start.1) | collective-permute-done | bytes 262176 | tf_op jit(solution)/shard_map/ppermute | solution.py:305
  50.7 0.7 %place.3 = bf16[256,4096]{1,0:T(8,128)(2,1)} custom-call(bf16[2,256,256]{2,1,0:T(8,128)(2,1)S(1)} %collective-permute-done.1.chunk, bf16[256,4096]{1,0:T(8,128)(2,1)} %whole.3._), custom_call_target="tpu_custom_call", output_to_operand_aliasing={{}: (1, {})} | custom-call | tf_op jit(solution)/shard_map/place/pallas_call | solution.py:264
  (2 shorter events, 0.0 us)
Async XLA Ops:
  1.3 20.5 %collective-permute-start = (bf16[2,256,1024]{2,1,0:T(8,128)(2,1)S(1)}, bf16[2,256,1024]{2,1,0:T(8,128)(2,1)S(1)}, u32[]{:S(2)}, u32[]{:S(2)}) collective-permute-start(bf16[2,256,1024]{2,1,0:T(8,128)(2,1)S(1)} %get-tuple-element.23), channel_id=1, source_target_pairs={{0,256},{2,258},{4,260},{6,262},{8,264},{10,266},{12,268},{14,270}... | collective-permute-start | bytes 3145736 | tf_op jit(solution)/shard_map/ppermute | solution.py:301
  7.5 41.4 %collective-permute-start.2 = (bf16[256,3200]{1,0:T(8,128)(2,1)S(1)}, bf16[256,3200]{1,0:T(8,128)(2,1)S(1)}, u32[]{:S(2)}, u32[]{:S(2)}) collective-permute-start(bf16[256,3200]{1,0:T(8,128)(2,1)S(1)} %get-tuple-element.26), channel_id=1, source_target_pairs={{1,257},{3,259},{5,261},{7,263},{9,265},{11,267},{13,269},{15,271}... | collective-permute-start | bytes 4915208 | tf_op jit(solution)/shard_map/ppermute | solution.py:303
  24.1 23.8 %collective-permute-start.3 = (bf16[2,256,768]{2,1,0:T(8,128)(2,1)S(1)}, bf16[2,256,768]{2,1,0:T(8,128)(2,1)S(1)}, u32[]{:S(2)}, u32[]{:S(2)}) collective-permute-start(bf16[2,256,768]{2,1,0:T(8,128)(2,1)S(1)} %get-tuple-element.27), channel_id=1, source_target_pairs={{0,256},{2,258},{4,260},{6,262},{8,264},{10,266},{12,268},{14,270}... | collective-permute-start | bytes 2359304 | tf_op jit(solution)/shard_map/ppermute | solution.py:305
  28.8 21.9 %collective-permute-start.1 = (bf16[2,256,256]{2,1,0:T(8,128)(2,1)S(1)}, bf16[2,256,256]{2,1,0:T(8,128)(2,1)S(1)}, u32[]{:S(2)}, u32[]{:S(2)}) collective-permute-start(bf16[2,256,256]{2,1,0:T(8,128)(2,1)S(1)} %get-tuple-element.24), channel_id=1, source_target_pairs={{0,256},{2,258},{4,260},{6,262},{8,264},{10,266},{12,268},{14,270}... | collective-permute-start | bytes 786440 | tf_op jit(solution)/shard_map/ppermute | solution.py:305

commit v9 on v6

--- a/solution.py
+++ b/solution.py
@@ -11,7 +11,7 @@
 HEADS = 8
 INNER = HEAD * HEADS
 KEPT = INNER // 2
-CHUNKS = (1, 1, 1, 1)
+CHUNKS = (2, 1, 1)
 TOGETHER = 4
 FACTOR = HEAD ** (-0.5)
 PARAMS = pltpu.CompilerParams(vmem_limit_bytes=12 * 1024 * 1024)

time: 52 us -> 52 us (level)
  waiting for transfers between devices: 9.61 us -> 16.4 us
  starting transfers between devices: 32.3 us -> 27.2 us
  Pallas kernels: 9.58 us -> 7.92 us
    ppermute x4 -> x3, waiting for transfers between devices: 0.01 us -> 5.96 us  [local(): received = [lax.ppermute(c, ('group', 'dp'), split_swaps) for c in sent]]
    ppermute x4 -> x3, starting transfers between devices: 16.8 us -> 14.2 us  [local(): returned.append(lax.ppermute(back, ('group', 'dp'), split_swaps))]
    ppermute x4 -> x3, starting transfers between devices: 14.7 us -> 12.3 us  [local(): received = [lax.ppermute(c, ('group', 'dp'), split_swaps) for c in sent]]
    pallas_call x4 -> x3, Pallas kernels: 3.71 us -> 2.86 us  [work(): pl.pallas_call(functools.partial(work_kernel, width), out_shape=[jax.Shap...]
    ppermute x4 -> x3, waiting for transfers between devices: 9.6 us -> 10.4 us  [local(): returned.append(lax.ppermute(back, ('group', 'dp'), split_swaps))]
    pallas_call x5 -> x4, Pallas kernels: 3.91 us -> 3.25 us  [place(): pl.pallas_call(functools.partial(place_kernel, kept, at, bool(extra)), ou...]
  transfers between devices with their start and end apart: 9 -> 7, of which waited for: 3 -> 4; matrix products, arithmetic and copies ran while one was open for 0% -> 0% of each run, Pallas kernels for 17% -> 14%
where the time goes in v9:
time: 52 us; the launch traced here: 51.7 us
  starting transfers between devices  27.2 us (52%)
  waiting for transfers between devices  16.4 us (32%)
  Pallas kernels  7.92 us (15%)
    ppermute x3, starting transfers between devices, local(): returned.append(lax.ppermute(back, ('group', 'dp'), split_swaps))  14.2 us
    ppermute x3, starting transfers between devices, local(): received = [lax.ppermute(c, ('group', 'dp'), split_swaps) for c in sent]  12.3 us
    ppermute x3, waiting for transfers between devices, local(): returned.append(lax.ppermute(back, ('group', 'dp'), split_swaps))  10.4 us
    ppermute x3, waiting for transfers between devices, local(): received = [lax.ppermute(c, ('group', 'dp'), split_swaps) for c in sent]  5.96 us
    pallas_call x4, Pallas kernels, place(): pl.pallas_call(functools.partial(place_kernel, kept, at, bool(extra)), ou...  3.25 us
    pallas_call x3, Pallas kernels, work(): pl.pallas_call(functools.partial(work_kernel, width), out_shape=[jax.Shap...  2.86 us
    pallas_call x1, Pallas kernels, load(): pl.pallas_call(functools.partial(load_kernel, [(kept, firsts[i]) for kept...  1.64 us
  transfers between devices with their start and end apart: 7, of which 4 were waited for; matrix products, arithmetic and copies ran while one was open for 0% of the time, Pallas kernels for 14%

profile of v9, /device:TPU:56, one launch (start us, length us, event | category | flops | bytes accessed | tf_op | source)
XLA Modules:
  0.0 51.7 jit_solution(6034712187070034777)
XLA Ops:
  0.0 0.8 %collective-permute-start.2 = (bf16[1,1,256,4096]{3,2,1,0:T(8,128)(2,1)}, bf16[1,1,256,4096]{3,2,1,0:T(8,128)(2,1)S(1)}, u32[]{:S(2)}, u32[]{:S(2)}) collective-permute-start(bf16[1,1,256,4096]{3,2,1,0:T(8,128)(2,1)} %param.1), channel_id=1, source_target_pairs={{1,257},{3,259},{5,261},{7,263},{9,265},{11,267},{13,269},{15,271}... | collective-permute-start | bytes 6291464 | tf_op jit(solution)/shard_map/ppermute | solution.py:250
  0.8 1.6 %load.1 = (bf16[2,256,512]{2,1,0:T(8,128)(2,1)S(1)}, bf16[2,256,256]{2,1,0:T(8,128)(2,1)S(1)}, bf16[2,256,256]{2,1,0:T(8,128)(2,1)S(1)}, bf16[2,256,512]{2,1,0:T...) custom-call(bf16[256,4096]{1,0:T(8,128)(2,1)} %bitcast.4), custom_call_target="tpu_custom_call" | custom-call | tf_op jit(solution)/shard_map/load/pallas_call | solution.py:197
  2.4 4.9 %collective-permute-start.5 = (bf16[2,256,512]{2,1,0:T(8,128)(2,1)S(1)}, bf16[2,256,512]{2,1,0:T(8,128)(2,1)S(1)}, u32[]{:S(2)}, u32[]{:S(2)}) collective-permute-start(bf16[2,256,512]{2,1,0:T(8,128)(2,1)S(1)} %get-tuple-element.26), channel_id=1, source_target_pairs={{0,256},{2,258},{4,260},{6,262},{8,264},{10,266},{12,268},{14,270}... | collective-permute-start | bytes 1572872 | tf_op jit(solution)/shard_map/ppermute | solution.py:254
  7.4 2.4 %collective-permute-start.3 = (bf16[2,256,256]{2,1,0:T(8,128)(2,1)S(1)}, bf16[2,256,256]{2,1,0:T(8,128)(2,1)S(1)}, u32[]{:S(2)}, u32[]{:S(2)}) collective-permute-start(bf16[2,256,256]{2,1,0:T(8,128)(2,1)S(1)} %get-tuple-element.23), channel_id=1, source_target_pairs={{0,256},{2,258},{4,260},{6,262},{8,264},{10,266},{12,268},{14,270}... | collective-permute-start | bytes 786440 | tf_op jit(solution)/shard_map/ppermute | solution.py:254
  9.8 4.9 %collective-permute-start = (bf16[2,256,256]{2,1,0:T(8,128)(2,1)S(1)}, bf16[2,256,256]{2,1,0:T(8,128)(2,1)S(1)}, u32[]{:S(2)}, u32[]{:S(2)}) collective-permute-start(bf16[2,256,256]{2,1,0:T(8,128)(2,1)S(1)} %get-tuple-element.19), channel_id=1, source_target_pairs={{0,256},{2,258},{4,260},{6,262},{8,264},{10,266},{12,268},{14,270}... | collective-permute-start | bytes 786440 | tf_op jit(solution)/shard_map/ppermute | solution.py:254
  14.7 6.0 %collective-permute-done.5.received = bf16[2,256,512]{2,1,0:T(8,128)(2,1)S(1)} collective-permute-done((bf16[2,256,512]{2,1,0:T(8,128)(2,1)S(1)}, bf16[2,256,512]{2,1,0:T(8,128)(2,1)S(1)}, u32[]{:S(2)}, u32[]{:S(2)}) %collective-permute-start.5) | collective-permute-done | bytes 524320 | tf_op jit(solution)/shard_map/ppermute | solution.py:254
  20.7 1.0 %work.5 = (bf16[2,256,512]{2,1,0:T(8,128)(2,1)S(1)}, bf16[2,256,512]{2,1,0:T(8,128)(2,1)S(1)}) custom-call(bf16[2,256,512]{2,1,0:T(8,128)(2,1)S(1)} %get-tuple-element.25.own, bf16[2,256,512]{2,1,0:T(8,128)(2,1)S(1)} %collective-permute-done.5.received), custom_call_target="tpu_custom_call" | custom-call | flops 402653184 | tf_op jit(solution)/shard_map/work/pallas_call | solution.py:210
  21.7 4.9 %collective-permute-start.6 = (bf16[2,256,512]{2,1,0:T(8,128)(2,1)S(1)}, bf16[2,256,512]{2,1,0:T(8,128)(2,1)S(1)}, u32[]{:S(2)}, u32[]{:S(2)}) collective-permute-start(bf16[2,256,512]{2,1,0:T(8,128)(2,1)S(1)} %get-tuple-element.27), channel_id=1, source_target_pairs={{0,256},{2,258},{4,260},{6,262},{8,264},{10,266},{12,268},{14,270}... | collective-permute-start | bytes 1572872 | tf_op jit(solution)/shard_map/ppermute | solution.py:259
  26.7 0.0 collective-permute-done.3.received
  26.7 0.9 %work.4 = (bf16[2,256,256]{2,1,0:T(8,128)(2,1)S(1)}, bf16[2,256,256]{2,1,0:T(8,128)(2,1)S(1)}) custom-call(bf16[2,256,256]{2,1,0:T(8,128)(2,1)S(1)} %get-tuple-element.22.own, bf16[2,256,256]{2,1,0:T(8,128)(2,1)S(1)} %collective-permute-done.3.received), custom_call_target="tpu_custom_call" | custom-call | flops 201326592 | tf_op jit(solution)/shard_map/work/pallas_call | solution.py:210
  27.6 4.6 %collective-permute-start.4 = (bf16[2,256,256]{2,1,0:T(8,128)(2,1)S(1)}, bf16[2,256,256]{2,1,0:T(8,128)(2,1)S(1)}, u32[]{:S(2)}, u32[]{:S(2)}) collective-permute-start(bf16[2,256,256]{2,1,0:T(8,128)(2,1)S(1)} %get-tuple-element.24), channel_id=1, source_target_pairs={{0,256},{2,258},{4,260},{6,262},{8,264},{10,266},{12,268},{14,270}... | collective-permute-start | bytes 786440 | tf_op jit(solution)/shard_map/ppermute | solution.py:259
  32.2 0.0 collective-permute-done.received
  32.2 0.9 %work.3 = (bf16[2,256,256]{2,1,0:T(8,128)(2,1)S(1)}, bf16[2,256,256]{2,1,0:T(8,128)(2,1)S(1)}) custom-call(bf16[2,256,256]{2,1,0:T(8,128)(2,1)S(1)} %get-tuple-element.18.own, bf16[2,256,256]{2,1,0:T(8,128)(2,1)S(1)} %collective-permute-done.received), custom_call_target="tpu_custom_call" | custom-call | flops 201326592 | tf_op jit(solution)/shard_map/work/pallas_call | solution.py:210
  33.1 4.7 %collective-permute-start.1 = (bf16[2,256,256]{2,1,0:T(8,128)(2,1)S(1)}, bf16[2,256,256]{2,1,0:T(8,128)(2,1)S(1)}, u32[]{:S(2)}, u32[]{:S(2)}) collective-permute-start(bf16[2,256,256]{2,1,0:T(8,128)(2,1)S(1)} %get-tuple-element.20), channel_id=1, source_target_pairs={{0,256},{2,258},{4,260},{6,262},{8,264},{10,266},{12,268},{14,270}... | collective-permute-start | bytes 786440 | tf_op jit(solution)/shard_map/ppermute | solution.py:259
  37.8 1.0 %place.4.rest_1_ = bf16[256,4096]{1,0:T(8,128)(2,1)} custom-call(bf16[2,256,512]{2,1,0:T(8,128)(2,1)S(1)} %get-tuple-element.28.rest_0_, bf16[2,256,256]{2,1,0:T(8,128)(2,1)S(1)} %get-tuple-element.29.rest_1_, bf16[2,256,256]{2,1,0:T(8,128)(2,1)S(1)} %get-tuple-element.30.rest_2_), custom_call_target="tpu_custom_call" | custom-call | tf_op jit(solution)/shard_map/place/pallas_call | solution.py:222
  38.8 4.3 %collective-permute-done.6.rest_0_ = bf16[2,256,512]{2,1,0:T(8,128)(2,1)S(1)} collective-permute-done((bf16[2,256,512]{2,1,0:T(8,128)(2,1)S(1)}, bf16[2,256,512]{2,1,0:T(8,128)(2,1)S(1)}, u32[]{:S(2)}, u32[]{:S(2)}) %collective-permute-start.6) | collective-permute-done | bytes 524320 | tf_op jit(solution)/shard_map/ppermute | solution.py:259
  43.2 0.8 %place.5.rest_1_ = bf16[256,4096]{1,0:T(8,128)(2,1)} custom-call(bf16[2,256,512]{2,1,0:T(8,128)(2,1)S(1)} %collective-permute-done.6.rest_0_, bf16[256,4096]{1,0:T(8,128)(2,1)} %place.4.rest_1_), custom_call_target="tpu_custom_call", output_to_operand_aliasing={{}: (1, {})} | custom-call | tf_op jit(solution)/shard_map/place/pallas_call | solution.py:222
  44.0 4.2 %collective-permute-done.4.rest_0_ = bf16[2,256,256]{2,1,0:T(8,128)(2,1)S(1)} collective-permute-done((bf16[2,256,256]{2,1,0:T(8,128)(2,1)S(1)}, bf16[2,256,256]{2,1,0:T(8,128)(2,1)S(1)}, u32[]{:S(2)}, u32[]{:S(2)}) %collective-permute-start.4) | collective-permute-done | bytes 262176 | tf_op jit(solution)/shard_map/ppermute | solution.py:259
  48.2 0.7 %place.6._ = bf16[256,4096]{1,0:T(8,128)(2,1)} custom-call(bf16[2,256,256]{2,1,0:T(8,128)(2,1)S(1)} %collective-permute-done.4.rest_0_, bf16[256,4096]{1,0:T(8,128)(2,1)} %place.5.rest_1_), custom_call_target="tpu_custom_call", output_to_operand_aliasing={{}: (1, {})} | custom-call | tf_op jit(solution)/shard_map/place/pallas_call | solution.py:222
  48.9 0.0 collective-permute-done.2
  48.9 0.2 whole.1.rest_1_
  49.1 1.9 %collective-permute-done.1.rest_0_ = bf16[2,256,256]{2,1,0:T(8,128)(2,1)S(1)} collective-permute-done((bf16[2,256,256]{2,1,0:T(8,128)(2,1)S(1)}, bf16[2,256,256]{2,1,0:T(8,128)(2,1)S(1)}, u32[]{:S(2)}, u32[]{:S(2)}) %collective-permute-start.1) | collective-permute-done | bytes 262176 | tf_op jit(solution)/shard_map/ppermute | solution.py:259
  51.0 0.7 %place.7 = bf16[256,4096]{1,0:T(8,128)(2,1)} custom-call(bf16[2,256,256]{2,1,0:T(8,128)(2,1)S(1)} %collective-permute-done.1.rest_0_, bf16[256,4096]{1,0:T(8,128)(2,1)} %whole.1.rest_1_), custom_call_target="tpu_custom_call", output_to_operand_aliasing={{}: (1, {})} | custom-call | tf_op jit(solution)/shard_map/place/pallas_call | solution.py:222
Async XLA Ops:
  0.0 48.9 %collective-permute-start.2 = (bf16[1,1,256,4096]{3,2,1,0:T(8,128)(2,1)}, bf16[1,1,256,4096]{3,2,1,0:T(8,128)(2,1)S(1)}, u32[]{:S(2)}, u32[]{:S(2)}) collective-permute-start(bf16[1,1,256,4096]{3,2,1,0:T(8,128)(2,1)} %param.1), channel_id=1, source_target_pairs={{1,257},{3,259},{5,261},{7,263},{9,265},{11,267},{13,269},{15,271}... | collective-permute-start | bytes 6291464 | tf_op jit(solution)/shard_map/ppermute | solution.py:250
  2.4 18.3 %collective-permute-start.5 = (bf16[2,256,512]{2,1,0:T(8,128)(2,1)S(1)}, bf16[2,256,512]{2,1,0:T(8,128)(2,1)S(1)}, u32[]{:S(2)}, u32[]{:S(2)}) collective-permute-start(bf16[2,256,512]{2,1,0:T(8,128)(2,1)S(1)} %get-tuple-element.26), channel_id=1, source_target_pairs={{0,256},{2,258},{4,260},{6,262},{8,264},{10,266},{12,268},{14,270}... | collective-permute-start | bytes 1572872 | tf_op jit(solution)/shard_map/ppermute | solution.py:254
  7.4 19.3 %collective-permute-start.3 = (bf16[2,256,256]{2,1,0:T(8,128)(2,1)S(1)}, bf16[2,256,256]{2,1,0:T(8,128)(2,1)S(1)}, u32[]{:S(2)}, u32[]{:S(2)}) collective-permute-start(bf16[2,256,256]{2,1,0:T(8,128)(2,1)S(1)} %get-tuple-element.23), channel_id=1, source_target_pairs={{0,256},{2,258},{4,260},{6,262},{8,264},{10,266},{12,268},{14,270}... | collective-permute-start | bytes 786440 | tf_op jit(solution)/shard_map/ppermute | solution.py:254
  9.8 22.4 %collective-permute-start = (bf16[2,256,256]{2,1,0:T(8,128)(2,1)S(1)}, bf16[2,256,256]{2,1,0:T(8,128)(2,1)S(1)}, u32[]{:S(2)}, u32[]{:S(2)}) collective-permute-start(bf16[2,256,256]{2,1,0:T(8,128)(2,1)S(1)} %get-tuple-element.19), channel_id=1, source_target_pairs={{0,256},{2,258},{4,260},{6,262},{8,264},{10,266},{12,268},{14,270}... | collective-permute-start | bytes 786440 | tf_op jit(solution)/shard_map/ppermute | solution.py:254
  21.7 21.5 %collective-permute-start.6 = (bf16[2,256,512]{2,1,0:T(8,128)(2,1)S(1)}, bf16[2,256,512]{2,1,0:T(8,128)(2,1)S(1)}, u32[]{:S(2)}, u32[]{:S(2)}) collective-permute-start(bf16[2,256,512]{2,1,0:T(8,128)(2,1)S(1)} %get-tuple-element.27), channel_id=1, source_target_pairs={{0,256},{2,258},{4,260},{6,262},{8,264},{10,266},{12,268},{14,270}... | collective-permute-start | bytes 1572872 | tf_op jit(solution)/shard_map/ppermute | solution.py:259
  27.6 20.6 %collective-permute-start.4 = (bf16[2,256,256]{2,1,0:T(8,128)(2,1)S(1)}, bf16[2,256,256]{2,1,0:T(8,128)(2,1)S(1)}, u32[]{:S(2)}, u32[]{:S(2)}) collective-permute-start(bf16[2,256,256]{2,1,0:T(8,128)(2,1)S(1)} %get-tuple-element.24), channel_id=1, source_target_pairs={{0,256},{2,258},{4,260},{6,262},{8,264},{10,266},{12,268},{14,270}... | collective-permute-start | bytes 786440 | tf_op jit(solution)/shard_map/ppermute | solution.py:259
  33.1 17.8 %collective-permute-start.1 = (bf16[2,256,256]{2,1,0:T(8,128)(2,1)S(1)}, bf16[2,256,256]{2,1,0:T(8,128)(2,1)S(1)}, u32[]{:S(2)}, u32[]{:S(2)}) collective-permute-start(bf16[2,256,256]{2,1,0:T(8,128)(2,1)S(1)} %get-tuple-element.20), channel_id=1, source_target_pairs={{0,256},{2,258},{4,260},{6,262},{8,264},{10,266},{12,268},{14,270}... | collective-permute-start | bytes 786440 | tf_op jit(solution)/shard_map/ppermute | solution.py:259
